TPU v7x, 32 devices: a whole 2x2x4 slice. The times are simulated.
32 devices in a mesh: seq: 16 (over z, x, core), ch: 2 (over y).
Axes of the slice: x: 2, y: 2, z: 4, core: 2. Of those that a mesh axis runs over, the one named last changes fastest.
Arguments:
- tokens: bfloat16 [2, 65536, 2048], P(None, 'seq', 'ch'), may hold values from -6 to 6
- inner_forward: bfloat16 [512, 512], replicated, may hold values from -0.25 to 0.25
- outer_forward: bfloat16 [128, 128], replicated, may hold values from -0.5 to 0.5
- twiddle_forward: float32 [128, 512], P('seq'), may hold values from 0.5 to 2
- freq_kernel: bfloat16 [128, 512, 2048], P(None, 'seq', 'ch'), may hold values from -6 to 6
- outer_inverse: bfloat16 [128, 128], replicated, may hold values from -0.5 to 0.5
- inner_inverse: bfloat16 [512, 512], replicated, may hold values from -0.25 to 0.25
- twiddle_inverse: float32 [128, 512], P(None, 'seq'), may hold values from 0.5 to 2
- gate_gain: float32 [2048], P('ch'), may hold values from 0.5 to 1.5
- gate_bias: float32 [2048], P('ch'), may hold values from -1 to 1
- norm_gain: float32 [2048], replicated, may hold values from 0.1 to 1.9
- up_weight: bfloat16 [4, 1024, 512], P(None, 'seq'), may hold values from -0.25 to 0.25
- down_weight: bfloat16 [4, 1024, 512], P(None, 'seq'), may hold values from -0.1875 to 0.1875
Outputs:
- layer_out: bfloat16 [2, 65536, 2048], P(None, 'seq', 'ch')
All inputs are finite; a program needn't handle non-finite values.
Results may differ from a plain program's by a relative error of at most 0.008.
Values may be sent and summed in bfloat16 or wider, within the bound.
No kernel may reach another device: no remote copies, remote signals or barrier semaphores. Data moves between devices by JAX's collectives and lax.ppermute only.
A program may use at most 256 MiB of HBM per device.

v0:
```python
import jax
import jax.numpy as jnp
from jax import lax
from jax.sharding import PartitionSpec as P


def local(
    tokens,
    inner_forward,
    outer_forward,
    twiddle_forward,
    freq_kernel,
    outer_inverse,
    inner_inverse,
    twiddle_inverse,
    gate_gain,
    gate_bias,
    norm_gain,
    up_weight,
    down_weight,
):
    seq_total, tok_dev, ch_dev = tokens.shape
    inner_size = inner_forward.shape[0]
    outer_dev = tok_dev // inner_size
    blocked = tokens.reshape(seq_total, outer_dev, inner_size, ch_dev)
    section_one = jnp.einsum(
        "kb,xabc->xakc", inner_forward, blocked, preferred_element_type=jnp.float32
    )
    section_one = (section_one * twiddle_forward[None, :, :, None]).astype(jnp.bfloat16)
    spread = lax.all_to_all(section_one, "seq", split_axis=2, concat_axis=1, tiled=True)
    spectrum = jnp.einsum(
        "ka,xabc->xkbc", outer_forward, spread, preferred_element_type=jnp.float32
    )
    spectrum = (spectrum * freq_kernel[None].astype(jnp.float32)).astype(jnp.bfloat16)
    section_two = jnp.einsum(
        "nk,xkbc->xnbc", outer_inverse, spectrum, preferred_element_type=jnp.float32
    )
    section_two = (section_two * twiddle_inverse[None, :, :, None]).astype(jnp.bfloat16)
    gathered = lax.all_to_all(section_two, "seq", split_axis=1, concat_axis=2, tiled=True)
    block_count = up_weight.shape[0]
    width_block = up_weight.shape[2]
    mixed = jnp.einsum("mk,xakc->xamc", inner_inverse, gathered, preferred_element_type=jnp.float32)
    flat = blocked.astype(jnp.float32)
    gate = jax.nn.sigmoid(flat * gate_gain + gate_bias)
    gated = (flat + gate * mixed).astype(jnp.bfloat16)
    full_rows = lax.all_to_all(
        gated.reshape(blocked.shape[0], tok_dev, ch_dev),
        "ch",
        split_axis=1,
        concat_axis=2,
        tiled=True,
    )
    rows_dev = full_rows.shape[1]
    width = full_rows.shape[2]
    rows_f = full_rows.astype(jnp.float32)
    scale = lax.rsqrt(jnp.mean(rows_f * rows_f, axis=-1, keepdims=True) + 1e-06)
    normed = (rows_f * scale * norm_gain).astype(jnp.bfloat16)
    normed_b = normed.reshape(seq_total * rows_dev, block_count, width_block)
    lifted = jnp.einsum(
        "rbi,bji->rbj",
        normed_b,
        lax.all_gather(up_weight, "seq", axis=1, tiled=True),
        preferred_element_type=jnp.float32,
    )
    hidden = jax.nn.gelu(lifted, approximate=True).astype(jnp.bfloat16)
    lowered = jnp.einsum(
        "rbj,bji->rbi",
        hidden,
        lax.all_gather(down_weight, "seq", axis=1, tiled=True),
        preferred_element_type=jnp.float32,
    )
    result_rows = (rows_f + lowered.reshape(seq_total, rows_dev, width)).astype(jnp.bfloat16)
    return lax.all_to_all(result_rows, "ch", split_axis=2, concat_axis=1, tiled=True)


def solution(mesh):
    in_specs = (
        P(None, "seq", "ch"),
        P(),
        P(),
        P("seq", None),
        P(None, "seq", "ch"),
        P(),
        P(),
        P(None, "seq"),
        P("ch"),
        P("ch"),
        P(),
        P(None, "seq", None),
        P(None, "seq", None),
    )
    out_specs = P(None, "seq", "ch")
    return jax.shard_map(local, mesh=mesh, in_specs=in_specs, out_specs=out_specs, check_vma=False)
```

profile of v0, /device:TPU:16, one launch (start us, length us, event | category | flops | bytes accessed | tf_op | source)
XLA Modules:
  0.0 1755.7 jit_solution(6505014984312301893)
XLA Ops:
  6.5 0.0 copy-start
  6.5 1.0 copy-done
  7.6 18.4 %fusion.25 = bf16[2,8,512,1024]{2,3,1,0:T(8,128)(2,1)} fusion(f32[8,512]{1,0:T(8,128)} %param.16, bf16[2,8,512,1024]{3,2,1,0:T(8,128)(2,1)} %bitcast.88, bf16[512,512]{1,0:T(8,128)(2,1)S(1)} %copy-done), kind=kOutput, calls=%fused_computation.33 | convolution fusion | flops 8606711808 | bytes 34095104 | tf_op jit(solution)/shard_map/kb,xabc->xakc/dot_general | solution.py:26
  26.0 23.9 %copy.60 = bf16[2,8,512,1024]{3,1,0,2:T(8,128)(2,1)} copy(bf16[2,8,512,1024]{2,3,1,0:T(8,128)(2,1)} %fusion.25) | data formatting | bytes 33554432 | tf_op jit(solution)/shard_map/convert_element_type | solution.py:29
  49.9 6.5 all-to-all-start
  56.3 0.0 copy-start.2
  56.4 0.0 copy-start.3
  56.4 0.0 copy-start.4
  56.4 14.3 copy.64
  70.7 347.9 %all-to-all-done = bf16[2,8,512,1024]{3,1,0,2:T(8,128)(2,1)} async-done(((bf16[2,8,512,1024]{3,1,0,2:T(8,128)(2,1)}), bf16[2,8,512,1024]{3,1,0,2:T(8,128)(2,1)}, u32[]{:S(2)}, u32[]{:S(2)}) %all-to-all-start) | async-done | bytes 16777248 | tf_op jit(solution)/shard_map/all_to_all | solution.py:30
  418.5 18.7 %copy.62 = bf16[2,16,8,32,1024]{4,3,2,1,0:T(8,128)(2,1)} copy(bf16[2,16,8,32,1024]{4,2,0,3,1:T(8,128)(2,1)} %bitcast.6) | data formatting | bytes 33554432 | tf_op jit(solution)/shard_map/all_to_all | solution.py:30
  437.2 0.0 copy-done.2
  437.2 0.0 copy-done.3
  437.2 0.0 copy-done.4
  437.2 39.0 %fusion.15 = bf16[2,128,32,1024]{1,3,2,0:T(8,128)(2,1)} fusion(f32[128,32]{0,1:T(8,128)S(1)} %copy-done.3, bf16[2,128,32,1024]{3,2,1,0:T(8,128)(2,1)} %bitcast.83, f32[128,32,1024]{0,2,1:T(8,128)} %copy.64, bf16[128,128]{1,0:T(8,128)(2,1)S(1)} %copy-done.4, bf16[128,128]{1,0:T(8,128)(2,1)S(1)} %copy-done.2), kind=kOutput, calls=%fused_computation.20 | convolution fusion | flops 4328521728 | bytes 50413568 | tf_op jit(solution)/shard_map/nk,xkbc->xnbc/dot_general | solution.py:35
  476.2 23.3 %copy.65 = bf16[2,128,32,1024]{3,2,0,1:T(8,128)(2,1)} copy(bf16[2,128,32,1024]{1,3,2,0:T(8,128)(2,1)} %fusion.15) | data formatting | bytes 33554432 | tf_op jit(solution)/shard_map/convert_element_type | solution.py:38
  499.5 0.0 copy-start.6
  499.5 5.3 all-to-all-start.1
  504.8 0.3 all-gather.3.cloned.1.call-start
  505.0 0.5 all-gather.3.cloned.1.call-update
  505.5 386.5 %all-to-all-done.1 = bf16[2,128,32,1024]{3,2,0,1:T(8,128)(2,1)} async-done(((bf16[2,128,32,1024]{3,2,0,1:T(8,128)(2,1)}), bf16[2,128,32,1024]{3,2,0,1:T(8,128)(2,1)}, u32[]{:S(2)}, u32[]{:S(2)}) %all-to-all-start.1) | async-done | bytes 16777248 | tf_op jit(solution)/shard_map/all_to_all | solution.py:39
  892.0 8.2 copy.67
  900.2 0.0 copy-done.6
  900.2 0.0 copy-done.7
  900.2 0.0 copy-done.8
  900.2 19.2 %fusion.17 = bf16[2,8,512,1024]{3,2,1,0:T(8,128)(2,1)} fusion(bf16[2,8,512,1024]{3,2,1,0:T(8,128)(2,1)} %bitcast.89, bf16[2,8,512,1024]{3,2,1,0:T(8,128)(2,1)S(1)} %bitcast.85, f32[1024]{0:T(1024)S(1)} %copy-done.7, f32[1024]{0:T(1024)S(1)} %copy-done.8, bf16[512,512]{1,0:T(8,128)(2,1)S(1)} %copy-done.6), kind=kOutput, calls=%fused_computation.26 | convolution fusion | flops 8665432064 | bytes 50864128 | tf_op jit(solution)/shard_map/mk,xakc->xamc/dot_general | solution.py:42
  919.4 31.0 %copy.68 = bf16[2,4096,1024]{2,0,1:T(2,128)(2,1)} copy(bf16[2,4096,1024]{2,1,0:T(8,128)(2,1)} %bitcast.86) | data formatting | bytes 33554432 | tf_op jit(solution)/shard_map/reshape | solution.py:47
  950.4 9.8 all-to-all-start.2
  960.2 0.0 all-gather.5.cloned.1.call-start
  960.2 0.7 all-gather.5.cloned.1.call-update
  960.9 0.0 copy-done.5
  960.9 181.5 %all-to-all-done.2 = bf16[2,4096,1024]{2,0,1:T(2,128)(2,1)} async-done(((bf16[2,4096,1024]{2,0,1:T(2,128)(2,1)}), bf16[2,4096,1024]{2,0,1:T(2,128)(2,1)}, u32[]{:S(2)}, u32[]{:S(2)}) %all-to-all-start.2) | async-done | bytes 16777248 | tf_op jit(solution)/shard_map/all_to_all | solution.py:46
  1142.5 19.2 %copy_convert_fusion = f32[2,4096,1024]{2,1,0:T(8,128)} fusion(bf16[2,4096,1024]{2,0,1:T(2,128)(2,1)} %all-to-all-done.2), kind=kLoop, calls=%fused_computation.28 | loop fusion | flops 8388608 | bytes 50331648 | tf_op jit(solution)/shard_map/convert_element_type | solution.py:55
  1161.7 49.5 %copy.71 = f32[2,2048,2,1024]{1,0,3,2:T(2,128)} copy(f32[2,2048,2,1024]{3,1,2,0:T(8,128)} %bitcast.81) | data formatting | bytes 67108864 | tf_op jit(solution)/shard_map/convert_element_type | solution.py:55
  1211.1 33.8 %copy.70 = f32[2,2048,2,1024]{1,3,2,0:T(8,128)} copy(f32[2,2048,2,1024]{3,1,2,0:T(8,128)} %bitcast.82) | data formatting | bytes 67108864 | tf_op jit(solution)/shard_map/convert_element_type | solution.py:55
  1244.9 14.2 multiply_reduce_fusion
  1259.3 42.8 %reshape.51 = f32[4096,4,512]{0,2,1:T(8,128)} reshape(f32[2,2048,2,1024]{1,0,3,2:T(2,128)} %copy.71) | data formatting | bytes 67108864 | tf_op jit(solution)/shard_map/convert_element_type | solution.py:55
  1302.1 52.3 %fusion.24 = f32[4096,4,512]{2,0,1:T(8,128)} fusion(bf16[4,1024,512]{2,1,0:T(8,128)(2,1)} %all-gather.5.cloned.1.call-done, bf16[4,1024,512]{2,1,0:T(8,128)(2,1)} %all-gather.3.cloned.1.call-done, f32[4096,4,512]{0,2,1:T(8,128)} %reshape.51, f32[4,512]{1,0:T(4,128)S(1)} %mul.95, f32[4096]{0:T(1024)S(1)} %bitcast.87), kind=kOutput, calls=%fused_computation.32 | convolution fusion | flops 34535899136 | bytes 75522048 | tf_op jit(solution)/shard_map/rbj,bji->rbi/dot_general | solution.py:66
  1354.4 38.2 %copy.73 = f32[4096,4,512]{2,1,0:T(4,128)} copy(f32[4096,4,512]{2,0,1:T(8,128)} %fusion.24) | data formatting | bytes 67108864 | tf_op jit(solution)/shard_map/rbj,bji->rbi/transpose | solution.py:66
  1392.6 39.8 %reshape.49 = f32[2,2048,2048]{2,1,0:T(8,128)} reshape(f32[4096,4,512]{2,1,0:T(4,128)} %copy.73) | data formatting | bytes 67108864 | tf_op jit(solution)/shard_map/reshape | solution.py:72
  1432.3 33.6 %copy.74 = f32[2,2048,2048]{1,2,0:T(8,128)} copy(f32[2,2048,2048]{2,1,0:T(8,128)} %reshape.49) | data formatting | bytes 67108864 | tf_op jit(solution)/shard_map/reshape | solution.py:72
  1465.9 27.5 %fusion.14 = bf16[2,2048,2048]{1,2,0:T(8,128)(2,1)} fusion(f32[2,2048,2048]{1,2,0:T(8,128)} %copy.74, f32[2,2048,2,1024]{1,3,2,0:T(8,128)} %copy.70), kind=kLoop, calls=%fused_computation.18 | loop fusion | flops 16777216 | bytes 83886080 | tf_op jit(solution)/shard_map/convert_element_type | solution.py:72
  1493.5 27.9 %copy.75 = bf16[2,2048,2048]{1,0,2:T(2,128)(2,1)S(1)} copy(bf16[2,2048,2048]{1,2,0:T(8,128)(2,1)} %fusion.14) | data formatting | bytes 33554432 | tf_op jit(solution)/shard_map/convert_element_type | solution.py:72
  1521.4 0.0 copy-start.1
  1521.4 187.1 %all_to_all.63 = bf16[2,2048,2048]{1,0,2:T(2,128)(2,1)} all-to-all(bf16[2,2048,2048]{1,0,2:T(2,128)(2,1)S(1)} %copy.75), channel_id=1, replica_groups=mesh['seq'=16,'ch'=2] {'ch'}, dimensions={2} | all-to-all | bytes 33554432 | tf_op jit(solution)/shard_map/all_to_all | solution.py:73
  1708.5 17.3 copy.76
  1725.9 22.5 %copy.77 = bf16[2,2,2048,1024]{3,2,1,0:T(8,128)(2,1)} copy(bf16[2,2,2048,1024]{2,3,1,0:T(8,128)(2,1)} %bitcast.84) | data formatting | bytes 33554432 | tf_op jit(solution)/shard_map/all_to_all | solution.py:73
  1748.4 0.0 copy-done.1
  (10 shorter events, 0.1 us)
Async XLA Ops:
  6.5 1.0 copy-start
  49.9 368.7 %all-to-all-start = ((bf16[2,8,512,1024]{3,1,0,2:T(8,128)(2,1)}), bf16[2,8,512,1024]{3,1,0,2:T(8,128)(2,1)}, u32[]{:S(2)}, u32[]{:S(2)}) async-start(bf16[2,8,512,1024]{3,1,0,2:T(8,128)(2,1)} %copy.60), calls=%async_computation | async-start | bytes 33554432 | tf_op jit(solution)/shard_map/all_to_all | solution.py:30
  56.3 380.8 %copy-start.2 = (bf16[128,128]{1,0:T(8,128)(2,1)S(1)}, bf16[128,128]{1,0:T(8,128)(2,1)}, u32[]{:S(2)}) copy-start(bf16[128,128]{1,0:T(8,128)(2,1)} %param.15) | copy-start | bytes 98308
  56.4 380.8 %copy-start.3 = (f32[128,32]{0,1:T(8,128)S(1)}, f32[128,32]{0,1:T(8,128)}, u32[]{:S(2)}) copy-start(f32[128,32]{0,1:T(8,128)} %param.20) | copy-start | bytes 49156
  56.4 380.8 %copy-start.4 = (bf16[128,128]{1,0:T(8,128)(2,1)S(1)}, bf16[128,128]{1,0:T(8,128)(2,1)}, u32[]{:S(2)}) copy-start(bf16[128,128]{1,0:T(8,128)(2,1)} %param.18) | copy-start | bytes 98308
  499.5 400.7 %copy-start.6 = (bf16[512,512]{1,0:T(8,128)(2,1)S(1)}, bf16[512,512]{1,0:T(8,128)(2,1)}, u32[]{:S(2)}) copy-start(bf16[512,512]{1,0:T(8,128)(2,1)} %param.19) | copy-start | bytes 1572868
  499.5 400.7 %copy-start.7 = (f32[1024]{0:T(1024)S(1)}, f32[1024]{0:T(1024)}, u32[]{:S(2)}) copy-start(f32[1024]{0:T(1024)} %param.22) | copy-start | bytes 12292
  499.5 400.7 %copy-start.8 = (f32[1024]{0:T(1024)S(1)}, f32[1024]{0:T(1024)}, u32[]{:S(2)}) copy-start(f32[1024]{0:T(1024)} %param.21) | copy-start | bytes 12292
  499.5 392.5 %all-to-all-start.1 = ((bf16[2,128,32,1024]{3,2,0,1:T(8,128)(2,1)}), bf16[2,128,32,1024]{3,2,0,1:T(8,128)(2,1)}, u32[]{:S(2)}, u32[]{:S(2)}) async-start(bf16[2,128,32,1024]{3,2,0,1:T(8,128)(2,1)} %copy.65), calls=%async_computation.1 | async-start | bytes 33554432 | tf_op jit(solution)/shard_map/all_to_all | solution.py:39
  504.8 797.3 %all-gather.3.cloned.1.call-start = ((), (), s32[]{:S(2)}) async-start(), calls=%async_computation.4 | async-start | bytes 4456448 | tf_op jit(solution)/shard_map/all_gather | solution.py:62
  919.4 41.5 %copy-start.5 = (f32[2048]{0:T(1024)S(1)}, f32[2048]{0:T(1024)}, u32[]{:S(2)}) copy-start(f32[2048]{0:T(1024)} %param.23) | copy-start | bytes 24580
  950.4 192.1 %all-to-all-start.2 = ((bf16[2,4096,1024]{2,0,1:T(2,128)(2,1)}), bf16[2,4096,1024]{2,0,1:T(2,128)(2,1)}, u32[]{:S(2)}, u32[]{:S(2)}) async-start(bf16[2,4096,1024]{2,0,1:T(2,128)(2,1)} %copy.68), calls=%async_computation.2 | async-start | bytes 33554432 | tf_op jit(solution)/shard_map/all_to_all | solution.py:46
  960.2 341.9 %all-gather.5.cloned.1.call-start = ((), (), s32[]{:S(2)}) async-start(), calls=%async_computation.5 | async-start | bytes 4456448 | tf_op jit(solution)/shard_map/all_gather | solution.py:69
  1521.4 227.0 %copy-start.1 = (bf16[512,512]{1,0:T(8,128)(2,1)S(1)}, bf16[512,512]{1,0:T(8,128)(2,1)}, u32[]{:S(2)}) copy-start(bf16[512,512]{1,0:T(8,128)(2,1)} %param.14) | copy-start | bytes 1572868
Sparse Core Ops, SparseCore 0:
  507.8 214.6 all-gather.2
  963.2 49.9 all-gather.4
where the time goes:
time: 1770 us; the launch traced here: 1760 us
  waiting for transfers between devices  917 us (52%)
  local copies, waits for them, and re-layouts  426 us (24%)
  blocking collectives  187 us (11%)
  matrix products  129 us (7%)
  other arithmetic  61 us (3%)
  starting transfers between devices  21.8 us (1%)
    all_to_all x1, waiting for transfers between devices, local(): lax.all_to_all(section_two, 'seq', split_axis=1, concat_axis=2, tiled=True)  386 us
    all_to_all x1, waiting for transfers between devices, local(): lax.all_to_all(section_one, 'seq', split_axis=2, concat_axis=1, tiled=True)  348 us
    all_to_all x1, blocking collectives, local(): lax.all_to_all(result_rows, 'ch', split_axis=2, concat_axis=1, tiled=True)  187 us
    all_to_all x1, waiting for transfers between devices, local(): lax.all_to_all(gated.reshape(blocked.shape[0], tok_dev, ch_dev), 'ch', sp...  182 us
    convert_element_type x3, local copies, waits for them, and re-layouts, local(): rows_f = full_rows.astype(jnp.float32)  126 us
    reshape x2, local copies, waits for them, and re-layouts, local(): lowered.reshape(seq_total, rows_dev, width)  73.3 us
    dot_general x1, matrix products, local(): jnp.einsum('rbj,bji->rbi', hidden, lax.all_gather(down_weight, 'seq', axi...  52.3 us
    all_to_all x2, local copies, waits for them, and re-layouts, local(): lax.all_to_all(result_rows, 'ch', split_axis=2, concat_axis=1, tiled=True)  39.9 us
  transfers between devices with their start and end apart: 5, of which 3 were waited for; matrix products, arithmetic and copies ran while one was open for 13% of the time, Pallas kernels for 0%

commit v1 on v0

--- a/solution.py
+++ b/solution.py
@@ -1,10 +1,244 @@
+import functools
+
 import jax
 import jax.numpy as jnp
 from jax import lax
+from jax.experimental import pallas as pl
+from jax.experimental.pallas import tpu as pltpu
 from jax.sharding import PartitionSpec as P
 
-
-def local(
+VMEM_BYTES = 56 * 1024 * 1024
+EPS = 1e-06
+GROUPS = ((8,), (4, 2, 1, 1))
+
+
+def params():
+    return pltpu.CompilerParams(vmem_limit_bytes=VMEM_BYTES)
+
+
+def first_kernel(n, me_ref, tok_ref, w_ref, tw_ref, *rest):
+    outs, buf = rest[:n], rest[n]
+    a = pl.program_id(0)
+    res = jnp.dot(w_ref[...], tok_ref[0, 0], preferred_element_type=jnp.float32)
+    cols = tw_ref[...].T
+    lane = lax.broadcasted_iota(jnp.int32, cols.shape, 1)
+    tw = jnp.sum(jnp.where(lane == a, cols, 0.0), axis=1, keepdims=True)
+    buf[...] = (res * tw).astype(jnp.bfloat16)
+    rows = buf.shape[0] // n
+    for m in range(n):
+        start = pl.multiple_of((me_ref[0] ^ m) * rows, rows)
+        outs[m][0] = buf[pl.ds(start, rows), :]
+
+
+def first_section(me, blocked, inner_forward, twiddle, s, n):
+    _, a_dev, inner, ch = blocked.shape
+    rows = inner // n
+    return pl.pallas_call(
+        functools.partial(first_kernel, n),
+        grid_spec=pltpu.PrefetchScalarGridSpec(
+            num_scalar_prefetch=1,
+            grid=(a_dev,),
+            in_specs=[
+                pl.BlockSpec((1, 1, inner, ch), lambda a, me: (s, a, 0, 0)),
+                pl.BlockSpec((inner, inner), lambda a, me: (0, 0)),
+                pl.BlockSpec((a_dev, inner), lambda a, me: (0, 0)),
+            ],
+            out_specs=[pl.BlockSpec((1, rows, ch), lambda a, me: (a, 0, 0))] * n,
+            scratch_shapes=[pltpu.VMEM((inner, ch), jnp.bfloat16)],
+        ),
+        out_shape=[jax.ShapeDtypeStruct((a_dev, rows, ch), jnp.bfloat16)] * n,
+        compiler_params=params(),
+        name="first_section",
+    )(me, blocked, inner_forward, twiddle)
+
+
+def gate_kernel(n, me_ref, tok_ref, w_ref, gain_ref, bias_ref, *rest):
+    parts, gated_ref, sq_ref, buf = rest[:n], rest[n], rest[n + 1], rest[n + 2]
+    rows = buf.shape[0] // n
+    for m in range(n):
+        start = pl.multiple_of((me_ref[0] ^ m) * rows, rows)
+        buf[pl.ds(start, rows), :] = parts[m][0]
+    mixed = jnp.dot(w_ref[...], buf[...], preferred_element_type=jnp.float32)
+    flat = tok_ref[0, 0].astype(jnp.float32)
+    gate = jax.nn.sigmoid(flat * gain_ref[...] + bias_ref[...])
+    gated = (flat + gate * mixed).astype(jnp.bfloat16)
+    gated_ref[0] = gated
+    g = gated.astype(jnp.float32)
+    sq = g * g
+    part = sq[:, :128]
+    for c in range(128, sq.shape[1], 128):
+        part = part + sq[:, c : c + 128]
+    sq_ref[0] = jnp.sum(part.T, axis=0, keepdims=True)
+
+
+def gate_rows(me, blocked, inner_inverse, gain, bias, parts, s, first, n):
+    _, _, inner, ch = blocked.shape
+    count, rows, _ = parts[0].shape
+    return pl.pallas_call(
+        functools.partial(gate_kernel, n),
+        grid_spec=pltpu.PrefetchScalarGridSpec(
+            num_scalar_prefetch=1,
+            grid=(count,),
+            in_specs=[
+                pl.BlockSpec((1, 1, inner, ch), lambda j, me: (s, first + j, 0, 0)),
+                pl.BlockSpec((inner, inner), lambda j, me: (0, 0)),
+                pl.BlockSpec((1, ch), lambda j, me: (0, 0)),
+                pl.BlockSpec((1, ch), lambda j, me: (0, 0)),
+            ]
+            + [pl.BlockSpec((1, rows, ch), lambda j, me: (j, 0, 0))] * n,
+            out_specs=[
+                pl.BlockSpec((1, inner, ch), lambda j, me: (j, 0, 0)),
+                pl.BlockSpec((1, 1, inner), lambda j, me: (j, 0, 0)),
+            ],
+            scratch_shapes=[pltpu.VMEM((inner, ch), jnp.bfloat16)],
+        ),
+        out_shape=[
+            jax.ShapeDtypeStruct((count, inner, ch), jnp.bfloat16),
+            jax.ShapeDtypeStruct((count, 1, inner), jnp.float32),
+        ],
+        compiler_params=params(),
+        name="gate_rows",
+    )(me, blocked, inner_inverse, gain, bias, *parts)
+
+
+def mlp_kernel(width, gated_ref, sq_ref, gain_ref, up_ref, down_ref, *rest):
+    out_ref = rest[-1]
+    blocks, _, wb = up_ref.shape
+    scale = lax.rsqrt(sq_ref[0] * (1.0 / width) + EPS)
+    scale = jnp.broadcast_to(scale, (128, scale.shape[1])).T[:, :1]
+    for b in range(blocks):
+        cols = slice(b * wb, (b + 1) * wb)
+        g = gated_ref[0, :, cols].astype(jnp.float32)
+        normed = (g * scale * gain_ref[:, cols]).astype(jnp.bfloat16)
+        lifted = lax.dot_general(
+            normed, up_ref[b], (((1,), (1,)), ((), ())), preferred_element_type=jnp.float32
+        )
+        hidden = jax.nn.gelu(lifted, approximate=True).astype(jnp.bfloat16)
+        lowered = jnp.dot(hidden, down_ref[b], preferred_element_type=jnp.float32)
+        out_ref[0, :, cols] = (g + lowered).astype(jnp.bfloat16)
+
+
+def mlp_rows(gated, sq, gain, up, down, out, first, total, width):
+    count, inner, ch = gated.shape
+    specs = [
+        pl.BlockSpec((1, inner, ch), lambda j: (j, 0, 0)),
+        pl.BlockSpec((1, 1, inner), lambda j: (j, 0, 0)),
+        pl.BlockSpec((1, ch), lambda j: (0, 0)),
+        pl.BlockSpec(up.shape, lambda j: (0, 0, 0), pipeline_mode=pl.Buffered(1)),
+        pl.BlockSpec(down.shape, lambda j: (0, 0, 0), pipeline_mode=pl.Buffered(1)),
+    ]
+    args = [gated, sq, gain, up, down]
+    aliases = {}
+    if out is not None:
+        specs.append(pl.BlockSpec(memory_space=pl.ANY))
+        args.append(out)
+        aliases = {5: 0}
+    return pl.pallas_call(
+        functools.partial(mlp_kernel, width),
+        grid=(count,),
+        in_specs=specs,
+        out_specs=pl.BlockSpec((1, inner, ch), lambda j: (first + j, 0, 0)),
+        out_shape=jax.ShapeDtypeStruct((total, inner, ch), jnp.bfloat16),
+        input_output_aliases=aliases,
+        compiler_params=params(),
+        name="mlp_rows",
+    )(*args)
+
+
+def swap(x, m, n):
+    return lax.ppermute(x, "seq", [(j, j ^ m) for j in range(n)])
+
+
+def send_order(n):
+    half = n // 2
+    order = []
+    for j in range(half):
+        order.append(half + j)
+        if j:
+            order.append(j)
+    return order
+
+
+def exchange(parts, n):
+    got = list(parts)
+    for m in send_order(n):
+        got[m] = swap(parts[m], m, n)
+    return got
+
+
+def local_blocks(
+    tokens,
+    inner_forward,
+    outer_forward,
+    twiddle_forward,
+    freq_kernel,
+    outer_inverse,
+    inner_inverse,
+    twiddle_inverse,
+    gate_gain,
+    gate_bias,
+    norm_gain,
+    up_weight,
+    down_weight,
+):
+    seqs, tok_dev, ch = tokens.shape
+    inner = inner_forward.shape[0]
+    a_dev = tok_dev // inner
+    n = lax.axis_size("seq")
+    n_ch = lax.axis_size("ch")
+    me = lax.axis_index("seq")
+    my_ch = lax.axis_index("ch")
+    outer = n * a_dev
+    me_arr = jnp.reshape(me, (1,)).astype(jnp.int32)
+    blocked = tokens.reshape(seqs, a_dev, inner, ch)
+    order = jnp.arange(n) ^ me
+    forward = outer_forward.reshape(outer, n, a_dev)[:, order].reshape(outer, outer)
+    inverse = outer_inverse.reshape(n, a_dev, outer)[order].reshape(outer, outer)
+    tw_inv = twiddle_inverse.reshape(n, a_dev, -1)[order].reshape(outer, -1)
+
+    held = ch // up_weight.shape[2]
+    up = lax.dynamic_slice_in_dim(up_weight, my_ch * held, held, 0)
+    down = lax.dynamic_slice_in_dim(down_weight, my_ch * held, held, 0)
+    up = lax.all_gather(up, "seq", axis=1, tiled=True)
+    down = lax.all_gather(down, "seq", axis=1, tiled=True)
+    norm = lax.dynamic_slice_in_dim(norm_gain, my_ch * ch, ch, 0).reshape(1, ch)
+    gain, bias = gate_gain.reshape(1, ch), gate_bias.reshape(1, ch)
+
+    got = []
+    for s in range(seqs):
+        parts = first_section(me_arr, blocked, inner_forward, twiddle_forward, s, n)
+        got.append(exchange(parts, n))
+
+    out = None
+    for s in range(seqs):
+        spread = jnp.concatenate(got[s], axis=0)
+        spectrum = jnp.einsum("ka,abc->kbc", forward, spread, preferred_element_type=jnp.float32)
+        spectrum = (spectrum * freq_kernel.astype(jnp.float32)).astype(jnp.bfloat16)
+        section_two = jnp.einsum(
+            "nk,kbc->nbc", inverse, spectrum, preferred_element_type=jnp.float32
+        )
+        section_two = (section_two * tw_inv[:, :, None]).astype(jnp.bfloat16)
+        section_two = section_two.reshape(n, a_dev, -1, ch)
+        first = 0
+        for count in GROUPS[min(s, 1)]:
+            parts = [section_two[m, first : first + count] for m in range(n)]
+            parts = exchange(parts, n)
+            gated, sq = gate_rows(
+                me_arr, blocked, inner_inverse, gain, bias, parts, s, first, n
+            )
+            total = sq
+            for r in range(1, n_ch):
+                total = total + lax.ppermute(
+                    sq, "ch", [(j, (j + r) % n_ch) for j in range(n_ch)]
+                )
+            out = mlp_rows(
+                gated, total, norm, up, down, out, s * a_dev + first, seqs * a_dev, ch * n_ch
+            )
+            first += count
+    return out.reshape(seqs, tok_dev, ch)
+
+
+def local_rows(
     tokens,
     inner_forward,
     outer_forward,
@@ -53,7 +287,7 @@
     rows_dev = full_rows.shape[1]
     width = full_rows.shape[2]
     rows_f = full_rows.astype(jnp.float32)
-    scale = lax.rsqrt(jnp.mean(rows_f * rows_f, axis=-1, keepdims=True) + 1e-06)
+    scale = lax.rsqrt(jnp.mean(rows_f * rows_f, axis=-1, keepdims=True) + EPS)
     normed = (rows_f * scale * norm_gain).astype(jnp.bfloat16)
     normed_b = normed.reshape(seq_total * rows_dev, block_count, width_block)
     lifted = jnp.einsum(
@@ -73,6 +307,14 @@
     return lax.all_to_all(result_rows, "ch", split_axis=2, concat_axis=1, tiled=True)
 
 
+def local(*args):
+    tokens, up_weight = args[0], args[11]
+    n = lax.axis_size("seq")
+    if tokens.shape[2] % up_weight.shape[2] == 0 and n & (n - 1) == 0:
+        return local_blocks(*args)
+    return local_rows(*args)
+
+
 def solution(mesh):
     in_specs = (
         P(None, "seq", "ch"),

time: 1770 us -> 1110 us (0.63)
  local copies, waits for them, and re-layouts: 426 us -> 48.8 us
  waiting for transfers between devices: 917 us -> 602 us
  blocking collectives: 187 us -> 0 us
  starting transfers between devices: 21.8 us -> 174 us
  Pallas kernels: 0 us -> 122 us
  matrix products: 129 us -> 69.2 us
    all_to_all x3 -> x0, waiting for transfers between devices: 916 us -> none  [the longest x1 386 us: local(): lax.all_to_all(section_two, 'seq', split_axis=1, concat_axis=2, tiled=True)]
    ppermute x0 -> x110, waiting for transfers between devices: none -> 602 us  [the longest x105 600 us: swap(): return lax.ppermute(x, 'seq', [(j, j ^ m) for j in range(n)])]
    convert_element_type x7 -> x0, local copies, waits for them, and re-layouts: 215 us -> none  [the longest x3 126 us: local(): rows_f = full_rows.astype(jnp.float32)]
    all_to_all x1 -> x0, blocking collectives: 187 us -> none  [local(): lax.all_to_all(result_rows, 'ch', split_axis=2, concat_axis=1, tiled=True)]
    ppermute x0 -> x110, starting transfers between devices: none -> 173 us  [the longest x105 166 us: swap(): return lax.ppermute(x, 'seq', [(j, j ^ m) for j in range(n)])]
    pallas_call x0 -> x12, Pallas kernels: none -> 122 us  [the longest x5 65 us: mlp_rows(): pl.pallas_call(functools.partial(mlp_kernel, width), grid=(count,), in_sp...]
    reshape x3 -> x0, local copies, waits for them, and re-layouts: 104 us -> none  [the longest x2 73.3 us: local(): lowered.reshape(seq_total, rows_dev, width)]
    all_to_all x4 -> x0, local copies, waits for them, and re-layouts: 66.7 us -> none  [the longest x2 39.9 us: local(): lax.all_to_all(result_rows, 'ch', split_axis=2, concat_axis=1, tiled=True)]
  transfers between devices with their start and end apart: 5 -> 112, of which waited for: 3 -> 57; matrix products, arithmetic and copies ran while one was open for 13% -> 16% of each run, Pallas kernels for 0% -> 4%
where the time goes in v1:
time: 1110 us; the launch traced here: 1090 us
  waiting for transfers between devices  602 us (54%)
  starting transfers between devices  174 us (16%)
  Pallas kernels  122 us (11%)
  matrix products  69.2 us (6%)
  other arithmetic  63.3 us (6%)
  local copies, waits for them, and re-layouts  48.8 us (4%)
  between operations  14.7 us (1%)
    ppermute x105, waiting for transfers between devices, swap(): return lax.ppermute(x, 'seq', [(j, j ^ m) for j in range(n)])  600 us
    ppermute x105, starting transfers between devices, swap(): return lax.ppermute(x, 'seq', [(j, j ^ m) for j in range(n)])  166 us
    pallas_call x5, Pallas kernels, mlp_rows(): pl.pallas_call(functools.partial(mlp_kernel, width), grid=(count,), in_sp...  65 us
    pallas_call x5, Pallas kernels, gate_rows(): pl.pallas_call(functools.partial(gate_kernel, n), grid_spec=pltpu.Prefetc...  34.8 us
    dot_general x2, matrix products, local_blocks(): jnp.einsum('nk,kbc->nbc', inverse, spectrum, preferred_element_type=jnp.f...  34.7 us
    dot_general x2, matrix products, local_blocks(): jnp.einsum('ka,abc->kbc', forward, spread, preferred_element_type=jnp.flo...  34.5 us
    convert_element_type x1, other arithmetic, local_blocks(): spectrum = (spectrum * freq_kernel.astype(jnp.float32)).astype(jnp.bfloat16)  30.2 us
    convert_element_type x1, other arithmetic, local_blocks(): section_two = (section_two * tw_inv[:, :, None]).astype(jnp.bfloat16)  29.5 us
  transfers between devices with their start and end apart: 112, of which 57 were waited for; matrix products, arithmetic and copies ran while one was open for 16% of the time, Pallas kernels for 4%

profile of v1, /device:TPU:16, one launch (start us, length us, event | category | flops | bytes accessed | tf_op | source)
XLA Modules:
  0.0 1093.4 jit_solution(9508512164313684571)
XLA Ops:
  6.5 11.2 %first_section.2 = (bf16[8,32,1024]{2,1,0:T(8,128)(2,1)}, bf16[8,32,1024]{2,1,0:T(8,128)(2,1)}, bf16[8,32,1024]{2,1,0:T(8,128)(2,1)}, bf16[8,32,1024]{2,1,0:T(8,...) custom-call(s32[1]{0:T(128)} %bitcast.me_ref, ...), custom_call_target="tpu_custom_call" | custom-call | tf_op jit(solution)/shard_map/first_section/pallas_call | solution.py:36
  24.0 11.2 %first_section.3 = (bf16[8,32,1024]{2,1,0:T(8,128)(2,1)}, bf16[8,32,1024]{2,1,0:T(8,128)(2,1)}, bf16[8,32,1024]{2,1,0:T(8,128)(2,1)}, bf16[8,32,1024]{2,1,0:T(8,...) custom-call(s32[1]{0:T(128)} %bitcast.me_ref, ...), custom_call_target="tpu_custom_call" | custom-call | tf_op jit(solution)/shard_map/first_section/pallas_call | solution.py:36
  49.1 9.6 collective-permute-done.4
  59.5 32.3 %collective-permute-done.5 = bf16[8,32,1024]{2,1,0:T(8,128)(2,1)S(1)} collective-permute-done((bf16[8,32,1024]{2,1,0:T(8,128)(2,1)}, bf16[8,32,1024]{2,1,0:T(8,128)(2,1)S(1)}, u32[]{:S(2)}, u32[]{:S(2)}) %collective-permute-start.5) | collective-permute-done | bytes 524320 | tf_op jit(solution)/shard_map/ppermute | solution.py:149
  95.6 6.9 collective-permute-done.6
  108.5 55.6 %collective-permute-done.9 = bf16[8,32,1024]{2,1,0:T(8,128)(2,1)S(1)} collective-permute-done((bf16[8,32,1024]{2,1,0:T(8,128)(2,1)}, bf16[8,32,1024]{2,1,0:T(8,128)(2,1)S(1)}, u32[]{:S(2)}, u32[]{:S(2)}) %collective-permute-start.9) | collective-permute-done | bytes 524320 | tf_op jit(solution)/shard_map/ppermute | solution.py:149
  171.1 15.5 %collective-permute-done.10 = bf16[8,32,1024]{2,1,0:T(8,128)(2,1)S(1)} collective-permute-done((bf16[8,32,1024]{2,1,0:T(8,128)(2,1)}, bf16[8,32,1024]{2,1,0:T(8,128)(2,1)S(1)}, u32[]{:S(2)}, u32[]{:S(2)}) %collective-permute-start.10) | collective-permute-done | bytes 524320 | tf_op jit(solution)/shard_map/ppermute | solution.py:149
  192.6 11.0 %collective-permute-done.11 = bf16[8,32,1024]{2,1,0:T(8,128)(2,1)S(1)} collective-permute-done((bf16[8,32,1024]{2,1,0:T(8,128)(2,1)}, bf16[8,32,1024]{2,1,0:T(8,128)(2,1)S(1)}, u32[]{:S(2)}, u32[]{:S(2)}) %collective-permute-start.11) | collective-permute-done | bytes 524320 | tf_op jit(solution)/shard_map/ppermute | solution.py:149
  205.6 9.0 collective-permute-done.12
  216.5 10.2 collective-permute-done.13
  227.6 10.6 collective-permute-done.14
  242.9 7.2 collective-permute-done.81
  257.2 26.0 %collective-permute-done.84 = bf16[8,32,1024]{2,1,0:T(8,128)(2,1)S(1)} collective-permute-done((bf16[8,32,1024]{2,1,0:T(8,128)(2,1)S(1)}, bf16[8,32,1024]{2,1,0:T(8,128)(2,1)S(1)}, u32[]{:S(2)}, u32[]{:S(2)}) %collective-permute-start.84) | collective-permute-done | bytes 524320 | tf_op jit(solution)/shard_map/ppermute | solution.py:149
  285.9 7.9 collective-permute-done.85
  296.4 46.7 %collective-permute-start.92 = (bf16[8,32,1024]{2,1,0:T(8,128)(2,1)S(1)}, bf16[8,32,1024]{2,1,0:T(8,128)(2,1)S(1)}, u32[]{:S(2)}, u32[]{:S(2)}) collective-permute-start(bf16[8,32,1024]{2,1,0:T(8,128)(2,1)S(1)} %copy-done.73), channel_id=1, source_target_pairs={{0,28},{2,30},{4,24},{6,26},{8,20},{10,22},{12,16},{14,18},{16,12}... | collective-permute-start | bytes 1572872 | tf_op jit(solution)/shard_map/ppermute | solution.py:149
  344.0 19.3 %collective-permute-done.88 = bf16[8,32,1024]{2,1,0:T(8,128)(2,1)S(1)} collective-permute-done((bf16[8,32,1024]{2,1,0:T(8,128)(2,1)S(1)}, bf16[8,32,1024]{2,1,0:T(8,128)(2,1)S(1)}, u32[]{:S(2)}, u32[]{:S(2)}) %collective-permute-start.88) | collective-permute-done | bytes 524320 | tf_op jit(solution)/shard_map/ppermute | solution.py:149
  365.5 20.3 %collective-permute-done.89 = bf16[8,32,1024]{2,1,0:T(8,128)(2,1)S(1)} collective-permute-done((bf16[8,32,1024]{2,1,0:T(8,128)(2,1)S(1)}, bf16[8,32,1024]{2,1,0:T(8,128)(2,1)S(1)}, u32[]{:S(2)}, u32[]{:S(2)}) %collective-permute-start.89) | collective-permute-done | bytes 524320 | tf_op jit(solution)/shard_map/ppermute | solution.py:149
  386.6 12.8 %collective-permute-done.90 = bf16[8,32,1024]{2,1,0:T(8,128)(2,1)S(1)} collective-permute-done((bf16[8,32,1024]{2,1,0:T(8,128)(2,1)S(1)}, bf16[8,32,1024]{2,1,0:T(8,128)(2,1)S(1)}, u32[]{:S(2)}, u32[]{:S(2)}) %collective-permute-start.90) | collective-permute-done | bytes 524320 | tf_op jit(solution)/shard_map/ppermute | solution.py:149
  400.2 8.0 collective-permute-done.91
  409.1 13.0 %collective-permute-done.92 = bf16[8,32,1024]{2,1,0:T(8,128)(2,1)S(1)} collective-permute-done((bf16[8,32,1024]{2,1,0:T(8,128)(2,1)S(1)}, bf16[8,32,1024]{2,1,0:T(8,128)(2,1)S(1)}, u32[]{:S(2)}, u32[]{:S(2)}) %collective-permute-start.92) | collective-permute-done | bytes 524320 | tf_op jit(solution)/shard_map/ppermute | solution.py:149
  423.0 14.3 %fusion.6 = f32[128,32,1024]{2,0,1:T(8,128)S(1)} fusion(bf16[128,32,1024]{2,1,0:T(8,128)(2,1)} %constant_dynamic-update-slice_fusion, bf16[16,128,8]{1,2,0:T(8,128)(2,1)S(1)} %gather_fusion.1), kind=kOutput, calls=%fused_computation.13 | convolution fusion | flops 1073741824 | bytes 25198592 | tf_op jit(solution)/shard_map/ka,abc->kbc/dot_general | solution.py:215
  438.2 20.1 %fusion.4 = f32[128,32,1024]{2,0,1:T(8,128)} fusion(bf16[128,32,1024]{2,1,0:T(8,128)(2,1)} %constant_dynamic-update-slice_fusion.16, bf16[16,128,8]{1,2,0:T(8,128)(2,1)S(1)} %gather_fusion.1), kind=kOutput, calls=%fused_computation.11 | convolution fusion | flops 1073741824 | bytes 25198592 | tf_op jit(solution)/shard_map/ka,abc->kbc/dot_general | solution.py:215
  458.4 30.2 %fusion.1 = (bf16[128,32,1024]{2,1,0:T(8,128)(2,1)}, bf16[128,32,1024]{2,1,0:T(8,128)(2,1)}) fusion(bf16[128,32,1024]{2,1,0:T(8,128)(2,1)} %param.17, f32[128,32,1024]{2,0,1:T(8,128)} %fusion.4, f32[128,32,1024]{2,0,1:T(8,128)S(1)} %fusion.6), kind=kLoop, calls=%fused_computation.6 | loop fusion | flops 20971520 | bytes 58720256 | tf_op jit(solution)/shard_map/convert_element_type | solution.py:216
  488.5 14.1 %fusion.10 = f32[128,32,1024]{2,0,1:T(8,128)S(1)} fusion(bf16[128,32,1024]{2,1,0:T(8,128)(2,1)} %get-tuple-element.106, bf16[16,8,128]{2,1,0:T(8,128)(2,1)S(1)} %gather_fusion), kind=kOutput, calls=%fused_computation.17 | convolution fusion | flops 1073741824 | bytes 25198592 | tf_op jit(solution)/shard_map/nk,kbc->nbc/dot_general | solution.py:217
  502.6 20.6 %fusion.8 = f32[128,32,1024]{2,0,1:T(8,128)} fusion(bf16[128,32,1024]{2,1,0:T(8,128)(2,1)} %get-tuple-element.105, bf16[16,8,128]{2,1,0:T(8,128)(2,1)S(1)} %gather_fusion), kind=kOutput, calls=%fused_computation.15 | convolution fusion | flops 1073741824 | bytes 25198592 | tf_op jit(solution)/shard_map/nk,kbc->nbc/dot_general | solution.py:217
  523.2 29.5 %fusion.2 = (bf16[128,32,1024]{2,1,0:T(8,128)(2,1)}, bf16[128,32,1024]{2,1,0:T(8,128)(2,1)}) fusion(f32[128,32,1024]{2,0,1:T(8,128)} %fusion.8, f32[128,32]{1,0:T(8,128)S(1)} %bitcast.169, f32[128,32,1024]{2,0,1:T(8,128)S(1)} %fusion.10), kind=kLoop, calls=%fused_computation.8 | loop fusion | flops 16777216 | bytes 50348032 | tf_op jit(solution)/shard_map/convert_element_type | solution.py:220
  627.9 6.5 collective-permute-done.51.rest_5_
  663.3 8.1 collective-permute-done.60.rest_14_
  677.1 12.3 %collective-permute-done.67.rest_5_ = bf16[4,32,1024]{2,1,0:T(8,128)(2,1)S(1)} collective-permute-done((bf16[4,32,1024]{2,1,0:T(8,128)(2,1)S(1)}, bf16[4,32,1024]{2,1,0:T(8,128)(2,1)S(1)}, u32[]{:S(2)}, u32[]{:S(2)}) %collective-permute-start.67) | collective-permute-done | bytes 262176 | tf_op jit(solution)/shard_map/ppermute | solution.py:149
  708.6 26.5 %collective-permute-done.72.rest_10_ = bf16[4,32,1024]{2,1,0:T(8,128)(2,1)S(1)} collective-permute-done((bf16[4,32,1024]{2,1,0:T(8,128)(2,1)S(1)}, bf16[4,32,1024]{2,1,0:T(8,128)(2,1)S(1)}, u32[]{:S(2)}, u32[]{:S(2)}) %collective-permute-start.72) | collective-permute-done | bytes 262176 | tf_op jit(solution)/shard_map/ppermute | solution.py:149
  747.6 27.9 %collective-permute-done.75.rest_13_ = bf16[4,32,1024]{2,1,0:T(8,128)(2,1)S(1)} collective-permute-done((bf16[4,32,1024]{2,1,0:T(8,128)(2,1)S(1)}, bf16[4,32,1024]{2,1,0:T(8,128)(2,1)S(1)}, u32[]{:S(2)}, u32[]{:S(2)}) %collective-permute-start.75) | collective-permute-done | bytes 262176 | tf_op jit(solution)/shard_map/ppermute | solution.py:149
  775.4 16.2 %collective-permute-done.76.rest_14_ = bf16[4,32,1024]{2,1,0:T(8,128)(2,1)S(1)} collective-permute-done((bf16[4,32,1024]{2,1,0:T(8,128)(2,1)S(1)}, bf16[4,32,1024]{2,1,0:T(8,128)(2,1)S(1)}, u32[]{:S(2)}, u32[]{:S(2)}) %collective-permute-start.76) | collective-permute-done | bytes 262176 | tf_op jit(solution)/shard_map/ppermute | solution.py:149
  793.5 31.5 %collective-permute-done.101.rest_8_ = bf16[8,32,1024]{2,1,0:T(8,128)(2,1)S(1)} collective-permute-done((bf16[8,32,1024]{2,1,0:T(8,128)(2,1)S(1)}, bf16[8,32,1024]{2,1,0:T(8,128)(2,1)S(1)}, u32[]{:S(2)}, u32[]{:S(2)}) %collective-permute-start.101) | collective-permute-done | bytes 524320 | tf_op jit(solution)/shard_map/ppermute | solution.py:149
  825.3 22.2 %collective-permute-done.102.rest_9_ = bf16[8,32,1024]{2,1,0:T(8,128)(2,1)S(1)} collective-permute-done((bf16[8,32,1024]{2,1,0:T(8,128)(2,1)S(1)}, bf16[8,32,1024]{2,1,0:T(8,128)(2,1)S(1)}, u32[]{:S(2)}, u32[]{:S(2)}) %collective-permute-start.102) | collective-permute-done | bytes 524320 | tf_op jit(solution)/shard_map/ppermute | solution.py:149
  847.5 22.5 %collective-permute-done.103.rest_10_ = bf16[8,32,1024]{2,1,0:T(8,128)(2,1)S(1)} collective-permute-done((bf16[8,32,1024]{2,1,0:T(8,128)(2,1)S(1)}, bf16[8,32,1024]{2,1,0:T(8,128)(2,1)S(1)}, u32[]{:S(2)}, u32[]{:S(2)}) %collective-permute-start.103) | collective-permute-done | bytes 524320 | tf_op jit(solution)/shard_map/ppermute | solution.py:149
  869.9 22.5 %collective-permute-done.104.rest_11_ = bf16[8,32,1024]{2,1,0:T(8,128)(2,1)S(1)} collective-permute-done((bf16[8,32,1024]{2,1,0:T(8,128)(2,1)S(1)}, bf16[8,32,1024]{2,1,0:T(8,128)(2,1)S(1)}, u32[]{:S(2)}, u32[]{:S(2)}) %collective-permute-start.104) | collective-permute-done | bytes 524320 | tf_op jit(solution)/shard_map/ppermute | solution.py:149
  892.4 12.4 %collective-permute-done.105.rest_12_ = bf16[8,32,1024]{2,1,0:T(8,128)(2,1)S(1)} collective-permute-done((bf16[8,32,1024]{2,1,0:T(8,128)(2,1)S(1)}, bf16[8,32,1024]{2,1,0:T(8,128)(2,1)S(1)}, u32[]{:S(2)}, u32[]{:S(2)}) %collective-permute-start.105) | collective-permute-done | bytes 524320 | tf_op jit(solution)/shard_map/ppermute | solution.py:149
  904.8 11.0 %collective-permute-done.106.rest_13_ = bf16[8,32,1024]{2,1,0:T(8,128)(2,1)S(1)} collective-permute-done((bf16[8,32,1024]{2,1,0:T(8,128)(2,1)S(1)}, bf16[8,32,1024]{2,1,0:T(8,128)(2,1)S(1)}, u32[]{:S(2)}, u32[]{:S(2)}) %collective-permute-start.106) | collective-permute-done | bytes 524320 | tf_op jit(solution)/shard_map/ppermute | solution.py:149
  915.9 10.7 collective-permute-done.107.rest_14_
  926.6 11.0 %collective-permute-done.108.rest_15_ = bf16[8,32,1024]{2,1,0:T(8,128)(2,1)S(1)} collective-permute-done((bf16[8,32,1024]{2,1,0:T(8,128)(2,1)S(1)}, bf16[8,32,1024]{2,1,0:T(8,128)(2,1)S(1)}, u32[]{:S(2)}, u32[]{:S(2)}) %collective-permute-start.108) | collective-permute-done | bytes 524320 | tf_op jit(solution)/shard_map/ppermute | solution.py:149
  942.1 26.0 %collective-permute-done.96.rest_3_ = bf16[8,32,1024]{2,1,0:T(8,128)(2,1)S(1)} collective-permute-done((bf16[8,32,1024]{2,1,0:T(8,128)(2,1)S(1)}, bf16[8,32,1024]{2,1,0:T(8,128)(2,1)S(1)}, u32[]{:S(2)}, u32[]{:S(2)}) %collective-permute-start.96) | collective-permute-done | bytes 524320 | tf_op jit(solution)/shard_map/ppermute | solution.py:149
  973.7 14.0 %gate_rows.9 = (bf16[8,512,1024]{2,1,0:T(8,128)(2,1)}, f32[8,1,512]{2,1,0:T(1,128)}) custom-call(s32[1]{0:T(128)} %bitcast.me_ref, bf16[2,8,512,1024]{3,2,1,0:T(8,128)(2,1)} %bitcast.159, bf16[512,512]{1,0:T(8,128)(2,1)} %w_ref.13, f32[1,1024]{1,0:T(1,128)} %bitcast.176, f32[1,1024]{1,0:T(1,128)} %bitcast.181, ...), custom_call_target="tpu_custom_call" | custom-call | tf_op jit(solution)/shard_map/gate_rows/pallas_call | solution.py:77
  990.5 8.1 gate_rows.8
  1021.1 27.1 %mlp_rows.5.rest_0_ = bf16[16,512,1024]{2,1,0:T(8,128)(2,1)} custom-call(bf16[8,512,1024]{2,1,0:T(8,128)(2,1)} %get-tuple-element.87.gated_ref, f32[8,1,512]{2,1,0:T(1,128)} %add.41.sq_ref, f32[1,1024]{1,0:T(1,128)} %bitcast.171, bf16[2,1024,512]{2,1,0:T(8,128)(2,1)} %all-gather.3.cloned.1.call-done.up_ref, ...), custom_call_target="tpu_custom_call" | custom-call | tf_op jit(solution)/shard_map/mlp_rows/pallas_call | solution.py:136
  1048.2 15.3 %mlp_rows.6.rest_0_ = bf16[16,512,1024]{2,1,0:T(8,128)(2,1)} custom-call(bf16[4,512,1024]{2,1,0:T(8,128)(2,1)} %get-tuple-element.69.gated_ref, f32[4,1,512]{2,1,0:T(1,128)} %add.40.sq_ref, f32[1,1024]{1,0:T(1,128)} %bitcast.172, bf16[2,1024,512]{2,1,0:T(8,128)(2,1)} %all-gather.3.cloned.1.call-done.up_ref, ...), custom_call_target="tpu_custom_call", output_to_operand_aliasing={{}: (5, {})} | custom-call | tf_op jit(solution)/shard_map/mlp_rows/pallas_call | solution.py:136
  1063.5 9.6 mlp_rows.7.rest_0_
  1073.2 6.4 mlp_rows.8.rest_0_
  1079.6 6.5 mlp_rows.9
  (426 shorter events, 251.1 us)
Async XLA Ops:
  6.5 1014.6 %all-gather.3.cloned.1.call-start = ((), (), s32[]{:S(2)}) async-start(), calls=%async_computation | async-start | bytes 2228224 | tf_op jit(solution)/shard_map/all_gather | solution.py:202
  21.2 37.5 %collective-permute-start.4 = (bf16[8,32,1024]{2,1,0:T(8,128)(2,1)}, bf16[8,32,1024]{2,1,0:T(8,128)(2,1)S(1)}, u32[]{:S(2)}, u32[]{:S(2)}) collective-permute-start(bf16[8,32,1024]{2,1,0:T(8,128)(2,1)} %get-tuple-element.52), channel_id=1, source_target_pairs={{0,10},{2,8},{4,14},{6,12},{8,2},{10,0},{12,6},{14,4},{16,26},{18,... | collective-permute-start | bytes 1572872 | tf_op jit(solution)/shard_map/ppermute | solution.py:149
  22.0 999.1 %all-gather.5.cloned.1.call-start = ((), (), s32[]{:S(2)}) async-start(), calls=%async_computation.1 | async-start | bytes 2228224 | tf_op jit(solution)/shard_map/all_gather | solution.py:203
  39.2 52.7 %collective-permute-start.5 = (bf16[8,32,1024]{2,1,0:T(8,128)(2,1)}, bf16[8,32,1024]{2,1,0:T(8,128)(2,1)S(1)}, u32[]{:S(2)}, u32[]{:S(2)}) collective-permute-start(bf16[8,32,1024]{2,1,0:T(8,128)(2,1)} %get-tuple-element.53), channel_id=1, source_target_pairs={{0,12},{2,14},{4,8},{6,10},{8,4},{10,6},{12,0},{14,2},{16,28},{18,... | collective-permute-start | bytes 1572872 | tf_op jit(solution)/shard_map/ppermute | solution.py:149
  42.6 59.9 %collective-permute-start.6 = (bf16[8,32,1024]{2,1,0:T(8,128)(2,1)}, bf16[8,32,1024]{2,1,0:T(8,128)(2,1)S(1)}, u32[]{:S(2)}, u32[]{:S(2)}) collective-permute-start(bf16[8,32,1024]{2,1,0:T(8,128)(2,1)} %get-tuple-element.54), channel_id=1, source_target_pairs={{0,14},{2,12},{4,10},{6,8},{8,6},{10,4},{12,2},{14,0},{16,30},{18,... | collective-permute-start | bytes 1572872 | tf_op jit(solution)/shard_map/ppermute | solution.py:149
  44.5 60.3 %collective-permute-start.7 = (bf16[8,32,1024]{2,1,0:T(8,128)(2,1)}, bf16[8,32,1024]{2,1,0:T(8,128)(2,1)S(1)}, u32[]{:S(2)}, u32[]{:S(2)}) collective-permute-start(bf16[8,32,1024]{2,1,0:T(8,128)(2,1)} %get-tuple-element.55), channel_id=1, source_target_pairs={{0,16},{2,18},{4,20},{6,22},{8,24},{10,26},{12,28},{14,30},{16,0},... | collective-permute-start | bytes 1572872 | tf_op jit(solution)/shard_map/ppermute | solution.py:149
  45.7 60.0 %collective-permute-start.8 = (bf16[8,32,1024]{2,1,0:T(8,128)(2,1)}, bf16[8,32,1024]{2,1,0:T(8,128)(2,1)S(1)}, u32[]{:S(2)}, u32[]{:S(2)}) collective-permute-start(bf16[8,32,1024]{2,1,0:T(8,128)(2,1)} %get-tuple-element.56), channel_id=1, source_target_pairs={{0,18},{2,16},{4,22},{6,20},{8,26},{10,24},{12,30},{14,28},{16,2},... | collective-permute-start | bytes 1572872 | tf_op jit(solution)/shard_map/ppermute | solution.py:149
  58.7 105.5 %collective-permute-start.9 = (bf16[8,32,1024]{2,1,0:T(8,128)(2,1)}, bf16[8,32,1024]{2,1,0:T(8,128)(2,1)S(1)}, u32[]{:S(2)}, u32[]{:S(2)}) collective-permute-start(bf16[8,32,1024]{2,1,0:T(8,128)(2,1)} %get-tuple-element.57), channel_id=1, source_target_pairs={{0,20},{2,22},{4,16},{6,18},{8,28},{10,30},{12,24},{14,26},{16,4},... | collective-permute-start | bytes 1572872 | tf_op jit(solution)/shard_map/ppermute | solution.py:149
  91.9 94.8 %collective-permute-start.10 = (bf16[8,32,1024]{2,1,0:T(8,128)(2,1)}, bf16[8,32,1024]{2,1,0:T(8,128)(2,1)S(1)}, u32[]{:S(2)}, u32[]{:S(2)}) collective-permute-start(bf16[8,32,1024]{2,1,0:T(8,128)(2,1)} %get-tuple-element.58), channel_id=1, source_target_pairs={{0,22},{2,20},{4,18},{6,16},{8,30},{10,28},{12,26},{14,24},{16,6},... | collective-permute-start | bytes 1572872 | tf_op jit(solution)/shard_map/ppermute | solution.py:149
  102.5 101.1 %collective-permute-start.11 = (bf16[8,32,1024]{2,1,0:T(8,128)(2,1)}, bf16[8,32,1024]{2,1,0:T(8,128)(2,1)S(1)}, u32[]{:S(2)}, u32[]{:S(2)}) collective-permute-start(bf16[8,32,1024]{2,1,0:T(8,128)(2,1)} %get-tuple-element.59), channel_id=1, source_target_pairs={{0,24},{2,26},{4,28},{6,30},{8,16},{10,18},{12,20},{14,22},{16,8},... | collective-permute-start | bytes 1572872 | tf_op jit(solution)/shard_map/ppermute | solution.py:149
  104.8 109.7 %collective-permute-start.12 = (bf16[8,32,1024]{2,1,0:T(8,128)(2,1)}, bf16[8,32,1024]{2,1,0:T(8,128)(2,1)S(1)}, u32[]{:S(2)}, u32[]{:S(2)}) collective-permute-start(bf16[8,32,1024]{2,1,0:T(8,128)(2,1)} %get-tuple-element.60), channel_id=1, source_target_pairs={{0,26},{2,24},{4,30},{6,28},{8,18},{10,16},{12,22},{14,20},{16,10}... | collective-permute-start | bytes 1572872 | tf_op jit(solution)/shard_map/ppermute | solution.py:149
  105.7 121.1 %collective-permute-start.13 = (bf16[8,32,1024]{2,1,0:T(8,128)(2,1)S(1)}, bf16[8,32,1024]{2,1,0:T(8,128)(2,1)S(1)}, u32[]{:S(2)}, u32[]{:S(2)}) collective-permute-start(bf16[8,32,1024]{2,1,0:T(8,128)(2,1)S(1)} %copy-done.85), channel_id=1, source_target_pairs={{0,28},{2,30},{4,24},{6,26},{8,20},{10,22},{12,16},{14,18},{16,12}... | collective-permute-start | bytes 1572872 | tf_op jit(solution)/shard_map/ppermute | solution.py:149
  164.2 74.0 %collective-permute-start.14 = (bf16[8,32,1024]{2,1,0:T(8,128)(2,1)S(1)}, bf16[8,32,1024]{2,1,0:T(8,128)(2,1)S(1)}, u32[]{:S(2)}, u32[]{:S(2)}) collective-permute-start(bf16[8,32,1024]{2,1,0:T(8,128)(2,1)S(1)} %copy-done.83), channel_id=1, source_target_pairs={{0,30},{2,28},{4,26},{6,24},{8,22},{10,20},{12,18},{14,16},{16,14}... | collective-permute-start | bytes 1572872 | tf_op jit(solution)/shard_map/ppermute | solution.py:149
  186.7 52.4 %collective-permute-start.79 = (bf16[8,32,1024]{2,1,0:T(8,128)(2,1)S(1)}, bf16[8,32,1024]{2,1,0:T(8,128)(2,1)S(1)}, u32[]{:S(2)}, u32[]{:S(2)}) collective-permute-start(bf16[8,32,1024]{2,1,0:T(8,128)(2,1)S(1)} %copy-done.88), channel_id=1, source_target_pairs={{0,2},{2,0},{4,6},{6,4},{8,10},{10,8},{12,14},{14,12},{16,18},{18,... | collective-permute-start | bytes 1572872 | tf_op jit(solution)/shard_map/ppermute | solution.py:149
  203.6 37.8 %collective-permute-start.80 = (bf16[8,32,1024]{2,1,0:T(8,128)(2,1)S(1)}, bf16[8,32,1024]{2,1,0:T(8,128)(2,1)S(1)}, u32[]{:S(2)}, u32[]{:S(2)}) collective-permute-start(bf16[8,32,1024]{2,1,0:T(8,128)(2,1)S(1)} %copy-done.87), channel_id=1, source_target_pairs={{0,4},{2,6},{4,0},{6,2},{8,12},{10,14},{12,8},{14,10},{16,20},{18,... | collective-permute-start | bytes 1572872 | tf_op jit(solution)/shard_map/ppermute | solution.py:149
  214.6 35.5 %collective-permute-start.81 = (bf16[8,32,1024]{2,1,0:T(8,128)(2,1)S(1)}, bf16[8,32,1024]{2,1,0:T(8,128)(2,1)S(1)}, u32[]{:S(2)}, u32[]{:S(2)}) collective-permute-start(bf16[8,32,1024]{2,1,0:T(8,128)(2,1)S(1)} %copy-done.86), channel_id=1, source_target_pairs={{0,6},{2,4},{4,2},{6,0},{8,14},{10,12},{12,10},{14,8},{16,22},{18,... | collective-permute-start | bytes 1572872 | tf_op jit(solution)/shard_map/ppermute | solution.py:149
  239.1 44.1 %collective-permute-start.84 = (bf16[8,32,1024]{2,1,0:T(8,128)(2,1)S(1)}, bf16[8,32,1024]{2,1,0:T(8,128)(2,1)S(1)}, u32[]{:S(2)}, u32[]{:S(2)}) collective-permute-start(bf16[8,32,1024]{2,1,0:T(8,128)(2,1)S(1)} %copy-done.81), channel_id=1, source_target_pairs={{0,12},{2,14},{4,8},{6,10},{8,4},{10,6},{12,0},{14,2},{16,28},{18,... | collective-permute-start | bytes 1572872 | tf_op jit(solution)/shard_map/ppermute | solution.py:149
  241.4 52.4 %collective-permute-start.85 = (bf16[8,32,1024]{2,1,0:T(8,128)(2,1)S(1)}, bf16[8,32,1024]{2,1,0:T(8,128)(2,1)S(1)}, u32[]{:S(2)}, u32[]{:S(2)}) collective-permute-start(bf16[8,32,1024]{2,1,0:T(8,128)(2,1)S(1)} %copy-done.80), channel_id=1, source_target_pairs={{0,14},{2,12},{4,10},{6,8},{8,6},{10,4},{12,2},{14,0},{16,30},{18,... | collective-permute-start | bytes 1572872 | tf_op jit(solution)/shard_map/ppermute | solution.py:149
  250.1 45.1 %collective-permute-start.86 = (bf16[8,32,1024]{2,1,0:T(8,128)(2,1)S(1)}, bf16[8,32,1024]{2,1,0:T(8,128)(2,1)S(1)}, u32[]{:S(2)}, u32[]{:S(2)}) collective-permute-start(bf16[8,32,1024]{2,1,0:T(8,128)(2,1)S(1)} %copy-done.79), channel_id=1, source_target_pairs={{0,16},{2,18},{4,20},{6,22},{8,24},{10,26},{12,28},{14,30},{16,0},... | collective-permute-start | bytes 1572872 | tf_op jit(solution)/shard_map/ppermute | solution.py:149
  250.9 45.4 %collective-permute-start.87 = (bf16[8,32,1024]{2,1,0:T(8,128)(2,1)S(1)}, bf16[8,32,1024]{2,1,0:T(8,128)(2,1)S(1)}, u32[]{:S(2)}, u32[]{:S(2)}) collective-permute-start(bf16[8,32,1024]{2,1,0:T(8,128)(2,1)S(1)} %copy-done.78), channel_id=1, source_target_pairs={{0,18},{2,16},{4,22},{6,20},{8,26},{10,24},{12,30},{14,28},{16,2},... | collective-permute-start | bytes 1572872 | tf_op jit(solution)/shard_map/ppermute | solution.py:149
  255.1 108.2 %collective-permute-start.88 = (bf16[8,32,1024]{2,1,0:T(8,128)(2,1)S(1)}, bf16[8,32,1024]{2,1,0:T(8,128)(2,1)S(1)}, u32[]{:S(2)}, u32[]{:S(2)}) collective-permute-start(bf16[8,32,1024]{2,1,0:T(8,128)(2,1)S(1)} %copy-done.77), channel_id=1, source_target_pairs={{0,20},{2,22},{4,16},{6,18},{8,28},{10,30},{12,24},{14,26},{16,4},... | collective-permute-start | bytes 1572872 | tf_op jit(solution)/shard_map/ppermute | solution.py:149
  283.2 102.5 %collective-permute-start.89 = (bf16[8,32,1024]{2,1,0:T(8,128)(2,1)S(1)}, bf16[8,32,1024]{2,1,0:T(8,128)(2,1)S(1)}, u32[]{:S(2)}, u32[]{:S(2)}) collective-permute-start(bf16[8,32,1024]{2,1,0:T(8,128)(2,1)S(1)} %copy-done.76), channel_id=1, source_target_pairs={{0,22},{2,20},{4,18},{6,16},{8,30},{10,28},{12,26},{14,24},{16,6},... | collective-permute-start | bytes 1572872 | tf_op jit(solution)/shard_map/ppermute | solution.py:149
  293.8 105.6 %collective-permute-start.90 = (bf16[8,32,1024]{2,1,0:T(8,128)(2,1)S(1)}, bf16[8,32,1024]{2,1,0:T(8,128)(2,1)S(1)}, u32[]{:S(2)}, u32[]{:S(2)}) collective-permute-start(bf16[8,32,1024]{2,1,0:T(8,128)(2,1)S(1)} %copy-done.75), channel_id=1, source_target_pairs={{0,24},{2,26},{4,28},{6,30},{8,16},{10,18},{12,20},{14,22},{16,8},... | collective-permute-start | bytes 1572872 | tf_op jit(solution)/shard_map/ppermute | solution.py:149
  295.1 113.1 %collective-permute-start.91 = (bf16[8,32,1024]{2,1,0:T(8,128)(2,1)S(1)}, bf16[8,32,1024]{2,1,0:T(8,128)(2,1)S(1)}, u32[]{:S(2)}, u32[]{:S(2)}) collective-permute-start(bf16[8,32,1024]{2,1,0:T(8,128)(2,1)S(1)} %copy-done.74), channel_id=1, source_target_pairs={{0,26},{2,24},{4,30},{6,28},{8,18},{10,16},{12,22},{14,20},{16,10}... | collective-permute-start | bytes 1572872 | tf_op jit(solution)/shard_map/ppermute | solution.py:149
  296.4 125.8 %collective-permute-start.92 = (bf16[8,32,1024]{2,1,0:T(8,128)(2,1)S(1)}, bf16[8,32,1024]{2,1,0:T(8,128)(2,1)S(1)}, u32[]{:S(2)}, u32[]{:S(2)}) collective-permute-start(bf16[8,32,1024]{2,1,0:T(8,128)(2,1)S(1)} %copy-done.73), channel_id=1, source_target_pairs={{0,28},{2,30},{4,24},{6,26},{8,20},{10,22},{12,16},{14,18},{16,12}... | collective-permute-start | bytes 1572872 | tf_op jit(solution)/shard_map/ppermute | solution.py:149
  363.3 74.1 %collective-permute-start.93 = (bf16[8,32,1024]{2,1,0:T(8,128)(2,1)S(1)}, bf16[8,32,1024]{2,1,0:T(8,128)(2,1)S(1)}, u32[]{:S(2)}, u32[]{:S(2)}) collective-permute-start(bf16[8,32,1024]{2,1,0:T(8,128)(2,1)S(1)} %copy-done.72), channel_id=1, source_target_pairs={{0,30},{2,28},{4,26},{6,24},{8,22},{10,20},{12,18},{14,16},{16,14}... | collective-permute-start | bytes 1572872 | tf_op jit(solution)/shard_map/ppermute | solution.py:149
  689.4 45.7 %collective-permute-start.72 = (bf16[4,32,1024]{2,1,0:T(8,128)(2,1)S(1)}, bf16[4,32,1024]{2,1,0:T(8,128)(2,1)S(1)}, u32[]{:S(2)}, u32[]{:S(2)}) collective-permute-start(bf16[4,32,1024]{2,1,0:T(8,128)(2,1)S(1)} %get-tuple-element.112), channel_id=1, source_target_pairs={{0,20},{2,22},{4,16},{6,18},{8,28},{10,30},{12,24},{14,26},{16,4},... | collective-permute-start | bytes 786440 | tf_op jit(solution)/shard_map/ppermute | solution.py:149
  694.9 45.8 %collective-permute-start.73 = (bf16[4,32,1024]{2,1,0:T(8,128)(2,1)S(1)}, bf16[4,32,1024]{2,1,0:T(8,128)(2,1)S(1)}, u32[]{:S(2)}, u32[]{:S(2)}) collective-permute-start(bf16[4,32,1024]{2,1,0:T(8,128)(2,1)S(1)} %get-tuple-element.111), channel_id=1, source_target_pairs={{0,22},{2,20},{4,18},{6,16},{8,30},{10,28},{12,26},{14,24},{16,6},... | collective-permute-start | bytes 786440 | tf_op jit(solution)/shard_map/ppermute | solution.py:149
  700.7 46.8 %collective-permute-start.74 = (bf16[4,32,1024]{2,1,0:T(8,128)(2,1)S(1)}, bf16[4,32,1024]{2,1,0:T(8,128)(2,1)S(1)}, u32[]{:S(2)}, u32[]{:S(2)}) collective-permute-start(bf16[4,32,1024]{2,1,0:T(8,128)(2,1)S(1)} %get-tuple-element.110), channel_id=1, source_target_pairs={{0,24},{2,26},{4,28},{6,30},{8,16},{10,18},{12,20},{14,22},{16,8},... | collective-permute-start | bytes 786440 | tf_op jit(solution)/shard_map/ppermute | solution.py:149
  701.4 74.0 %collective-permute-start.75 = (bf16[4,32,1024]{2,1,0:T(8,128)(2,1)S(1)}, bf16[4,32,1024]{2,1,0:T(8,128)(2,1)S(1)}, u32[]{:S(2)}, u32[]{:S(2)}) collective-permute-start(bf16[4,32,1024]{2,1,0:T(8,128)(2,1)S(1)} %get-tuple-element.109), channel_id=1, source_target_pairs={{0,26},{2,24},{4,30},{6,28},{8,18},{10,16},{12,22},{14,20},{16,10}... | collective-permute-start | bytes 786440 | tf_op jit(solution)/shard_map/ppermute | solution.py:149
  703.0 88.6 %collective-permute-start.76 = (bf16[4,32,1024]{2,1,0:T(8,128)(2,1)S(1)}, bf16[4,32,1024]{2,1,0:T(8,128)(2,1)S(1)}, u32[]{:S(2)}, u32[]{:S(2)}) collective-permute-start(bf16[4,32,1024]{2,1,0:T(8,128)(2,1)S(1)} %get-tuple-element.108), channel_id=1, source_target_pairs={{0,28},{2,30},{4,24},{6,26},{8,20},{10,22},{12,16},{14,18},{16,12}... | collective-permute-start | bytes 786440 | tf_op jit(solution)/shard_map/ppermute | solution.py:149
  735.1 56.5 %collective-permute-start.100 = (bf16[8,32,1024]{2,1,0:T(8,128)(2,1)S(1)}, bf16[8,32,1024]{2,1,0:T(8,128)(2,1)S(1)}, u32[]{:S(2)}, u32[]{:S(2)}) collective-permute-start(bf16[8,32,1024]{2,1,0:T(8,128)(2,1)S(1)} %get-tuple-element.97), channel_id=1, source_target_pairs={{0,14},{2,12},{4,10},{6,8},{8,6},{10,4},{12,2},{14,0},{16,30},{18,... | collective-permute-start | bytes 1572872 | tf_op jit(solution)/shard_map/ppermute | solution.py:149
  740.7 84.3 %collective-permute-start.101 = (bf16[8,32,1024]{2,1,0:T(8,128)(2,1)S(1)}, bf16[8,32,1024]{2,1,0:T(8,128)(2,1)S(1)}, u32[]{:S(2)}, u32[]{:S(2)}) collective-permute-start(bf16[8,32,1024]{2,1,0:T(8,128)(2,1)S(1)} %get-tuple-element.96), channel_id=1, source_target_pairs={{0,16},{2,18},{4,20},{6,22},{8,24},{10,26},{12,28},{14,30},{16,0},... | collective-permute-start | bytes 1572872 | tf_op jit(solution)/shard_map/ppermute | solution.py:149
  747.5 99.9 %collective-permute-start.102 = (bf16[8,32,1024]{2,1,0:T(8,128)(2,1)S(1)}, bf16[8,32,1024]{2,1,0:T(8,128)(2,1)S(1)}, u32[]{:S(2)}, u32[]{:S(2)}) collective-permute-start(bf16[8,32,1024]{2,1,0:T(8,128)(2,1)S(1)} %get-tuple-element.95), channel_id=1, source_target_pairs={{0,18},{2,16},{4,22},{6,20},{8,26},{10,24},{12,30},{14,28},{16,2},... | collective-permute-start | bytes 1572872 | tf_op jit(solution)/shard_map/ppermute | solution.py:149
  775.4 94.5 %collective-permute-start.103 = (bf16[8,32,1024]{2,1,0:T(8,128)(2,1)S(1)}, bf16[8,32,1024]{2,1,0:T(8,128)(2,1)S(1)}, u32[]{:S(2)}, u32[]{:S(2)}) collective-permute-start(bf16[8,32,1024]{2,1,0:T(8,128)(2,1)S(1)} %get-tuple-element.94), channel_id=1, source_target_pairs={{0,20},{2,22},{4,16},{6,18},{8,28},{10,30},{12,24},{14,26},{16,4},... | collective-permute-start | bytes 1572872 | tf_op jit(solution)/shard_map/ppermute | solution.py:149
  791.6 100.8 %collective-permute-start.104 = (bf16[8,32,1024]{2,1,0:T(8,128)(2,1)S(1)}, bf16[8,32,1024]{2,1,0:T(8,128)(2,1)S(1)}, u32[]{:S(2)}, u32[]{:S(2)}) collective-permute-start(bf16[8,32,1024]{2,1,0:T(8,128)(2,1)S(1)} %get-tuple-element.93), channel_id=1, source_target_pairs={{0,22},{2,20},{4,18},{6,16},{8,30},{10,28},{12,26},{14,24},{16,6},... | collective-permute-start | bytes 1572872 | tf_op jit(solution)/shard_map/ppermute | solution.py:149
  791.6 113.2 %collective-permute-start.105 = (bf16[8,32,1024]{2,1,0:T(8,128)(2,1)S(1)}, bf16[8,32,1024]{2,1,0:T(8,128)(2,1)S(1)}, u32[]{:S(2)}, u32[]{:S(2)}) collective-permute-start(bf16[8,32,1024]{2,1,0:T(8,128)(2,1)S(1)} %get-tuple-element.92), channel_id=1, source_target_pairs={{0,24},{2,26},{4,28},{6,30},{8,16},{10,18},{12,20},{14,22},{16,8},... | collective-permute-start | bytes 1572872 | tf_op jit(solution)/shard_map/ppermute | solution.py:149
  825.0 90.9 %collective-permute-start.106 = (bf16[8,32,1024]{2,1,0:T(8,128)(2,1)S(1)}, bf16[8,32,1024]{2,1,0:T(8,128)(2,1)S(1)}, u32[]{:S(2)}, u32[]{:S(2)}) collective-permute-start(bf16[8,32,1024]{2,1,0:T(8,128)(2,1)S(1)} %get-tuple-element.91), channel_id=1, source_target_pairs={{0,26},{2,24},{4,30},{6,28},{8,18},{10,16},{12,22},{14,20},{16,10}... | collective-permute-start | bytes 1572872 | tf_op jit(solution)/shard_map/ppermute | solution.py:149
  847.5 79.1 %collective-permute-start.107 = (bf16[8,32,1024]{2,1,0:T(8,128)(2,1)S(1)}, bf16[8,32,1024]{2,1,0:T(8,128)(2,1)S(1)}, u32[]{:S(2)}, u32[]{:S(2)}) collective-permute-start(bf16[8,32,1024]{2,1,0:T(8,128)(2,1)S(1)} %get-tuple-element.90), channel_id=1, source_target_pairs={{0,28},{2,30},{4,24},{6,26},{8,20},{10,22},{12,16},{14,18},{16,12}... | collective-permute-start | bytes 1572872 | tf_op jit(solution)/shard_map/ppermute | solution.py:149
  869.9 67.7 %collective-permute-start.108 = (bf16[8,32,1024]{2,1,0:T(8,128)(2,1)S(1)}, bf16[8,32,1024]{2,1,0:T(8,128)(2,1)S(1)}, u32[]{:S(2)}, u32[]{:S(2)}) collective-permute-start(bf16[8,32,1024]{2,1,0:T(8,128)(2,1)S(1)} %get-tuple-element.89), channel_id=1, source_target_pairs={{0,30},{2,28},{4,26},{6,24},{8,22},{10,20},{12,18},{14,16},{16,14}... | collective-permute-start | bytes 1572872 | tf_op jit(solution)/shard_map/ppermute | solution.py:149
  892.4 45.2 %collective-permute-start.94 = (bf16[8,32,1024]{2,1,0:T(8,128)(2,1)S(1)}, bf16[8,32,1024]{2,1,0:T(8,128)(2,1)S(1)}, u32[]{:S(2)}, u32[]{:S(2)}) collective-permute-start(bf16[8,32,1024]{2,1,0:T(8,128)(2,1)S(1)} %get-tuple-element.103), channel_id=1, source_target_pairs={{0,2},{2,0},{4,6},{6,4},{8,10},{10,8},{12,14},{14,12},{16,18},{18,... | collective-permute-start | bytes 1572872 | tf_op jit(solution)/shard_map/ppermute | solution.py:149
  904.8 37.3 %collective-permute-start.95 = (bf16[8,32,1024]{2,1,0:T(8,128)(2,1)S(1)}, bf16[8,32,1024]{2,1,0:T(8,128)(2,1)S(1)}, u32[]{:S(2)}, u32[]{:S(2)}) collective-permute-start(bf16[8,32,1024]{2,1,0:T(8,128)(2,1)S(1)} %get-tuple-element.102), channel_id=1, source_target_pairs={{0,4},{2,6},{4,0},{6,2},{8,12},{10,14},{12,8},{14,10},{16,20},{18,... | collective-permute-start | bytes 1572872 | tf_op jit(solution)/shard_map/ppermute | solution.py:149
  915.9 52.2 %collective-permute-start.96 = (bf16[8,32,1024]{2,1,0:T(8,128)(2,1)S(1)}, bf16[8,32,1024]{2,1,0:T(8,128)(2,1)S(1)}, u32[]{:S(2)}, u32[]{:S(2)}) collective-permute-start(bf16[8,32,1024]{2,1,0:T(8,128)(2,1)S(1)} %get-tuple-element.101), channel_id=1, source_target_pairs={{0,6},{2,4},{4,2},{6,0},{8,14},{10,12},{12,10},{14,8},{16,22},{18,... | collective-permute-start | bytes 1572872 | tf_op jit(solution)/shard_map/ppermute | solution.py:149
  926.6 43.0 %collective-permute-start.97 = (bf16[8,32,1024]{2,1,0:T(8,128)(2,1)S(1)}, bf16[8,32,1024]{2,1,0:T(8,128)(2,1)S(1)}, u32[]{:S(2)}, u32[]{:S(2)}) collective-permute-start(bf16[8,32,1024]{2,1,0:T(8,128)(2,1)S(1)} %get-tuple-element.100), channel_id=1, source_target_pairs={{0,8},{2,10},{4,12},{6,14},{8,0},{10,2},{12,4},{14,6},{16,24},{18,... | collective-permute-start | bytes 1572872 | tf_op jit(solution)/shard_map/ppermute | solution.py:149
  942.1 45.6 %collective-permute-start.77 = (bf16[4,32,1024]{2,1,0:T(8,128)(2,1)}, bf16[4,32,1024]{2,1,0:T(8,128)(2,1)S(1)}, u32[]{:S(2)}, u32[]{:S(2)}) collective-permute-start(bf16[4,32,1024]{2,1,0:T(8,128)(2,1)} %get-tuple-element.107), channel_id=1, source_target_pairs={{0,30},{2,28},{4,26},{6,24},{8,22},{10,20},{12,18},{14,16},{16,14}... | collective-permute-start | bytes 786440 | tf_op jit(solution)/shard_map/ppermute | solution.py:149
  969.6 35.2 %collective-permute-start.24 = (bf16[1,32,1024]{2,1,0:T(8,128)(2,1)}, bf16[1,32,1024]{2,1,0:T(8,128)(2,1)S(1)}, u32[]{:S(2)}, u32[]{:S(2)}) collective-permute-start(bf16[1,32,1024]{2,1,0:T(8,128)(2,1)} %get-tuple-element.160), channel_id=1, source_target_pairs={{0,20},{2,22},{4,16},{6,18},{8,28},{10,30},{12,24},{14,26},{16,4},... | collective-permute-start | bytes 196616 | tf_op jit(solution)/shard_map/ppermute | solution.py:149
  969.6 40.3 %collective-permute-start.25 = (bf16[1,32,1024]{2,1,0:T(8,128)(2,1)}, bf16[1,32,1024]{2,1,0:T(8,128)(2,1)}, u32[]{:S(2)}, u32[]{:S(2)}) collective-permute-start(bf16[1,32,1024]{2,1,0:T(8,128)(2,1)} %get-tuple-element.159), channel_id=1, source_target_pairs={{0,22},{2,20},{4,18},{6,16},{8,30},{10,28},{12,26},{14,24},{16,6},... | collective-permute-start | bytes 196616 | tf_op jit(solution)/shard_map/ppermute | solution.py:149
  972.7 37.9 %collective-permute-start.26 = (bf16[1,32,1024]{2,1,0:T(8,128)(2,1)}, bf16[1,32,1024]{2,1,0:T(8,128)(2,1)}, u32[]{:S(2)}, u32[]{:S(2)}) collective-permute-start(bf16[1,32,1024]{2,1,0:T(8,128)(2,1)} %get-tuple-element.158), channel_id=1, source_target_pairs={{0,24},{2,26},{4,28},{6,30},{8,16},{10,18},{12,20},{14,22},{16,8},... | collective-permute-start | bytes 196616 | tf_op jit(solution)/shard_map/ppermute | solution.py:149
  (153 other events, 8575.9 us)
Sparse Core Ops, SparseCore 0:
  22.2 137.1 all-gather.2
  566.6 50.8 all-gather.4

commit v2 on v0

--- a/solution.py
+++ b/solution.py
@@ -1,10 +1,289 @@
+import functools
+
 import jax
 import jax.numpy as jnp
 from jax import lax
+from jax.experimental import pallas as pl
+from jax.experimental.pallas import tpu as pltpu
 from jax.sharding import PartitionSpec as P
 
-
-def local(
+VMEM_BYTES = 56 * 1024 * 1024
+EPS = 1e-06
+RETURN_ROWS = ((8,), (6, 2))
+GATE_ROWS = 4
+MLP_ROWS = 4
+
+
+def params():
+    return pltpu.CompilerParams(vmem_limit_bytes=VMEM_BYTES)
+
+
+def first_kernel(tok_ref, w_ref, tw_ref, out_ref):
+    a = pl.program_id(0)
+    res = jnp.dot(w_ref[...], tok_ref[0, 0], preferred_element_type=jnp.float32)
+    cols = tw_ref[...].T
+    lane = lax.broadcasted_iota(jnp.int32, cols.shape, 1)
+    tw = jnp.sum(jnp.where(lane == a, cols, 0.0), axis=1, keepdims=True)
+    n, _, rows, ch = out_ref.shape
+    out_ref[...] = (res * tw).astype(jnp.bfloat16).reshape(n, 1, rows, ch)
+
+
+def first_section(blocked, inner_forward, twiddle, s, n):
+    _, a_dev, inner, ch = blocked.shape
+    rows = inner // n
+    return pl.pallas_call(
+        first_kernel,
+        grid=(a_dev,),
+        in_specs=[
+            pl.BlockSpec((1, 1, inner, ch), lambda a: (s, a, 0, 0)),
+            pl.BlockSpec((inner, inner), lambda a: (0, 0)),
+            pl.BlockSpec((a_dev, inner), lambda a: (0, 0)),
+        ],
+        out_specs=pl.BlockSpec((n, 1, rows, ch), lambda a: (0, a, 0, 0)),
+        out_shape=jax.ShapeDtypeStruct((n, a_dev, rows, ch), jnp.bfloat16),
+        compiler_params=params(),
+        name="first_section",
+    )(blocked, inner_forward, twiddle)
+
+
+def outer_kernel(groups, fwd_ref, inv_ref, tw_ref, freq_ref, spread_ref, *rest):
+    outs, (xs, fs, ys) = rest[:-3], rest[-3:]
+    steps, outer, block = xs.shape
+    xs[...] = jnp.swapaxes(spread_ref[...].astype(jnp.float32), 0, 1)
+    fs[...] = jnp.swapaxes(freq_ref[...].astype(jnp.float32), 0, 1)
+    tw = tw_ref[0]
+    for k in range(steps):
+        spectrum = jnp.dot(
+            fwd_ref[...], xs[k].astype(jnp.bfloat16), preferred_element_type=jnp.float32
+        )
+        spectrum = (spectrum * fs[k]).astype(jnp.bfloat16)
+        two = jnp.dot(inv_ref[...], spectrum, preferred_element_type=jnp.float32)
+        ys[k] = two * tw[:, k : k + 1]
+    res = jnp.swapaxes(ys[...], 0, 1).astype(jnp.bfloat16)
+    n = outs[0].shape[0]
+    res = res.reshape(n, outer // n, steps, block)
+    first = 0
+    for out, count in zip(outs, groups):
+        out[...] = res[:, first : first + count]
+        first += count
+
+
+def outer_section(spread, forward, inverse, tw, freq, groups, n):
+    outer, k_dev, ch = freq.shape
+    rows, block = min(16, k_dev), min(256, ch)
+    tw = tw.reshape(outer, k_dev // rows, rows).swapaxes(0, 1)
+    return pl.pallas_call(
+        functools.partial(outer_kernel, groups),
+        grid=(k_dev // rows, ch // block),
+        in_specs=[
+            pl.BlockSpec((outer, outer), lambda h, c: (0, 0)),
+            pl.BlockSpec((outer, outer), lambda h, c: (0, 0)),
+            pl.BlockSpec((1, outer, rows), lambda h, c: (h, 0, 0)),
+            pl.BlockSpec((outer, rows, block), lambda h, c: (0, h, c)),
+            pl.BlockSpec((outer, rows, block), lambda h, c: (0, h, c)),
+        ],
+        out_specs=[
+            pl.BlockSpec((n, count, rows, block), lambda h, c: (0, 0, h, c)) for count in groups
+        ],
+        out_shape=[
+            jax.ShapeDtypeStruct((n, count, k_dev, ch), jnp.bfloat16) for count in groups
+        ],
+        scratch_shapes=[pltpu.VMEM((rows, outer, block), jnp.float32)] * 3,
+        compiler_params=params(),
+        name="outer_section",
+    )(forward, inverse, tw, freq, spread)
+
+
+def gate_kernel(tok_ref, w_ref, gain_ref, bias_ref, part_ref, gated_ref, sq_ref):
+    flat = tok_ref[0, 0].astype(jnp.float32)
+    section = part_ref[...].reshape(flat.shape)
+    mixed = jnp.dot(w_ref[...], section, preferred_element_type=jnp.float32)
+    gate = jax.nn.sigmoid(flat * gain_ref[...] + bias_ref[...])
+    gated = (flat + gate * mixed).astype(jnp.bfloat16)
+    gated_ref[0] = gated
+    g = gated.astype(jnp.float32)
+    sq = g * g
+    part = sq[:, :128]
+    for c in range(128, sq.shape[1], 128):
+        part = part + sq[:, c : c + 128]
+    sq_ref[0] = jnp.sum(part.T, axis=0, keepdims=True)
+
+
+def gate_rows(blocked, inner_inverse, gain, bias, parts, s, first, skip, count):
+    _, _, inner, ch = blocked.shape
+    n, _, rows, _ = parts.shape
+    return pl.pallas_call(
+        gate_kernel,
+        grid=(count,),
+        in_specs=[
+            pl.BlockSpec((1, 1, inner, ch), lambda j: (s, first + skip + j, 0, 0)),
+            pl.BlockSpec((inner, inner), lambda j: (0, 0)),
+            pl.BlockSpec((1, ch), lambda j: (0, 0)),
+            pl.BlockSpec((1, ch), lambda j: (0, 0)),
+            pl.BlockSpec((n, 1, rows, ch), lambda j: (0, skip + j, 0, 0)),
+        ],
+        out_specs=[
+            pl.BlockSpec((1, inner, ch), lambda j: (j, 0, 0)),
+            pl.BlockSpec((1, 1, inner), lambda j: (j, 0, 0)),
+        ],
+        out_shape=[
+            jax.ShapeDtypeStruct((count, inner, ch), jnp.bfloat16),
+            jax.ShapeDtypeStruct((count, 1, inner), jnp.float32),
+        ],
+        compiler_params=params(),
+        name="gate_rows",
+    )(blocked, inner_inverse, gain, bias, parts)
+
+
+def mlp_kernel(width, gated_ref, sq_ref, gain_ref, weight_ref, *rest):
+    out_ref = rest[-1]
+    _, blocks, _, wb = weight_ref.shape
+    scale = lax.rsqrt(sq_ref[0] * (1.0 / width) + EPS)
+    scale = jnp.broadcast_to(scale, (128, scale.shape[1])).T[:, :1]
+    for b in range(blocks):
+        cols = slice(b * wb, (b + 1) * wb)
+        g = gated_ref[0, :, cols].astype(jnp.float32)
+        normed = (g * scale * gain_ref[:, cols]).astype(jnp.bfloat16)
+        lifted = lax.dot_general(
+            normed, weight_ref[0, b], (((1,), (1,)), ((), ())), preferred_element_type=jnp.float32
+        )
+        hidden = jax.nn.gelu(lifted, approximate=True).astype(jnp.bfloat16)
+        lowered = jnp.dot(hidden, weight_ref[1, b], preferred_element_type=jnp.float32)
+        out_ref[0, :, cols] = (g + lowered).astype(jnp.bfloat16)
+
+
+def mlp_rows(gated, sq, gain, weights, out, skip, count, first, total, width):
+    _, inner, ch = gated.shape
+    specs = [
+        pl.BlockSpec((1, inner, ch), lambda j: (skip + j, 0, 0)),
+        pl.BlockSpec((1, 1, inner), lambda j: (skip + j, 0, 0)),
+        pl.BlockSpec((1, ch), lambda j: (0, 0)),
+        pl.BlockSpec(weights.shape, lambda j: (0, 0, 0, 0), pipeline_mode=pl.Buffered(1)),
+    ]
+    args = [gated, sq, gain, weights]
+    aliases = {}
+    if out is not None:
+        specs.append(pl.BlockSpec(memory_space=pl.ANY))
+        args.append(out)
+        aliases = {4: 0}
+    return pl.pallas_call(
+        functools.partial(mlp_kernel, width),
+        grid=(count,),
+        in_specs=specs,
+        out_specs=pl.BlockSpec((1, inner, ch), lambda j: (first + j, 0, 0)),
+        out_shape=jax.ShapeDtypeStruct((total, inner, ch), jnp.bfloat16),
+        input_output_aliases=aliases,
+        compiler_params=params(),
+        name="mlp_rows",
+    )(*args)
+
+
+def after(x, *deps):
+    return lax.optimization_barrier((x,) + deps)[0]
+
+
+def after(x, *deps):
+    return lax.optimization_barrier((x,) + deps)[0]
+
+
+def exchange(x):
+    return lax.all_to_all(x, "seq", split_axis=0, concat_axis=0, tiled=True)
+
+
+def more_hidden(weights, n, step):
+    other = lax.ppermute(weights, "seq", [(j, j ^ step) for j in range(n)])
+    return jnp.concatenate([weights, other], axis=2)
+
+
+def local_blocks(
+    tokens,
+    inner_forward,
+    outer_forward,
+    twiddle_forward,
+    freq_kernel,
+    outer_inverse,
+    inner_inverse,
+    twiddle_inverse,
+    gate_gain,
+    gate_bias,
+    norm_gain,
+    up_weight,
+    down_weight,
+):
+
+    seqs, tok_dev, ch = tokens.shape
+    inner = inner_forward.shape[0]
+    a_dev = tok_dev // inner
+    n = lax.axis_size("seq")
+    n_ch = lax.axis_size("ch")
+    my_ch = lax.axis_index("ch")
+    outer = n * a_dev
+    blocked = tokens.reshape(seqs, a_dev, inner, ch)
+    norm = lax.dynamic_slice_in_dim(norm_gain, my_ch * ch, ch, 0).reshape(1, ch)
+    gain, bias = gate_gain.reshape(1, ch), gate_bias.reshape(1, ch)
+    held = ch // up_weight.shape[2]
+    weights = lax.dynamic_slice_in_dim(
+        jnp.stack([up_weight, down_weight]), my_ch * held, held, 1
+    )
+    weights = more_hidden(weights, n, n // 2)
+
+    parts = [
+        first_section(blocked, inner_forward, twiddle_forward, s, n) for s in range(seqs)
+    ]
+    step = n // 2
+    spread = []
+    waits = [weights]
+    for p in parts:
+        last = exchange(after(p, *waits))
+        spread.append(last.reshape(outer, -1, ch))
+        if step > 1:
+            step //= 2
+            weights = more_hidden(weights, n, step)
+        waits = [last, weights]
+    out = None
+    for s in range(seqs):
+        groups = RETURN_ROWS[min(s, 1)]
+        back = outer_section(
+            spread[s], outer_forward, outer_inverse, twiddle_inverse, freq_kernel, groups, n
+        )
+        first = 0
+        for part, count in zip(back, groups):
+            part = exchange(after(part, *waits))
+            waits = [part] if out is None else [part, out]
+            if out is not None:
+                part = after(part, out)
+            while step > 1:
+                step //= 2
+                weights = more_hidden(weights, n, step)
+                waits.append(weights)
+            for skip in range(0, count, GATE_ROWS):
+                size = min(GATE_ROWS, count - skip)
+                gated, sq = gate_rows(
+                    blocked, inner_inverse, gain, bias, part, s, first, skip, size
+                )
+                total = sq
+                for r in range(1, n_ch):
+                    total = total + lax.ppermute(
+                        sq, "ch", [(j, (j + r) % n_ch) for j in range(n_ch)]
+                    )
+                for done in range(0, size, MLP_ROWS):
+                    out = mlp_rows(
+                        gated,
+                        total,
+                        norm,
+                        weights,
+                        out,
+                        done,
+                        min(MLP_ROWS, size - done),
+                        s * a_dev + first + skip + done,
+                        seqs * a_dev,
+                        ch * n_ch,
+                    )
+            first += count
+    return out.reshape(seqs, tok_dev, ch)
+
+
+def local_rows(
     tokens,
     inner_forward,
     outer_forward,
@@ -53,7 +332,7 @@
     rows_dev = full_rows.shape[1]
     width = full_rows.shape[2]
     rows_f = full_rows.astype(jnp.float32)
-    scale = lax.rsqrt(jnp.mean(rows_f * rows_f, axis=-1, keepdims=True) + 1e-06)
+    scale = lax.rsqrt(jnp.mean(rows_f * rows_f, axis=-1, keepdims=True) + EPS)
     normed = (rows_f * scale * norm_gain).astype(jnp.bfloat16)
     normed_b = normed.reshape(seq_total * rows_dev, block_count, width_block)
     lifted = jnp.einsum(
@@ -73,6 +352,14 @@
     return lax.all_to_all(result_rows, "ch", split_axis=2, concat_axis=1, tiled=True)
 
 
+def local(*args):
+    tokens, up_weight = args[0], args[11]
+    n = lax.axis_size("seq")
+    if tokens.shape[2] % up_weight.shape[2] == 0 and n & (n - 1) == 0:
+        return local_blocks(*args)
+    return local_rows(*args)
+
+
 def solution(mesh):
     in_specs = (
         P(None, "seq", "ch"),

time: 1770 us -> 796 us (0.45)
  local copies, waits for them, and re-layouts: 426 us -> 6.7 us
  waiting for transfers between devices: 917 us -> 587 us
  blocking collectives: 187 us -> 0 us
  Pallas kernels: 0 us -> 156 us
  matrix products: 129 us -> 0 us
  other arithmetic: 61 us -> 7.67 us
    all_to_all x3 -> x5, waiting for transfers between devices: 916 us -> 366 us  [exchange(): return lax.all_to_all(x, 'seq', split_axis=0, concat_axis=0, tiled=True)]
    ppermute x0 -> x9, waiting for transfers between devices: none -> 222 us  [the longest x4 216 us: more_hidden(): other = lax.ppermute(weights, 'seq', [(j, j ^ step) for j in range(n)])]
    convert_element_type x7 -> x0, local copies, waits for them, and re-layouts: 215 us -> none  [the longest x3 126 us: local(): rows_f = full_rows.astype(jnp.float32)]
    all_to_all x1 -> x0, blocking collectives: 187 us -> none  [local(): lax.all_to_all(result_rows, 'ch', split_axis=2, concat_axis=1, tiled=True)]
    pallas_call x0 -> x14, Pallas kernels: none -> 156 us  [the longest x5 64.5 us: mlp_rows(): pl.pallas_call(functools.partial(mlp_kernel, width), grid=(count,), in_sp...]
    dot_general x4 -> x0, matrix products: 129 us -> none  [the longest x1 52.3 us: local(): jnp.einsum('rbj,bji->rbi', hidden, lax.all_gather(down_weight, 'seq', axi...]
    reshape x3 -> x1, local copies, waits for them, and re-layouts: 104 us -> 0.74 us  [outer_section(): tw = tw.reshape(outer, k_dev // rows, rows).swapaxes(0, 1)]
    all_to_all x4 -> x0, local copies, waits for them, and re-layouts: 66.7 us -> none  [the longest x2 39.9 us: local(): lax.all_to_all(result_rows, 'ch', split_axis=2, concat_axis=1, tiled=True)]
  transfers between devices with their start and end apart: 5 -> 14, of which waited for: 3 -> 11; matrix products, arithmetic and copies ran while one was open for 13% -> 1% of each run, Pallas kernels for 0% -> 18%
where the time goes in v2:
time: 796 us; the launch traced here: 795 us
  waiting for transfers between devices  587 us (74%)
  Pallas kernels  156 us (20%)
  starting transfers between devices  36.7 us (5%)
    all_to_all x5, waiting for transfers between devices, exchange(): return lax.all_to_all(x, 'seq', split_axis=0, concat_axis=0, tiled=True)  366 us
    ppermute x4, waiting for transfers between devices, more_hidden(): other = lax.ppermute(weights, 'seq', [(j, j ^ step) for j in range(n)])  216 us
    pallas_call x5, Pallas kernels, mlp_rows(): pl.pallas_call(functools.partial(mlp_kernel, width), grid=(count,), in_sp...  64.5 us
    pallas_call x2, Pallas kernels, outer_section(): pl.pallas_call(functools.partial(outer_kernel, groups), grid=(k_dev // ro...  36.6 us
    pallas_call x5, Pallas kernels, gate_rows(): pl.pallas_call(gate_kernel, grid=(count,), in_specs=[pl.BlockSpec((1, 1,...  33.2 us
    all_to_all x5, starting transfers between devices, exchange(): return lax.all_to_all(x, 'seq', split_axis=0, concat_axis=0, tiled=True)  28 us
    pallas_call x2, Pallas kernels, first_section(): pl.pallas_call(first_kernel, grid=(a_dev,), in_specs=[pl.BlockSpec((1, 1,...  22 us
  transfers between devices with their start and end apart: 14, of which 11 were waited for; matrix products, arithmetic and copies ran while one was open for 1% of the time, Pallas kernels for 18%

profile of v2, /device:TPU:16, one launch (start us, length us, event | category | flops | bytes accessed | tf_op | source)
XLA Modules:
  0.0 794.8 jit_solution(14739060135515491043)
XLA Ops:
  0.0 1.7 constant_dynamic-update-slice_fusion.4
  1.7 11.0 %first_section.3 = bf16[16,8,32,1024]{3,2,1,0:T(8,128)(2,1)} custom-call(bf16[2,8,512,1024]{3,2,1,0:T(8,128)(2,1)} %bitcast.11, bf16[512,512]{1,0:T(8,128)(2,1)} %w_ref.8, f32[8,512]{1,0:T(8,128)} %tw_ref.3), custom_call_target="tpu_custom_call" | custom-call | tf_op jit(solution)/shard_map/first_section/pallas_call | solution.py:34
  13.2 9.2 %all-to-all-start = ((bf16[16,8,32,1024]{3,2,1,0:T(8,128)(2,1)}), bf16[16,8,32,1024]{3,2,1,0:T(8,128)(2,1)}, u32[]{:S(2)}, u32[]{:S(2)}) async-start(bf16[16,8,32,1024]{3,2,1,0:T(8,128)(2,1)} %first_section.3), calls=%async_computation | async-start | bytes 16777216 | tf_op jit(solution)/shard_map/all_to_all | solution.py:190
  22.4 1.5 collective-permute-start.1
  23.8 11.0 %first_section.2 = bf16[16,8,32,1024]{3,2,1,0:T(8,128)(2,1)} custom-call(bf16[2,8,512,1024]{3,2,1,0:T(8,128)(2,1)} %bitcast.12, bf16[512,512]{1,0:T(8,128)(2,1)} %w_ref.8, f32[8,512]{1,0:T(8,128)} %tw_ref.3), custom_call_target="tpu_custom_call" | custom-call | tf_op jit(solution)/shard_map/first_section/pallas_call | solution.py:34
  34.8 136.5 %collective-permute-done.1 = bf16[2,2,128,512]{3,2,1,0:T(8,128)(2,1)S(1)} collective-permute-done((bf16[2,2,128,512]{3,2,1,0:T(8,128)(2,1)S(1)}, bf16[2,2,128,512]{3,2,1,0:T(8,128)(2,1)S(1)}, u32[]{:S(2)}, u32[]{:S(2)}) %collective-permute-start.1) | collective-permute-done | bytes 524320 | tf_op jit(solution)/shard_map/ppermute | solution.py:194
  171.4 33.6 %all-to-all-done = bf16[16,8,32,1024]{3,2,1,0:T(8,128)(2,1)} async-done(((bf16[16,8,32,1024]{3,2,1,0:T(8,128)(2,1)}), bf16[16,8,32,1024]{3,2,1,0:T(8,128)(2,1)}, u32[]{:S(2)}, u32[]{:S(2)}) %all-to-all-start) | async-done | bytes 8388640 | tf_op jit(solution)/shard_map/all_to_all | solution.py:190
  204.9 4.7 all-to-all-start.1
  209.6 1.4 collective-permute-start.2
  211.1 0.7 copy.18
  211.8 77.2 %collective-permute-done.2 = bf16[2,2,256,512]{3,2,1,0:T(8,128)(2,1)S(1)} collective-permute-done((bf16[2,2,256,512]{3,2,1,0:T(8,128)(2,1)S(1)}, bf16[2,2,256,512]{3,2,1,0:T(8,128)(2,1)S(1)}, u32[]{:S(2)}, u32[]{:S(2)}) %collective-permute-start.2) | collective-permute-done | bytes 1048608 | tf_op jit(solution)/shard_map/ppermute | solution.py:194
  289.0 1.5 pad_maximum_fusion
  290.5 18.3 %outer_section.3 = bf16[16,8,32,1024]{3,2,1,0:T(8,128)(2,1)} custom-call(bf16[128,128]{1,0:T(8,128)(2,1)} %fwd_ref.3, bf16[128,128]{1,0:T(8,128)(2,1)} %inv_ref.3, f32[2,128,16]{2,1,0:T(8,128)} %bitcast.18, bf16[128,32,1024]{2,1,0:T(8,128)(2,1)} %freq_ref.3, bf16[128,32,1024]{2,1,0:T(8,128)(2,1)} %bitcast.8.spread_ref), custom_call_target="tpu_custom_call" | custom-call | tf_op jit(solution)/shard_map/outer_section/pallas_call | solution.py:75
  308.9 83.3 %all-to-all-done.1 = bf16[16,8,32,1024]{3,2,1,0:T(8,128)(2,1)} async-done(((bf16[16,8,32,1024]{3,2,1,0:T(8,128)(2,1)}), bf16[16,8,32,1024]{3,2,1,0:T(8,128)(2,1)}, u32[]{:S(2)}, u32[]{:S(2)}) %all-to-all-start.1) | async-done | bytes 8388640 | tf_op jit(solution)/shard_map/all_to_all | solution.py:190
  392.2 4.8 all-to-all-start.2
  397.1 0.7 constant_dynamic-update-slice_fusion.3
  397.8 0.8 constant_dynamic-update-slice_fusion.2
  398.7 1.1 constant_dynamic-update-slice_fusion.1
  399.7 2.0 collective-permute-done.3
  401.7 1.4 constant_dynamic-update-slice_fusion.weight_ref
  403.1 18.3 %outer_section.2 = (bf16[16,6,32,1024]{3,2,1,0:T(8,128)(2,1)}, bf16[16,2,32,1024]{3,2,1,0:T(8,128)(2,1)}) custom-call(bf16[128,128]{1,0:T(8,128)(2,1)} %fwd_ref.3, bf16[128,128]{1,0:T(8,128)(2,1)} %inv_ref.3, f32[2,128,16]{2,1,0:T(8,128)} %bitcast.19, bf16[128,32,1024]{2,1,0:T(8,128)(2,1)} %freq_ref.3, bf16[128,32,1024]{2,1,0:T(8,128)(2,1)} %bitcast.7.spread_ref), custom_call_target="tpu_custom_call" | custom-call | tf_op jit(solution)/shard_map/outer_section/pallas_call | solution.py:75
  421.4 158.1 %all-to-all-done.2.part_ref = bf16[16,8,32,1024]{3,2,1,0:T(8,128)(2,1)} async-done(((bf16[16,8,32,1024]{3,2,1,0:T(8,128)(2,1)}), bf16[16,8,32,1024]{3,2,1,0:T(8,128)(2,1)}, u32[]{:S(2)}, u32[]{:S(2)}) %all-to-all-start.2) | async-done | bytes 8388640 | tf_op jit(solution)/shard_map/all_to_all | solution.py:190
  579.5 4.7 all-to-all-start.3
  584.2 7.9 gate_rows.6
  592.1 1.6 collective-permute-start.5
  593.7 7.8 gate_rows.5
  602.0 0.6 dynamic_slice.7
  602.6 0.6 add.24.sq_ref
  603.2 15.2 %mlp_rows.5.rest_0_ = bf16[16,512,1024]{2,1,0:T(8,128)(2,1)} custom-call(bf16[4,512,1024]{2,1,0:T(8,128)(2,1)} %get-tuple-element.32.gated_ref, f32[4,1,512]{2,1,0:T(1,128)} %add.24.sq_ref, f32[1,1024]{1,0:T(1,128)} %bitcast.22, bf16[2,2,1024,512]{3,2,1,0:T(8,128)(2,1)} %constant_dynamic-update-slice_fusion.weight_ref), custom_call_target="tpu_custom_call" | custom-call | tf_op jit(solution)/shard_map/mlp_rows/pallas_call | solution.py:169
  618.5 0.6 add.22.sq_ref
  619.1 15.2 %mlp_rows.6.rest_0_ = bf16[16,512,1024]{2,1,0:T(8,128)(2,1)} custom-call(bf16[4,512,1024]{2,1,0:T(8,128)(2,1)} %get-tuple-element.30.gated_ref, f32[4,1,512]{2,1,0:T(1,128)} %add.22.sq_ref, f32[1,1024]{1,0:T(1,128)} %bitcast.23, bf16[2,2,1024,512]{3,2,1,0:T(8,128)(2,1)} %constant_dynamic-update-slice_fusion.weight_ref, ...), custom_call_target="tpu_custom_call", output_to_operand_aliasing={{}: (4, {})} | custom-call | tf_op jit(solution)/shard_map/mlp_rows/pallas_call | solution.py:169
  634.3 87.5 %all-to-all-done.3.part_ref = bf16[16,6,32,1024]{3,2,1,0:T(8,128)(2,1)} async-done(((bf16[16,6,32,1024]{3,2,1,0:T(8,128)(2,1)}), bf16[16,6,32,1024]{3,2,1,0:T(8,128)(2,1)}, u32[]{:S(2)}, u32[]{:S(2)}) %all-to-all-start.3) | async-done | bytes 6291488 | tf_op jit(solution)/shard_map/all_to_all | solution.py:190
  721.9 4.7 all-to-all-start.4
  726.5 7.8 gate_rows.8
  734.4 1.6 collective-permute-start.7
  736.0 4.8 gate_rows.7
  741.3 3.3 collective-permute-done.6
  744.6 1.3 add.25.sq_ref
  745.9 0.6 add.26.sq_ref
  746.5 15.2 %mlp_rows.7.rest_0_ = bf16[16,512,1024]{2,1,0:T(8,128)(2,1)} custom-call(bf16[4,512,1024]{2,1,0:T(8,128)(2,1)} %get-tuple-element.38.gated_ref, f32[4,1,512]{2,1,0:T(1,128)} %add.26.sq_ref, f32[1,1024]{1,0:T(1,128)} %bitcast.24, bf16[2,2,1024,512]{3,2,1,0:T(8,128)(2,1)} %constant_dynamic-update-slice_fusion.weight_ref, ...), custom_call_target="tpu_custom_call", output_to_operand_aliasing={{}: (4, {})} | custom-call | tf_op jit(solution)/shard_map/mlp_rows/pallas_call | solution.py:169
  761.7 9.4 %mlp_rows.8.rest_0_ = bf16[16,512,1024]{2,1,0:T(8,128)(2,1)} custom-call(bf16[2,512,1024]{2,1,0:T(8,128)(2,1)} %get-tuple-element.36.gated_ref, f32[2,1,512]{2,1,0:T(1,128)} %add.25.sq_ref, f32[1,1024]{1,0:T(1,128)} %bitcast.25, bf16[2,2,1024,512]{3,2,1,0:T(8,128)(2,1)} %constant_dynamic-update-slice_fusion.weight_ref, ...), custom_call_target="tpu_custom_call", output_to_operand_aliasing={{}: (4, {})} | custom-call | tf_op jit(solution)/shard_map/mlp_rows/pallas_call | solution.py:169
  771.1 3.1 all-to-all-done.4.part_ref
  774.2 1.3 copy-done
  775.5 4.8 gate_rows.9
  780.3 1.5 collective-permute-start.8
  781.8 2.3 collective-permute-done.8
  784.1 1.3 add.27.sq_ref
  785.4 9.4 %mlp_rows.9 = bf16[16,512,1024]{2,1,0:T(8,128)(2,1)} custom-call(bf16[2,512,1024]{2,1,0:T(8,128)(2,1)} %get-tuple-element.41.gated_ref, f32[2,1,512]{2,1,0:T(1,128)} %add.27.sq_ref, f32[1,1024]{1,0:T(1,128)} %bitcast.26, bf16[2,2,1024,512]{3,2,1,0:T(8,128)(2,1)} %constant_dynamic-update-slice_fusion.weight_ref, ...), custom_call_target="tpu_custom_call", output_to_operand_aliasing={{}: (4, {})} | custom-call | tf_op jit(solution)/shard_map/mlp_rows/pallas_call | solution.py:169
  (21 shorter events, 1.7 us)
Async XLA Ops:
  1.7 11.5 %collective-permute-start = (bf16[2,2,64,512]{3,2,1,0:T(8,128)(2,1)S(1)}, bf16[2,2,64,512]{3,2,1,0:T(8,128)(2,1)S(1)}, u32[]{:S(2)}, u32[]{:S(2)}) collective-permute-start(bf16[2,2,64,512]{3,2,1,0:T(8,128)(2,1)S(1)} %get-tuple-element.44), channel_id=1, source_target_pairs={{0,16},{2,18},{4,20},{6,22},{8,24},{10,26},{12,28},{14,30},{16,0},... | collective-permute-start | bytes 786440 | tf_op jit(solution)/shard_map/ppermute | solution.py:194
  13.2 191.7 %all-to-all-start = ((bf16[16,8,32,1024]{3,2,1,0:T(8,128)(2,1)}), bf16[16,8,32,1024]{3,2,1,0:T(8,128)(2,1)}, u32[]{:S(2)}, u32[]{:S(2)}) async-start(bf16[16,8,32,1024]{3,2,1,0:T(8,128)(2,1)} %first_section.3), calls=%async_computation | async-start | bytes 16777216 | tf_op jit(solution)/shard_map/all_to_all | solution.py:190
  22.4 148.9 %collective-permute-start.1 = (bf16[2,2,128,512]{3,2,1,0:T(8,128)(2,1)S(1)}, bf16[2,2,128,512]{3,2,1,0:T(8,128)(2,1)S(1)}, u32[]{:S(2)}, u32[]{:S(2)}) collective-permute-start(bf16[2,2,128,512]{3,2,1,0:T(8,128)(2,1)S(1)} %pad_maximum_fusion.2), channel_id=1, source_target_pairs={{0,8},{2,10},{4,12},{6,14},{8,0},{10,2},{12,4},{14,6},{16,24},{18,... | collective-permute-start | bytes 1572872 | tf_op jit(solution)/shard_map/ppermute | solution.py:194
  171.3 39.7 %copy-start.1 = (f32[128,32]{0,1:T(8,128)S(1)}, f32[128,32]{0,1:T(8,128)}, u32[]{:S(2)}) copy-start(f32[128,32]{0,1:T(8,128)} %param.20) | copy-start | bytes 49156
  204.9 187.3 %all-to-all-start.1 = ((bf16[16,8,32,1024]{3,2,1,0:T(8,128)(2,1)}), bf16[16,8,32,1024]{3,2,1,0:T(8,128)(2,1)}, u32[]{:S(2)}, u32[]{:S(2)}) async-start(bf16[16,8,32,1024]{3,2,1,0:T(8,128)(2,1)} %first_section.2), calls=%async_computation.1 | async-start | bytes 16777216 | tf_op jit(solution)/shard_map/all_to_all | solution.py:190
  209.6 79.4 %collective-permute-start.2 = (bf16[2,2,256,512]{3,2,1,0:T(8,128)(2,1)S(1)}, bf16[2,2,256,512]{3,2,1,0:T(8,128)(2,1)S(1)}, u32[]{:S(2)}, u32[]{:S(2)}) collective-permute-start(bf16[2,2,256,512]{3,2,1,0:T(8,128)(2,1)S(1)} %pad_maximum_fusion.1), channel_id=1, source_target_pairs={{0,4},{2,6},{4,0},{6,2},{8,12},{10,14},{12,8},{14,10},{16,20},{18,... | collective-permute-start | bytes 3145736 | tf_op jit(solution)/shard_map/ppermute | solution.py:194
  392.2 187.3 %all-to-all-start.2 = ((bf16[16,8,32,1024]{3,2,1,0:T(8,128)(2,1)}), bf16[16,8,32,1024]{3,2,1,0:T(8,128)(2,1)}, u32[]{:S(2)}, u32[]{:S(2)}) async-start(bf16[16,8,32,1024]{3,2,1,0:T(8,128)(2,1)} %outer_section.3), calls=%async_computation.2 | async-start | bytes 16777216 | tf_op jit(solution)/shard_map/all_to_all | solution.py:190
  397.0 4.8 collective-permute-start.3
  579.5 142.3 %all-to-all-start.3 = ((bf16[16,6,32,1024]{3,2,1,0:T(8,128)(2,1)}), bf16[16,6,32,1024]{3,2,1,0:T(8,128)(2,1)}, u32[]{:S(2)}, u32[]{:S(2)}) async-start(bf16[16,6,32,1024]{3,2,1,0:T(8,128)(2,1)} %get-tuple-element.29), calls=%async_computation.3 | async-start | bytes 12582912 | tf_op jit(solution)/shard_map/all_to_all | solution.py:190
  592.1 9.9 %copy-start.5 = (f32[2048]{0:T(1024)S(1)}, f32[2048]{0:T(1024)}, u32[]{:S(2)}) copy-start(f32[2048]{0:T(1024)} %param.23) | copy-start | bytes 24580
  592.1 10.5 %copy-start.3 = (f32[4,1,512]{2,1,0:T(1,128)S(1)}, f32[4,1,512]{2,1,0:T(1,128)}, u32[]{:S(2)}) copy-start(f32[4,1,512]{2,1,0:T(1,128)} %get-tuple-element.33) | copy-start | bytes 24580
  592.1 10.5 %collective-permute-start.5 = (f32[4,1,512]{2,1,0:T(1,128)}, f32[4,1,512]{2,1,0:T(1,128)S(1)}, u32[]{:S(2)}, u32[]{:S(2)}) collective-permute-start(f32[4,1,512]{2,1,0:T(1,128)} %get-tuple-element.33), channel_id=1, source_target_pairs={{0,1},{1,0},{2,3},{3,2},{4,5},{5,4},{6,7},{7,6},{8,9},{9,8},{10,11... | collective-permute-start | bytes 24584 | tf_op jit(solution)/shard_map/ppermute | solution.py:266
  601.5 16.9 %collective-permute-start.4 = (f32[4,1,512]{2,1,0:T(1,128)}, f32[4,1,512]{2,1,0:T(1,128)S(1)}, u32[]{:S(2)}, u32[]{:S(2)}) collective-permute-start(f32[4,1,512]{2,1,0:T(1,128)} %get-tuple-element.31), channel_id=1, source_target_pairs={{0,1},{1,0},{2,3},{3,2},{4,5},{5,4},{6,7},{7,6},{8,9},{9,8},{10,11... | collective-permute-start | bytes 24584 | tf_op jit(solution)/shard_map/ppermute | solution.py:266
  603.2 15.2 %copy-start.2 = (f32[4,1,512]{2,1,0:T(1,128)S(1)}, f32[4,1,512]{2,1,0:T(1,128)}, u32[]{:S(2)}) copy-start(f32[4,1,512]{2,1,0:T(1,128)} %get-tuple-element.31) | copy-start | bytes 24580
  721.9 52.3 %all-to-all-start.4 = ((bf16[16,2,32,1024]{3,2,1,0:T(8,128)(2,1)}), bf16[16,2,32,1024]{3,2,1,0:T(8,128)(2,1)S(1)}, u32[]{:S(2)}, u32[]{:S(2)}) async-start(bf16[16,2,32,1024]{3,2,1,0:T(8,128)(2,1)} %get-tuple-element.34), calls=%async_computation.4 | async-start | bytes 4194304 | tf_op jit(solution)/shard_map/all_to_all | solution.py:190
  734.4 11.5 %copy-start.4 = (f32[4,1,512]{2,1,0:T(1,128)S(1)}, f32[4,1,512]{2,1,0:T(1,128)}, u32[]{:S(2)}) copy-start(f32[4,1,512]{2,1,0:T(1,128)} %get-tuple-element.39) | copy-start | bytes 24580
  734.4 11.5 %collective-permute-start.7 = (f32[4,1,512]{2,1,0:T(1,128)}, f32[4,1,512]{2,1,0:T(1,128)S(1)}, u32[]{:S(2)}, u32[]{:S(2)}) collective-permute-start(f32[4,1,512]{2,1,0:T(1,128)} %get-tuple-element.39), channel_id=1, source_target_pairs={{0,1},{1,0},{2,3},{3,2},{4,5},{5,4},{6,7},{7,6},{8,9},{9,8},{10,11... | collective-permute-start | bytes 24584 | tf_op jit(solution)/shard_map/ppermute | solution.py:266
  740.8 3.8 collective-permute-start.6
  774.2 1.3 copy-start
  780.3 3.8 collective-permute-start.8

commit v3 on v2

--- a/solution.py
+++ b/solution.py
@@ -7,11 +7,10 @@
 from jax.experimental.pallas import tpu as pltpu
 from jax.sharding import PartitionSpec as P
 
-VMEM_BYTES = 56 * 1024 * 1024
+VMEM_BYTES = 32 * 1024 * 1024
 EPS = 1e-06
 RETURN_ROWS = ((8,), (6, 2))
-GATE_ROWS = 4
-MLP_ROWS = 4
+STEP_ROWS = 2
 
 
 def params():
@@ -19,27 +18,29 @@
 
 
 def first_kernel(tok_ref, w_ref, tw_ref, out_ref):
-    a = pl.program_id(0)
-    res = jnp.dot(w_ref[...], tok_ref[0, 0], preferred_element_type=jnp.float32)
+    n, step, rows, ch = out_ref.shape
     cols = tw_ref[...].T
     lane = lax.broadcasted_iota(jnp.int32, cols.shape, 1)
-    tw = jnp.sum(jnp.where(lane == a, cols, 0.0), axis=1, keepdims=True)
-    n, _, rows, ch = out_ref.shape
-    out_ref[...] = (res * tw).astype(jnp.bfloat16).reshape(n, 1, rows, ch)
+    for j in range(step):
+        a = pl.program_id(0) * step + j
+        res = jnp.dot(w_ref[...], tok_ref[0, j], preferred_element_type=jnp.float32)
+        tw = jnp.sum(jnp.where(lane == a, cols, 0.0), axis=1, keepdims=True)
+        out_ref[:, j] = (res * tw).astype(jnp.bfloat16).reshape(n, rows, ch)
 
 
 def first_section(blocked, inner_forward, twiddle, s, n):
     _, a_dev, inner, ch = blocked.shape
     rows = inner // n
+    step = STEP_ROWS if a_dev % STEP_ROWS == 0 else 1
     return pl.pallas_call(
         first_kernel,
-        grid=(a_dev,),
+        grid=(a_dev // step,),
         in_specs=[
-            pl.BlockSpec((1, 1, inner, ch), lambda a: (s, a, 0, 0)),
+            pl.BlockSpec((1, step, inner, ch), lambda a: (s, a, 0, 0)),
             pl.BlockSpec((inner, inner), lambda a: (0, 0)),
             pl.BlockSpec((a_dev, inner), lambda a: (0, 0)),
         ],
-        out_specs=pl.BlockSpec((n, 1, rows, ch), lambda a: (0, a, 0, 0)),
+        out_specs=pl.BlockSpec((n, step, rows, ch), lambda a: (0, a, 0, 0)),
         out_shape=jax.ShapeDtypeStruct((n, a_dev, rows, ch), jnp.bfloat16),
         compiler_params=params(),
         name="first_section",
@@ -109,18 +110,18 @@
     sq_ref[0] = jnp.sum(part.T, axis=0, keepdims=True)
 
 
-def gate_rows(blocked, inner_inverse, gain, bias, parts, s, first, skip, count):
+def gate_rows(blocked, inner_inverse, gain, bias, parts, s, first):
     _, _, inner, ch = blocked.shape
-    n, _, rows, _ = parts.shape
+    n, count, rows, _ = parts.shape
     return pl.pallas_call(
         gate_kernel,
         grid=(count,),
         in_specs=[
-            pl.BlockSpec((1, 1, inner, ch), lambda j: (s, first + skip + j, 0, 0)),
+            pl.BlockSpec((1, 1, inner, ch), lambda j: (s, first + j, 0, 0)),
             pl.BlockSpec((inner, inner), lambda j: (0, 0)),
             pl.BlockSpec((1, ch), lambda j: (0, 0)),
             pl.BlockSpec((1, ch), lambda j: (0, 0)),
-            pl.BlockSpec((n, 1, rows, ch), lambda j: (0, skip + j, 0, 0)),
+            pl.BlockSpec((n, 1, rows, ch), lambda j: (0, j, 0, 0)),
         ],
         out_specs=[
             pl.BlockSpec((1, inner, ch), lambda j: (j, 0, 0)),
@@ -135,10 +136,13 @@
     )(blocked, inner_inverse, gain, bias, parts)
 
 
-def mlp_kernel(width, gated_ref, sq_ref, gain_ref, weight_ref, *rest):
+def mlp_kernel(width, n_sq, gated_ref, gain_ref, weight_ref, *rest):
     out_ref = rest[-1]
     _, blocks, _, wb = weight_ref.shape
-    scale = lax.rsqrt(sq_ref[0] * (1.0 / width) + EPS)
+    total = rest[0][0]
+    for sq_ref in rest[1:n_sq]:
+        total = total + sq_ref[0]
+    scale = lax.rsqrt(total * (1.0 / width) + EPS)
     scale = jnp.broadcast_to(scale, (128, scale.shape[1])).T[:, :1]
     for b in range(blocks):
         cols = slice(b * wb, (b + 1) * wb)
@@ -152,22 +156,21 @@
         out_ref[0, :, cols] = (g + lowered).astype(jnp.bfloat16)
 
 
-def mlp_rows(gated, sq, gain, weights, out, skip, count, first, total, width):
-    _, inner, ch = gated.shape
+def mlp_rows(gated, sqs, gain, weights, out, first, total, width):
+    count, inner, ch = gated.shape
     specs = [
-        pl.BlockSpec((1, inner, ch), lambda j: (skip + j, 0, 0)),
-        pl.BlockSpec((1, 1, inner), lambda j: (skip + j, 0, 0)),
+        pl.BlockSpec((1, inner, ch), lambda j: (j, 0, 0)),
         pl.BlockSpec((1, ch), lambda j: (0, 0)),
-        pl.BlockSpec(weights.shape, lambda j: (0, 0, 0, 0), pipeline_mode=pl.Buffered(1)),
-    ]
-    args = [gated, sq, gain, weights]
+        pl.BlockSpec(memory_space=pltpu.VMEM),
+    ] + [pl.BlockSpec((1, 1, inner), lambda j: (j, 0, 0))] * len(sqs)
+    args = [gated, gain, weights, *sqs]
     aliases = {}
     if out is not None:
+        aliases = {len(args): 0}
         specs.append(pl.BlockSpec(memory_space=pl.ANY))
         args.append(out)
-        aliases = {4: 0}
     return pl.pallas_call(
-        functools.partial(mlp_kernel, width),
+        functools.partial(mlp_kernel, width, len(sqs)),
         grid=(count,),
         in_specs=specs,
         out_specs=pl.BlockSpec((1, inner, ch), lambda j: (first + j, 0, 0)),
@@ -256,29 +259,14 @@
                 step //= 2
                 weights = more_hidden(weights, n, step)
                 waits.append(weights)
-            for skip in range(0, count, GATE_ROWS):
-                size = min(GATE_ROWS, count - skip)
-                gated, sq = gate_rows(
-                    blocked, inner_inverse, gain, bias, part, s, first, skip, size
-                )
-                total = sq
-                for r in range(1, n_ch):
-                    total = total + lax.ppermute(
-                        sq, "ch", [(j, (j + r) % n_ch) for j in range(n_ch)]
-                    )
-                for done in range(0, size, MLP_ROWS):
-                    out = mlp_rows(
-                        gated,
-                        total,
-                        norm,
-                        weights,
-                        out,
-                        done,
-                        min(MLP_ROWS, size - done),
-                        s * a_dev + first + skip + done,
-                        seqs * a_dev,
-                        ch * n_ch,
-                    )
+            gated, sq = gate_rows(blocked, inner_inverse, gain, bias, part, s, first)
+            sqs = [sq] + [
+                lax.ppermute(sq, "ch", [(j, (j + r) % n_ch) for j in range(n_ch)])
+                for r in range(1, n_ch)
+            ]
+            out = mlp_rows(
+                gated, sqs, norm, weights, out, s * a_dev + first, seqs * a_dev, ch * n_ch
+            )
             first += count
     return out.reshape(seqs, tok_dev, ch)
 

time: 796 us -> 794 us (level)
  local copies, waits for them, and re-layouts: 6.7 us -> 41.5 us
  Pallas kernels: 156 us -> 126 us
    unnamed x15 -> x51, local copies, waits for them, and re-layouts: 3.95 us -> 39.9 us
    pallas_call x7 -> x5, Pallas kernels: 86.5 us -> 64.8 us  [the longest x3 49.9 us: mlp_rows(): pl.pallas_call(functools.partial(mlp_kernel, width, len(sqs)), grid=(coun...]
    pallas_call x5 -> x3, Pallas kernels: 33.2 us -> 24.2 us  [gate_rows(): pl.pallas_call(gate_kernel, grid=(count,), in_specs=[pl.BlockSpec((1, 1,...]
  transfers between devices with their start and end apart: 14 -> 12, of which waited for: 11 -> 11; matrix products, arithmetic and copies ran while one was open for 1% -> 1% of each run, Pallas kernels for 18% -> 15%
where the time goes in v3:
time: 794 us; the launch traced here: 793 us
  waiting for transfers between devices  586 us (74%)
  Pallas kernels  126 us (16%)
  local copies, waits for them, and re-layouts  41.5 us (5%)
  starting transfers between devices  35.1 us (4%)
    all_to_all x5, waiting for transfers between devices, exchange(): return lax.all_to_all(x, 'seq', split_axis=0, concat_axis=0, tiled=True)  363 us
    ppermute x4, waiting for transfers between devices, more_hidden(): other = lax.ppermute(weights, 'seq', [(j, j ^ step) for j in range(n)])  216 us
    pallas_call x3, Pallas kernels, mlp_rows(): pl.pallas_call(functools.partial(mlp_kernel, width, len(sqs)), grid=(coun...  49.9 us
    unnamed x51, local copies, waits for them, and re-layouts  39.9 us
    pallas_call x2, Pallas kernels, outer_section(): pl.pallas_call(functools.partial(outer_kernel, groups), grid=(k_dev // ro...  37.4 us
    all_to_all x5, starting transfers between devices, exchange(): return lax.all_to_all(x, 'seq', split_axis=0, concat_axis=0, tiled=True)  27.2 us
    pallas_call x3, Pallas kernels, gate_rows(): pl.pallas_call(gate_kernel, grid=(count,), in_specs=[pl.BlockSpec((1, 1,...  24.2 us
  transfers between devices with their start and end apart: 12, of which 11 were waited for; matrix products, arithmetic and copies ran while one was open for 1% of the time, Pallas kernels for 15%

profile of v3, /device:TPU:16, one launch (start us, length us, event | category | flops | bytes accessed | tf_op | source)
XLA Modules:
  0.0 793.3 jit_solution(13630249410613570338)
XLA Ops:
  0.0 1.7 constant_dynamic-update-slice_fusion.4
  1.7 1.0 copy-done.13
  3.5 7.4 first_section.3
  10.9 3.3 copy-done.8
  14.3 8.3 %all-to-all-start = ((bf16[16,8,32,1024]{3,2,1,0:T(8,128)(2,1)}), bf16[16,8,32,1024]{3,2,1,0:T(8,128)(2,1)}, u32[]{:S(2)}, u32[]{:S(2)}) async-start(bf16[16,8,32,1024]{3,2,1,0:T(8,128)(2,1)} %copy-done.8), calls=%async_computation | async-start | bytes 16777216 | tf_op jit(solution)/shard_map/all_to_all | solution.py:193
  22.5 1.5 collective-permute-start.1
  24.0 7.4 first_section.2
  31.4 3.4 copy-done.7
  34.8 136.6 %collective-permute-done.1 = bf16[2,2,128,512]{3,2,1,0:T(8,128)(2,1)S(1)} collective-permute-done((bf16[2,2,128,512]{3,2,1,0:T(8,128)(2,1)S(1)}, bf16[2,2,128,512]{3,2,1,0:T(8,128)(2,1)S(1)}, u32[]{:S(2)}, u32[]{:S(2)}) %collective-permute-start.1) | collective-permute-done | bytes 524320 | tf_op jit(solution)/shard_map/ppermute | solution.py:197
  171.4 1.1 pad_maximum_fusion.1
  172.5 32.6 %all-to-all-done = bf16[16,8,32,1024]{3,2,1,0:T(8,128)(2,1)} async-done(((bf16[16,8,32,1024]{3,2,1,0:T(8,128)(2,1)}), bf16[16,8,32,1024]{3,2,1,0:T(8,128)(2,1)}, u32[]{:S(2)}, u32[]{:S(2)}) %all-to-all-start) | async-done | bytes 8388640 | tf_op jit(solution)/shard_map/all_to_all | solution.py:193
  205.1 4.7 all-to-all-start.1
  209.8 1.5 collective-permute-start.2
  211.4 77.8 %collective-permute-done.2 = bf16[2,2,256,512]{3,2,1,0:T(8,128)(2,1)S(1)} collective-permute-done((bf16[2,2,256,512]{3,2,1,0:T(8,128)(2,1)}, bf16[2,2,256,512]{3,2,1,0:T(8,128)(2,1)S(1)}, u32[]{:S(2)}, u32[]{:S(2)}) %collective-permute-start.2) | collective-permute-done | bytes 1048608 | tf_op jit(solution)/shard_map/ppermute | solution.py:197
  289.3 1.4 pad_maximum_fusion
  290.7 3.4 copy-done.4
  294.1 18.7 %outer_section.3 = bf16[16,8,32,1024]{3,2,1,0:T(8,128)(2,1)S(1)} custom-call(bf16[128,128]{1,0:T(8,128)(2,1)S(1)} %copy-done.16, bf16[128,128]{1,0:T(8,128)(2,1)S(1)} %copy-done.17, f32[2,128,16]{2,1,0:T(8,128)S(1)} %bitcast.16, bf16[128,32,1024]{2,1,0:T(8,128)(2,1)S(1)} %copy-done.4, bf16[128,32,1024]{2,1,0:T(8,128)(2,1)} %bitcast.8.spread_ref), custom_call_target="tpu_custom_call" | custom-call | tf_op jit(solution)/shard_map/outer_section/pallas_call | solution.py:76
  312.9 3.3 copy-done.6
  316.1 76.2 %all-to-all-done.1 = bf16[16,8,32,1024]{3,2,1,0:T(8,128)(2,1)} async-done(((bf16[16,8,32,1024]{3,2,1,0:T(8,128)(2,1)}), bf16[16,8,32,1024]{3,2,1,0:T(8,128)(2,1)}, u32[]{:S(2)}, u32[]{:S(2)}) %all-to-all-start.1) | async-done | bytes 8388640 | tf_op jit(solution)/shard_map/all_to_all | solution.py:193
  392.4 4.8 all-to-all-start.2
  398.9 1.0 constant_dynamic-update-slice_fusion.1
  399.9 2.0 collective-permute-done.3
  401.9 1.5 constant_dynamic-update-slice_fusion.weight_ref
  403.4 3.4 copy-done.5
  406.8 18.7 %outer_section.2 = (bf16[16,6,32,1024]{3,2,1,0:T(8,128)(2,1)S(1)}, bf16[16,2,32,1024]{3,2,1,0:T(8,128)(2,1)S(1)}) custom-call(bf16[128,128]{1,0:T(8,128)(2,1)S(1)} %copy-done.16, bf16[128,128]{1,0:T(8,128)(2,1)S(1)} %copy-done.17, f32[2,128,16]{2,1,0:T(8,128)S(1)} %bitcast.17, bf16[128,32,1024]{2,1,0:T(8,128)(2,1)S(1)} %copy-done.5, ...), custom_call_target="tpu_custom_call" | custom-call | tf_op jit(solution)/shard_map/outer_section/pallas_call | solution.py:76
  425.5 2.7 copy-done.11
  428.2 1.4 copy-done.15
  429.6 150.1 %all-to-all-done.2.part_ref = bf16[16,8,32,1024]{3,2,1,0:T(8,128)(2,1)} async-done(((bf16[16,8,32,1024]{3,2,1,0:T(8,128)(2,1)}), bf16[16,8,32,1024]{3,2,1,0:T(8,128)(2,1)}, u32[]{:S(2)}, u32[]{:S(2)}) %all-to-all-start.2) | async-done | bytes 8388640 | tf_op jit(solution)/shard_map/all_to_all | solution.py:193
  579.7 4.8 all-to-all-start.3
  584.6 12.2 %gate_rows.3 = (bf16[8,512,1024]{2,1,0:T(8,128)(2,1)S(1)}, f32[8,1,512]{2,1,0:T(1,128)S(1)}) custom-call(bf16[2,8,512,1024]{3,2,1,0:T(8,128)(2,1)} %bitcast.13, bf16[512,512]{1,0:T(8,128)(2,1)S(1)} %copy-done.12, f32[1,1024]{1,0:T(1,128)S(1)} %bitcast.21, f32[1,1024]{1,0:T(1,128)S(1)} %bitcast.24, bf16[16,8,32,1024]{3,2,1,0:T(8,128)(2,1)} %all-to-all-done.2.part_ref), custom_call_target="tpu_custom_call" | custom-call | tf_op jit(solution)/shard_map/gate_rows/pallas_call | solution.py:116
  596.8 3.4 copy-done.9
  600.2 1.5 collective-permute-start.4
  601.7 2.2 collective-permute-done.4.rest_1_
  603.9 2.2 copy-done.1
  606.1 3.4 copy-done.10
  609.5 24.4 %mlp_rows.3.rest_2_ = bf16[16,512,1024]{2,1,0:T(8,128)(2,1)} custom-call(bf16[8,512,1024]{2,1,0:T(8,128)(2,1)S(1)} %copy-done.10, f32[1,1024]{1,0:T(1,128)S(1)} %bitcast.18, bf16[2,2,1024,512]{3,2,1,0:T(8,128)(2,1)S(1)} %copy-done.1, f32[8,1,512]{2,1,0:T(1,128)S(1)} %get-tuple-element.27.rest_0_, f32[8,1,512]{2,1,0:T(1,128)S(1)} %collective-permute-done.4.rest_1_), custom_call_target="tpu_custom_call" | custom-call | tf_op jit(solution)/shard_map/mlp_rows/pallas_call | solution.py:172
  633.9 88.3 %all-to-all-done.3.part_ref = bf16[16,6,32,1024]{3,2,1,0:T(8,128)(2,1)} async-done(((bf16[16,6,32,1024]{3,2,1,0:T(8,128)(2,1)}), bf16[16,6,32,1024]{3,2,1,0:T(8,128)(2,1)}, u32[]{:S(2)}, u32[]{:S(2)}) %all-to-all-start.3) | async-done | bytes 6291488 | tf_op jit(solution)/shard_map/all_to_all | solution.py:193
  722.2 4.7 all-to-all-start.4
  726.9 9.6 %gate_rows.4 = (bf16[6,512,1024]{2,1,0:T(8,128)(2,1)S(1)}, f32[6,1,512]{2,1,0:T(1,128)S(1)}) custom-call(bf16[2,8,512,1024]{3,2,1,0:T(8,128)(2,1)} %bitcast.14, bf16[512,512]{1,0:T(8,128)(2,1)S(1)} %copy-done.12, f32[1,1024]{1,0:T(1,128)S(1)} %bitcast.22, f32[1,1024]{1,0:T(1,128)S(1)} %bitcast.25, bf16[16,6,32,1024]{3,2,1,0:T(8,128)(2,1)} %all-to-all-done.3.part_ref), custom_call_target="tpu_custom_call" | custom-call | tf_op jit(solution)/shard_map/gate_rows/pallas_call | solution.py:116
  736.4 1.6 collective-permute-start.5
  738.0 2.2 collective-permute-done.5.rest_1_
  740.2 18.7 %mlp_rows.4.rest_2_ = bf16[16,512,1024]{2,1,0:T(8,128)(2,1)} custom-call(bf16[6,512,1024]{2,1,0:T(8,128)(2,1)S(1)} %get-tuple-element.30.gated_ref, f32[1,1024]{1,0:T(1,128)S(1)} %bitcast.19, bf16[2,2,1024,512]{3,2,1,0:T(8,128)(2,1)S(1)} %copy-done.2, f32[6,1,512]{2,1,0:T(1,128)S(1)} %get-tuple-element.31.rest_0_, ...), custom_call_target="tpu_custom_call", output_to_operand_aliasing={{}: (5, {})} | custom-call | tf_op jit(solution)/shard_map/mlp_rows/pallas_call | solution.py:172
  758.9 15.6 %all-to-all-done.4.part_ref = bf16[16,2,32,1024]{3,2,1,0:T(8,128)(2,1)S(1)} async-done(((bf16[16,2,32,1024]{3,2,1,0:T(8,128)(2,1)}), bf16[16,2,32,1024]{3,2,1,0:T(8,128)(2,1)S(1)}, u32[]{:S(2)}, u32[]{:S(2)}) %all-to-all-start.4) | async-done | bytes 2097184 | tf_op jit(solution)/shard_map/all_to_all | solution.py:193
  774.5 5.8 copy-done
  780.3 2.5 gate_rows.5
  782.7 1.6 collective-permute-start.6
  784.3 2.1 collective-permute-done.6.rest_1_
  786.4 6.9 mlp_rows.5
  (44 shorter events, 2.6 us)
Async XLA Ops:
  1.7 12.5 %collective-permute-start = (bf16[2,2,64,512]{3,2,1,0:T(8,128)(2,1)S(1)}, bf16[2,2,64,512]{3,2,1,0:T(8,128)(2,1)S(1)}, u32[]{:S(2)}, u32[]{:S(2)}) collective-permute-start(bf16[2,2,64,512]{3,2,1,0:T(8,128)(2,1)S(1)} %get-tuple-element.36), channel_id=1, source_target_pairs={{0,16},{2,18},{4,20},{6,22},{8,24},{10,26},{12,28},{14,30},{16,0},... | collective-permute-start | bytes 786440 | tf_op jit(solution)/shard_map/ppermute | solution.py:197
  1.7 1.0 copy-start.13
  2.8 0.7 copy-start.18
  10.9 3.3 copy-start.8
  14.2 9.8 %copy-start.14 = (bf16[512,512]{1,0:T(8,128)(2,1)S(1)}, bf16[512,512]{1,0:T(8,128)(2,1)}, u32[]{:S(2)}) copy-start(bf16[512,512]{1,0:T(8,128)(2,1)} %w_ref.6) | copy-start | bytes 1572868
  14.2 9.8 %copy-start.19 = (f32[8,512]{1,0:T(8,128)S(1)}, f32[8,512]{1,0:T(8,128)}, u32[]{:S(2)}) copy-start(f32[8,512]{1,0:T(8,128)} %tw_ref.3) | copy-start | bytes 49156
  14.3 190.9 %all-to-all-start = ((bf16[16,8,32,1024]{3,2,1,0:T(8,128)(2,1)}), bf16[16,8,32,1024]{3,2,1,0:T(8,128)(2,1)}, u32[]{:S(2)}, u32[]{:S(2)}) async-start(bf16[16,8,32,1024]{3,2,1,0:T(8,128)(2,1)} %copy-done.8), calls=%async_computation | async-start | bytes 16777216 | tf_op jit(solution)/shard_map/all_to_all | solution.py:193
  22.5 148.9 %collective-permute-start.1 = (bf16[2,2,128,512]{3,2,1,0:T(8,128)(2,1)S(1)}, bf16[2,2,128,512]{3,2,1,0:T(8,128)(2,1)S(1)}, u32[]{:S(2)}, u32[]{:S(2)}) collective-permute-start(bf16[2,2,128,512]{3,2,1,0:T(8,128)(2,1)S(1)} %pad_maximum_fusion.2), channel_id=1, source_target_pairs={{0,8},{2,10},{4,12},{6,14},{8,0},{10,2},{12,4},{14,6},{16,24},{18,... | collective-permute-start | bytes 1572872 | tf_op jit(solution)/shard_map/ppermute | solution.py:197
  31.4 3.4 copy-start.7
  172.5 38.8 %copy-start.22 = (f32[128,32]{0,1:T(8,128)S(1)}, f32[128,32]{0,1:T(8,128)}, u32[]{:S(2)}) copy-start(f32[128,32]{0,1:T(8,128)} %param.20) | copy-start | bytes 49156
  205.1 187.3 %all-to-all-start.1 = ((bf16[16,8,32,1024]{3,2,1,0:T(8,128)(2,1)}), bf16[16,8,32,1024]{3,2,1,0:T(8,128)(2,1)}, u32[]{:S(2)}, u32[]{:S(2)}) async-start(bf16[16,8,32,1024]{3,2,1,0:T(8,128)(2,1)} %copy-done.7), calls=%async_computation.1 | async-start | bytes 16777216 | tf_op jit(solution)/shard_map/all_to_all | solution.py:193
  209.8 80.9 %copy-start.16 = (bf16[128,128]{1,0:T(8,128)(2,1)S(1)}, bf16[128,128]{1,0:T(8,128)(2,1)}, u32[]{:S(2)}) copy-start(bf16[128,128]{1,0:T(8,128)(2,1)} %fwd_ref.3) | copy-start | bytes 98308
  209.8 80.9 %copy-start.17 = (bf16[128,128]{1,0:T(8,128)(2,1)S(1)}, bf16[128,128]{1,0:T(8,128)(2,1)}, u32[]{:S(2)}) copy-start(bf16[128,128]{1,0:T(8,128)(2,1)} %inv_ref.3) | copy-start | bytes 98308
  209.8 79.5 %collective-permute-start.2 = (bf16[2,2,256,512]{3,2,1,0:T(8,128)(2,1)}, bf16[2,2,256,512]{3,2,1,0:T(8,128)(2,1)S(1)}, u32[]{:S(2)}, u32[]{:S(2)}) collective-permute-start(bf16[2,2,256,512]{3,2,1,0:T(8,128)(2,1)} %pad_maximum_fusion.1), channel_id=1, source_target_pairs={{0,4},{2,6},{4,0},{6,2},{8,12},{10,14},{12,8},{14,10},{16,20},{18,... | collective-permute-start | bytes 3145736 | tf_op jit(solution)/shard_map/ppermute | solution.py:197
  290.7 3.4 copy-start.4
  312.8 3.3 copy-start.6
  392.4 187.3 %all-to-all-start.2 = ((bf16[16,8,32,1024]{3,2,1,0:T(8,128)(2,1)}), bf16[16,8,32,1024]{3,2,1,0:T(8,128)(2,1)}, u32[]{:S(2)}, u32[]{:S(2)}) async-start(bf16[16,8,32,1024]{3,2,1,0:T(8,128)(2,1)} %copy-done.6), calls=%async_computation.2 | async-start | bytes 16777216 | tf_op jit(solution)/shard_map/all_to_all | solution.py:193
  397.1 4.8 collective-permute-start.3
  403.4 3.4 copy-start.5
  425.5 2.7 copy-start.11
  428.2 1.4 copy-start.15
  579.7 4.9 copy-start.12
  579.7 4.9 copy-start.20
  579.7 4.9 copy-start.21
  579.7 142.4 %all-to-all-start.3 = ((bf16[16,6,32,1024]{3,2,1,0:T(8,128)(2,1)}), bf16[16,6,32,1024]{3,2,1,0:T(8,128)(2,1)}, u32[]{:S(2)}, u32[]{:S(2)}) async-start(bf16[16,6,32,1024]{3,2,1,0:T(8,128)(2,1)} %copy-done.11), calls=%async_computation.3 | async-start | bytes 12582912 | tf_op jit(solution)/shard_map/all_to_all | solution.py:193
  584.6 17.1 %copy-start.23 = (f32[2048]{0:T(1024)S(1)}, f32[2048]{0:T(1024)}, u32[]{:S(2)}) copy-start(f32[2048]{0:T(1024)} %param.23) | copy-start | bytes 24580
  596.8 3.4 copy-start.9
  600.2 3.7 collective-permute-start.4
  603.9 2.2 copy-start.1
  606.1 3.4 copy-start.10
  722.2 52.3 %all-to-all-start.4 = ((bf16[16,2,32,1024]{3,2,1,0:T(8,128)(2,1)}), bf16[16,2,32,1024]{3,2,1,0:T(8,128)(2,1)S(1)}, u32[]{:S(2)}, u32[]{:S(2)}) async-start(bf16[16,2,32,1024]{3,2,1,0:T(8,128)(2,1)} %copy-done.15), calls=%async_computation.4 | async-start | bytes 4194304 | tf_op jit(solution)/shard_map/all_to_all | solution.py:193
  726.8 13.3 %copy-start.2 = (bf16[2,2,1024,512]{3,2,1,0:T(8,128)(2,1)S(1)}, bf16[2,2,1024,512]{3,2,1,0:T(8,128)(2,1)}, u32[]{:S(2)}) copy-start(bf16[2,2,1024,512]{3,2,1,0:T(8,128)(2,1)} %constant_dynamic-update-slice_fusion.weight_ref) | copy-start | bytes 12582916
  736.4 3.8 collective-permute-start.5
  774.5 5.8 copy-start
  780.3 6.1 copy-start.3
  782.7 3.7 collective-permute-start.6

commit v4 on v3

--- a/solution.py
+++ b/solution.py
@@ -9,12 +9,12 @@
 
 VMEM_BYTES = 32 * 1024 * 1024
 EPS = 1e-06
-RETURN_ROWS = ((8,), (6, 2))
 STEP_ROWS = 2
-
-
-def params():
-    return pltpu.CompilerParams(vmem_limit_bytes=VMEM_BYTES)
+LAST_ROWS = 2
+
+
+def params(size=VMEM_BYTES):
+    return pltpu.CompilerParams(vmem_limit_bytes=size)
 
 
 def first_kernel(tok_ref, w_ref, tw_ref, out_ref):
@@ -185,10 +185,6 @@
     return lax.optimization_barrier((x,) + deps)[0]
 
 
-def after(x, *deps):
-    return lax.optimization_barrier((x,) + deps)[0]
-
-
 def exchange(x):
     return lax.all_to_all(x, "seq", split_axis=0, concat_axis=0, tiled=True)
 
@@ -213,7 +209,6 @@
     up_weight,
     down_weight,
 ):
-
     seqs, tok_dev, ch = tokens.shape
     inner = inner_forward.shape[0]
     a_dev = tok_dev // inner
@@ -245,7 +240,8 @@
         waits = [last, weights]
     out = None
     for s in range(seqs):
-        groups = RETURN_ROWS[min(s, 1)]
+        last_rows = LAST_ROWS if s + 1 == seqs and a_dev > LAST_ROWS else 0
+        groups = (a_dev - last_rows, last_rows) if last_rows else (a_dev,)
         back = outer_section(
             spread[s], outer_forward, outer_inverse, twiddle_inverse, freq_kernel, groups, n
         )

time: 794 us -> 794 us (level)
  no operation moved by 1% of the time
where the time goes in v4:
time: 794 us; the launch traced here: 793 us
  waiting for transfers between devices  586 us (74%)
  Pallas kernels  126 us (16%)
  local copies, waits for them, and re-layouts  41.5 us (5%)
  starting transfers between devices  35.1 us (4%)
    all_to_all x5, waiting for transfers between devices, exchange(): return lax.all_to_all(x, 'seq', split_axis=0, concat_axis=0, tiled=True)  363 us
    ppermute x4, waiting for transfers between devices, more_hidden(): other = lax.ppermute(weights, 'seq', [(j, j ^ step) for j in range(n)])  216 us
    pallas_call x3, Pallas kernels, mlp_rows(): pl.pallas_call(functools.partial(mlp_kernel, width, len(sqs)), grid=(coun...  49.9 us
    unnamed x51, local copies, waits for them, and re-layouts  39.9 us
    pallas_call x2, Pallas kernels, outer_section(): pl.pallas_call(functools.partial(outer_kernel, groups), grid=(k_dev // ro...  37.4 us
    all_to_all x5, starting transfers between devices, exchange(): return lax.all_to_all(x, 'seq', split_axis=0, concat_axis=0, tiled=True)  27.2 us
    pallas_call x3, Pallas kernels, gate_rows(): pl.pallas_call(gate_kernel, grid=(count,), in_specs=[pl.BlockSpec((1, 1,...  24.2 us
  transfers between devices with their start and end apart: 12, of which 11 were waited for; matrix products, arithmetic and copies ran while one was open for 1% of the time, Pallas kernels for 15%

profile of v4, /device:TPU:16, one launch (start us, length us, event | category | flops | bytes accessed | tf_op | source)
XLA Modules:
  0.0 793.3 jit_solution(13630249410613570338)
XLA Ops:
  0.0 1.7 constant_dynamic-update-slice_fusion.4
  1.7 1.0 copy-done.13
  3.5 7.4 first_section.3
  10.9 3.3 copy-done.8
  14.3 8.3 %all-to-all-start = ((bf16[16,8,32,1024]{3,2,1,0:T(8,128)(2,1)}), bf16[16,8,32,1024]{3,2,1,0:T(8,128)(2,1)}, u32[]{:S(2)}, u32[]{:S(2)}) async-start(bf16[16,8,32,1024]{3,2,1,0:T(8,128)(2,1)} %copy-done.8), calls=%async_computation | async-start | bytes 16777216 | tf_op jit(solution)/shard_map/all_to_all | solution.py:189
  22.5 1.5 collective-permute-start.1
  24.0 7.4 first_section.2
  31.4 3.4 copy-done.7
  34.8 136.6 %collective-permute-done.1 = bf16[2,2,128,512]{3,2,1,0:T(8,128)(2,1)S(1)} collective-permute-done((bf16[2,2,128,512]{3,2,1,0:T(8,128)(2,1)S(1)}, bf16[2,2,128,512]{3,2,1,0:T(8,128)(2,1)S(1)}, u32[]{:S(2)}, u32[]{:S(2)}) %collective-permute-start.1) | collective-permute-done | bytes 524320 | tf_op jit(solution)/shard_map/ppermute | solution.py:193
  171.4 1.1 pad_maximum_fusion.1
  172.5 32.6 %all-to-all-done = bf16[16,8,32,1024]{3,2,1,0:T(8,128)(2,1)} async-done(((bf16[16,8,32,1024]{3,2,1,0:T(8,128)(2,1)}), bf16[16,8,32,1024]{3,2,1,0:T(8,128)(2,1)}, u32[]{:S(2)}, u32[]{:S(2)}) %all-to-all-start) | async-done | bytes 8388640 | tf_op jit(solution)/shard_map/all_to_all | solution.py:189
  205.1 4.7 all-to-all-start.1
  209.8 1.5 collective-permute-start.2
  211.4 77.8 %collective-permute-done.2 = bf16[2,2,256,512]{3,2,1,0:T(8,128)(2,1)S(1)} collective-permute-done((bf16[2,2,256,512]{3,2,1,0:T(8,128)(2,1)}, bf16[2,2,256,512]{3,2,1,0:T(8,128)(2,1)S(1)}, u32[]{:S(2)}, u32[]{:S(2)}) %collective-permute-start.2) | collective-permute-done | bytes 1048608 | tf_op jit(solution)/shard_map/ppermute | solution.py:193
  289.3 1.4 pad_maximum_fusion
  290.7 3.4 copy-done.4
  294.1 18.7 %outer_section.3 = bf16[16,8,32,1024]{3,2,1,0:T(8,128)(2,1)S(1)} custom-call(bf16[128,128]{1,0:T(8,128)(2,1)S(1)} %copy-done.16, bf16[128,128]{1,0:T(8,128)(2,1)S(1)} %copy-done.17, f32[2,128,16]{2,1,0:T(8,128)S(1)} %bitcast.16, bf16[128,32,1024]{2,1,0:T(8,128)(2,1)S(1)} %copy-done.4, bf16[128,32,1024]{2,1,0:T(8,128)(2,1)} %bitcast.8.spread_ref), custom_call_target="tpu_custom_call" | custom-call | tf_op jit(solution)/shard_map/outer_section/pallas_call | solution.py:76
  312.9 3.3 copy-done.6
  316.1 76.2 %all-to-all-done.1 = bf16[16,8,32,1024]{3,2,1,0:T(8,128)(2,1)} async-done(((bf16[16,8,32,1024]{3,2,1,0:T(8,128)(2,1)}), bf16[16,8,32,1024]{3,2,1,0:T(8,128)(2,1)}, u32[]{:S(2)}, u32[]{:S(2)}) %all-to-all-start.1) | async-done | bytes 8388640 | tf_op jit(solution)/shard_map/all_to_all | solution.py:189
  392.4 4.8 all-to-all-start.2
  398.9 1.0 constant_dynamic-update-slice_fusion.1
  399.9 2.0 collective-permute-done.3
  401.9 1.5 constant_dynamic-update-slice_fusion.weight_ref
  403.4 3.4 copy-done.5
  406.8 18.7 %outer_section.2 = (bf16[16,6,32,1024]{3,2,1,0:T(8,128)(2,1)S(1)}, bf16[16,2,32,1024]{3,2,1,0:T(8,128)(2,1)S(1)}) custom-call(bf16[128,128]{1,0:T(8,128)(2,1)S(1)} %copy-done.16, bf16[128,128]{1,0:T(8,128)(2,1)S(1)} %copy-done.17, f32[2,128,16]{2,1,0:T(8,128)S(1)} %bitcast.17, bf16[128,32,1024]{2,1,0:T(8,128)(2,1)S(1)} %copy-done.5, ...), custom_call_target="tpu_custom_call" | custom-call | tf_op jit(solution)/shard_map/outer_section/pallas_call | solution.py:76
  425.5 2.7 copy-done.11
  428.2 1.4 copy-done.15
  429.6 150.1 %all-to-all-done.2.part_ref = bf16[16,8,32,1024]{3,2,1,0:T(8,128)(2,1)} async-done(((bf16[16,8,32,1024]{3,2,1,0:T(8,128)(2,1)}), bf16[16,8,32,1024]{3,2,1,0:T(8,128)(2,1)}, u32[]{:S(2)}, u32[]{:S(2)}) %all-to-all-start.2) | async-done | bytes 8388640 | tf_op jit(solution)/shard_map/all_to_all | solution.py:189
  579.7 4.8 all-to-all-start.3
  584.6 12.2 %gate_rows.3 = (bf16[8,512,1024]{2,1,0:T(8,128)(2,1)S(1)}, f32[8,1,512]{2,1,0:T(1,128)S(1)}) custom-call(bf16[2,8,512,1024]{3,2,1,0:T(8,128)(2,1)} %bitcast.13, bf16[512,512]{1,0:T(8,128)(2,1)S(1)} %copy-done.12, f32[1,1024]{1,0:T(1,128)S(1)} %bitcast.21, f32[1,1024]{1,0:T(1,128)S(1)} %bitcast.24, bf16[16,8,32,1024]{3,2,1,0:T(8,128)(2,1)} %all-to-all-done.2.part_ref), custom_call_target="tpu_custom_call" | custom-call | tf_op jit(solution)/shard_map/gate_rows/pallas_call | solution.py:116
  596.8 3.4 copy-done.9
  600.2 1.5 collective-permute-start.4
  601.7 2.2 collective-permute-done.4.rest_1_
  603.9 2.2 copy-done.1
  606.1 3.4 copy-done.10
  609.5 24.4 %mlp_rows.3.rest_2_ = bf16[16,512,1024]{2,1,0:T(8,128)(2,1)} custom-call(bf16[8,512,1024]{2,1,0:T(8,128)(2,1)S(1)} %copy-done.10, f32[1,1024]{1,0:T(1,128)S(1)} %bitcast.18, bf16[2,2,1024,512]{3,2,1,0:T(8,128)(2,1)S(1)} %copy-done.1, f32[8,1,512]{2,1,0:T(1,128)S(1)} %get-tuple-element.27.rest_0_, f32[8,1,512]{2,1,0:T(1,128)S(1)} %collective-permute-done.4.rest_1_), custom_call_target="tpu_custom_call" | custom-call | tf_op jit(solution)/shard_map/mlp_rows/pallas_call | solution.py:172
  633.9 88.3 %all-to-all-done.3.part_ref = bf16[16,6,32,1024]{3,2,1,0:T(8,128)(2,1)} async-done(((bf16[16,6,32,1024]{3,2,1,0:T(8,128)(2,1)}), bf16[16,6,32,1024]{3,2,1,0:T(8,128)(2,1)}, u32[]{:S(2)}, u32[]{:S(2)}) %all-to-all-start.3) | async-done | bytes 6291488 | tf_op jit(solution)/shard_map/all_to_all | solution.py:189
  722.2 4.7 all-to-all-start.4
  726.9 9.6 %gate_rows.4 = (bf16[6,512,1024]{2,1,0:T(8,128)(2,1)S(1)}, f32[6,1,512]{2,1,0:T(1,128)S(1)}) custom-call(bf16[2,8,512,1024]{3,2,1,0:T(8,128)(2,1)} %bitcast.14, bf16[512,512]{1,0:T(8,128)(2,1)S(1)} %copy-done.12, f32[1,1024]{1,0:T(1,128)S(1)} %bitcast.22, f32[1,1024]{1,0:T(1,128)S(1)} %bitcast.25, bf16[16,6,32,1024]{3,2,1,0:T(8,128)(2,1)} %all-to-all-done.3.part_ref), custom_call_target="tpu_custom_call" | custom-call | tf_op jit(solution)/shard_map/gate_rows/pallas_call | solution.py:116
  736.4 1.6 collective-permute-start.5
  738.0 2.2 collective-permute-done.5.rest_1_
  740.2 18.7 %mlp_rows.4.rest_2_ = bf16[16,512,1024]{2,1,0:T(8,128)(2,1)} custom-call(bf16[6,512,1024]{2,1,0:T(8,128)(2,1)S(1)} %get-tuple-element.30.gated_ref, f32[1,1024]{1,0:T(1,128)S(1)} %bitcast.19, bf16[2,2,1024,512]{3,2,1,0:T(8,128)(2,1)S(1)} %copy-done.2, f32[6,1,512]{2,1,0:T(1,128)S(1)} %get-tuple-element.31.rest_0_, ...), custom_call_target="tpu_custom_call", output_to_operand_aliasing={{}: (5, {})} | custom-call | tf_op jit(solution)/shard_map/mlp_rows/pallas_call | solution.py:172
  758.9 15.6 %all-to-all-done.4.part_ref = bf16[16,2,32,1024]{3,2,1,0:T(8,128)(2,1)S(1)} async-done(((bf16[16,2,32,1024]{3,2,1,0:T(8,128)(2,1)}), bf16[16,2,32,1024]{3,2,1,0:T(8,128)(2,1)S(1)}, u32[]{:S(2)}, u32[]{:S(2)}) %all-to-all-start.4) | async-done | bytes 2097184 | tf_op jit(solution)/shard_map/all_to_all | solution.py:189
  774.5 5.8 copy-done
  780.3 2.5 gate_rows.5
  782.7 1.6 collective-permute-start.6
  784.3 2.1 collective-permute-done.6.rest_1_
  786.4 6.9 mlp_rows.5
  (44 shorter events, 2.6 us)
Async XLA Ops:
  1.7 12.5 %collective-permute-start = (bf16[2,2,64,512]{3,2,1,0:T(8,128)(2,1)S(1)}, bf16[2,2,64,512]{3,2,1,0:T(8,128)(2,1)S(1)}, u32[]{:S(2)}, u32[]{:S(2)}) collective-permute-start(bf16[2,2,64,512]{3,2,1,0:T(8,128)(2,1)S(1)} %get-tuple-element.36), channel_id=1, source_target_pairs={{0,16},{2,18},{4,20},{6,22},{8,24},{10,26},{12,28},{14,30},{16,0},... | collective-permute-start | bytes 786440 | tf_op jit(solution)/shard_map/ppermute | solution.py:193
  1.7 1.0 copy-start.13
  2.8 0.7 copy-start.18
  10.9 3.3 copy-start.8
  14.2 9.8 %copy-start.14 = (bf16[512,512]{1,0:T(8,128)(2,1)S(1)}, bf16[512,512]{1,0:T(8,128)(2,1)}, u32[]{:S(2)}) copy-start(bf16[512,512]{1,0:T(8,128)(2,1)} %w_ref.6) | copy-start | bytes 1572868
  14.2 9.8 %copy-start.19 = (f32[8,512]{1,0:T(8,128)S(1)}, f32[8,512]{1,0:T(8,128)}, u32[]{:S(2)}) copy-start(f32[8,512]{1,0:T(8,128)} %tw_ref.3) | copy-start | bytes 49156
  14.3 190.9 %all-to-all-start = ((bf16[16,8,32,1024]{3,2,1,0:T(8,128)(2,1)}), bf16[16,8,32,1024]{3,2,1,0:T(8,128)(2,1)}, u32[]{:S(2)}, u32[]{:S(2)}) async-start(bf16[16,8,32,1024]{3,2,1,0:T(8,128)(2,1)} %copy-done.8), calls=%async_computation | async-start | bytes 16777216 | tf_op jit(solution)/shard_map/all_to_all | solution.py:189
  22.5 148.9 %collective-permute-start.1 = (bf16[2,2,128,512]{3,2,1,0:T(8,128)(2,1)S(1)}, bf16[2,2,128,512]{3,2,1,0:T(8,128)(2,1)S(1)}, u32[]{:S(2)}, u32[]{:S(2)}) collective-permute-start(bf16[2,2,128,512]{3,2,1,0:T(8,128)(2,1)S(1)} %pad_maximum_fusion.2), channel_id=1, source_target_pairs={{0,8},{2,10},{4,12},{6,14},{8,0},{10,2},{12,4},{14,6},{16,24},{18,... | collective-permute-start | bytes 1572872 | tf_op jit(solution)/shard_map/ppermute | solution.py:193
  31.4 3.4 copy-start.7
  172.5 38.8 %copy-start.22 = (f32[128,32]{0,1:T(8,128)S(1)}, f32[128,32]{0,1:T(8,128)}, u32[]{:S(2)}) copy-start(f32[128,32]{0,1:T(8,128)} %param.20) | copy-start | bytes 49156
  205.1 187.3 %all-to-all-start.1 = ((bf16[16,8,32,1024]{3,2,1,0:T(8,128)(2,1)}), bf16[16,8,32,1024]{3,2,1,0:T(8,128)(2,1)}, u32[]{:S(2)}, u32[]{:S(2)}) async-start(bf16[16,8,32,1024]{3,2,1,0:T(8,128)(2,1)} %copy-done.7), calls=%async_computation.1 | async-start | bytes 16777216 | tf_op jit(solution)/shard_map/all_to_all | solution.py:189
  209.8 80.9 %copy-start.16 = (bf16[128,128]{1,0:T(8,128)(2,1)S(1)}, bf16[128,128]{1,0:T(8,128)(2,1)}, u32[]{:S(2)}) copy-start(bf16[128,128]{1,0:T(8,128)(2,1)} %fwd_ref.3) | copy-start | bytes 98308
  209.8 80.9 %copy-start.17 = (bf16[128,128]{1,0:T(8,128)(2,1)S(1)}, bf16[128,128]{1,0:T(8,128)(2,1)}, u32[]{:S(2)}) copy-start(bf16[128,128]{1,0:T(8,128)(2,1)} %inv_ref.3) | copy-start | bytes 98308
  209.8 79.5 %collective-permute-start.2 = (bf16[2,2,256,512]{3,2,1,0:T(8,128)(2,1)}, bf16[2,2,256,512]{3,2,1,0:T(8,128)(2,1)S(1)}, u32[]{:S(2)}, u32[]{:S(2)}) collective-permute-start(bf16[2,2,256,512]{3,2,1,0:T(8,128)(2,1)} %pad_maximum_fusion.1), channel_id=1, source_target_pairs={{0,4},{2,6},{4,0},{6,2},{8,12},{10,14},{12,8},{14,10},{16,20},{18,... | collective-permute-start | bytes 3145736 | tf_op jit(solution)/shard_map/ppermute | solution.py:193
  290.7 3.4 copy-start.4
  312.8 3.3 copy-start.6
  392.4 187.3 %all-to-all-start.2 = ((bf16[16,8,32,1024]{3,2,1,0:T(8,128)(2,1)}), bf16[16,8,32,1024]{3,2,1,0:T(8,128)(2,1)}, u32[]{:S(2)}, u32[]{:S(2)}) async-start(bf16[16,8,32,1024]{3,2,1,0:T(8,128)(2,1)} %copy-done.6), calls=%async_computation.2 | async-start | bytes 16777216 | tf_op jit(solution)/shard_map/all_to_all | solution.py:189
  397.1 4.8 collective-permute-start.3
  403.4 3.4 copy-start.5
  425.5 2.7 copy-start.11
  428.2 1.4 copy-start.15
  579.7 4.9 copy-start.12
  579.7 4.9 copy-start.20
  579.7 4.9 copy-start.21
  579.7 142.4 %all-to-all-start.3 = ((bf16[16,6,32,1024]{3,2,1,0:T(8,128)(2,1)}), bf16[16,6,32,1024]{3,2,1,0:T(8,128)(2,1)}, u32[]{:S(2)}, u32[]{:S(2)}) async-start(bf16[16,6,32,1024]{3,2,1,0:T(8,128)(2,1)} %copy-done.11), calls=%async_computation.3 | async-start | bytes 12582912 | tf_op jit(solution)/shard_map/all_to_all | solution.py:189
  584.6 17.1 %copy-start.23 = (f32[2048]{0:T(1024)S(1)}, f32[2048]{0:T(1024)}, u32[]{:S(2)}) copy-start(f32[2048]{0:T(1024)} %param.23) | copy-start | bytes 24580
  596.8 3.4 copy-start.9
  600.2 3.7 collective-permute-start.4
  603.9 2.2 copy-start.1
  606.1 3.4 copy-start.10
  722.2 52.3 %all-to-all-start.4 = ((bf16[16,2,32,1024]{3,2,1,0:T(8,128)(2,1)}), bf16[16,2,32,1024]{3,2,1,0:T(8,128)(2,1)S(1)}, u32[]{:S(2)}, u32[]{:S(2)}) async-start(bf16[16,2,32,1024]{3,2,1,0:T(8,128)(2,1)} %copy-done.15), calls=%async_computation.4 | async-start | bytes 4194304 | tf_op jit(solution)/shard_map/all_to_all | solution.py:189
  726.8 13.3 %copy-start.2 = (bf16[2,2,1024,512]{3,2,1,0:T(8,128)(2,1)S(1)}, bf16[2,2,1024,512]{3,2,1,0:T(8,128)(2,1)}, u32[]{:S(2)}) copy-start(bf16[2,2,1024,512]{3,2,1,0:T(8,128)(2,1)} %constant_dynamic-update-slice_fusion.weight_ref) | copy-start | bytes 12582916
  736.4 3.8 collective-permute-start.5
  774.5 5.8 copy-start
  780.3 6.1 copy-start.3
  782.7 3.7 collective-permute-start.6

commit v5 on v4

--- a/solution.py
+++ b/solution.py
@@ -8,6 +8,8 @@
 from jax.sharding import PartitionSpec as P
 
 VMEM_BYTES = 32 * 1024 * 1024
+MOST_VMEM_BYTES = 56 * 1024 * 1024
+GATE_VMEM_BYTES = 48 * 1024 * 1024
 EPS = 1e-06
 STEP_ROWS = 2
 LAST_ROWS = 2
@@ -42,7 +44,7 @@
         ],
         out_specs=pl.BlockSpec((n, step, rows, ch), lambda a: (0, a, 0, 0)),
         out_shape=jax.ShapeDtypeStruct((n, a_dev, rows, ch), jnp.bfloat16),
-        compiler_params=params(),
+        compiler_params=params(MOST_VMEM_BYTES),
         name="first_section",
     )(blocked, inner_forward, twiddle)
 
@@ -131,14 +133,14 @@
             jax.ShapeDtypeStruct((count, inner, ch), jnp.bfloat16),
             jax.ShapeDtypeStruct((count, 1, inner), jnp.float32),
         ],
-        compiler_params=params(),
+        compiler_params=params(GATE_VMEM_BYTES),
         name="gate_rows",
     )(blocked, inner_inverse, gain, bias, parts)
 
 
-def mlp_kernel(width, n_sq, gated_ref, gain_ref, weight_ref, *rest):
+def mlp_kernel(width, n_sq, gated_ref, gain_ref, up_ref, down_ref, *rest):
     out_ref = rest[-1]
-    _, blocks, _, wb = weight_ref.shape
+    blocks, _, wb = up_ref.shape
     total = rest[0][0]
     for sq_ref in rest[1:n_sq]:
         total = total + sq_ref[0]
@@ -149,10 +151,10 @@
         g = gated_ref[0, :, cols].astype(jnp.float32)
         normed = (g * scale * gain_ref[:, cols]).astype(jnp.bfloat16)
         lifted = lax.dot_general(
-            normed, weight_ref[0, b], (((1,), (1,)), ((), ())), preferred_element_type=jnp.float32
+            normed, up_ref[b], (((1,), (1,)), ((), ())), preferred_element_type=jnp.float32
         )
         hidden = jax.nn.gelu(lifted, approximate=True).astype(jnp.bfloat16)
-        lowered = jnp.dot(hidden, weight_ref[1, b], preferred_element_type=jnp.float32)
+        lowered = jnp.dot(hidden, down_ref[b], preferred_element_type=jnp.float32)
         out_ref[0, :, cols] = (g + lowered).astype(jnp.bfloat16)
 
 
@@ -162,8 +164,9 @@
         pl.BlockSpec((1, inner, ch), lambda j: (j, 0, 0)),
         pl.BlockSpec((1, ch), lambda j: (0, 0)),
         pl.BlockSpec(memory_space=pltpu.VMEM),
+        pl.BlockSpec(memory_space=pltpu.VMEM),
     ] + [pl.BlockSpec((1, 1, inner), lambda j: (j, 0, 0))] * len(sqs)
-    args = [gated, gain, weights, *sqs]
+    args = [gated, gain, *weights, *sqs]
     aliases = {}
     if out is not None:
         aliases = {len(args): 0}
@@ -190,8 +193,8 @@
 
 
 def more_hidden(weights, n, step):
-    other = lax.ppermute(weights, "seq", [(j, j ^ step) for j in range(n)])
-    return jnp.concatenate([weights, other], axis=2)
+    pairs = [(j, j ^ step) for j in range(n)]
+    return [jnp.concatenate([w, lax.ppermute(w, "seq", pairs)], axis=1) for w in weights]
 
 
 def local_blocks(
@@ -220,9 +223,9 @@
     norm = lax.dynamic_slice_in_dim(norm_gain, my_ch * ch, ch, 0).reshape(1, ch)
     gain, bias = gate_gain.reshape(1, ch), gate_bias.reshape(1, ch)
     held = ch // up_weight.shape[2]
-    weights = lax.dynamic_slice_in_dim(
-        jnp.stack([up_weight, down_weight]), my_ch * held, held, 1
-    )
+    weights = [
+        lax.dynamic_slice_in_dim(w, my_ch * held, held, 0) for w in (up_weight, down_weight)
+    ]
     weights = more_hidden(weights, n, n // 2)
 
     parts = [
@@ -230,14 +233,14 @@
     ]
     step = n // 2
     spread = []
-    waits = [weights]
+    waits = weights
     for p in parts:
         last = exchange(after(p, *waits))
         spread.append(last.reshape(outer, -1, ch))
         if step > 1:
             step //= 2
             weights = more_hidden(weights, n, step)
-        waits = [last, weights]
+        waits = [last, *weights]
     out = None
     for s in range(seqs):
         last_rows = LAST_ROWS if s + 1 == seqs and a_dev > LAST_ROWS else 0
@@ -254,7 +257,7 @@
             while step > 1:
                 step //= 2
                 weights = more_hidden(weights, n, step)
-                waits.append(weights)
+                waits += weights
             gated, sq = gate_rows(blocked, inner_inverse, gain, bias, part, s, first)
             sqs = [sq] + [
                 lax.ppermute(sq, "ch", [(j, (j + r) % n_ch) for j in range(n_ch)])

time: 794 us -> 790 us (level)
  local copies, waits for them, and re-layouts: 41.5 us -> 31.8 us
  Pallas kernels: 126 us -> 134 us
  waiting for transfers between devices: 586 us -> 578 us
    unnamed x51 -> x52, local copies, waits for them, and re-layouts: 39.9 us -> 31.6 us
    ppermute x4 -> x8, waiting for transfers between devices: 216 us -> 212 us  [more_hidden(): lax.ppermute(w, 'seq', pairs)]
  transfers between devices with their start and end apart: 12 -> 16, of which waited for: 11 -> 12; matrix products, arithmetic and copies ran while one was open for 1% -> 2% of each run, Pallas kernels for 15% -> 16%
where the time goes in v5:
time: 790 us; the launch traced here: 789 us
  waiting for transfers between devices  578 us (73%)
  Pallas kernels  134 us (17%)
  starting transfers between devices  37.4 us (5%)
  local copies, waits for them, and re-layouts  31.8 us (4%)
    all_to_all x5, waiting for transfers between devices, exchange(): return lax.all_to_all(x, 'seq', split_axis=0, concat_axis=0, tiled=True)  360 us
    ppermute x8, waiting for transfers between devices, more_hidden(): lax.ppermute(w, 'seq', pairs)  212 us
    pallas_call x3, Pallas kernels, mlp_rows(): pl.pallas_call(functools.partial(mlp_kernel, width, len(sqs)), grid=(coun...  49.7 us
    pallas_call x2, Pallas kernels, outer_section(): pl.pallas_call(functools.partial(outer_kernel, groups), grid=(k_dev // ro...  37.4 us
    unnamed x52, local copies, waits for them, and re-layouts  31.6 us
    pallas_call x3, Pallas kernels, gate_rows(): pl.pallas_call(gate_kernel, grid=(count,), in_specs=[pl.BlockSpec((1, 1,...  28.4 us
    all_to_all x5, starting transfers between devices, exchange(): return lax.all_to_all(x, 'seq', split_axis=0, concat_axis=0, tiled=True)  25.2 us
    pallas_call x2, Pallas kernels, first_section(): pl.pallas_call(first_kernel, grid=(a_dev // step,), in_specs=[pl.BlockSpe...  18.9 us
  transfers between devices with their start and end apart: 16, of which 12 were waited for; matrix products, arithmetic and copies ran while one was open for 2% of the time, Pallas kernels for 16%

profile of v5, /device:TPU:16, one launch (start us, length us, event | category | flops | bytes accessed | tf_op | source)
XLA Modules:
  0.0 788.5 jit_solution(1860292139267020597)
XLA Ops:
  1.0 1.6 constant_dynamic-update-slice_fusion.9
  2.6 2.9 collective-permute-start.1
  5.5 9.5 %first_section.3 = bf16[16,8,32,1024]{3,2,1,0:T(8,128)(2,1)} custom-call(bf16[2,8,512,1024]{3,2,1,0:T(8,128)(2,1)} %bitcast.20, bf16[512,512]{1,0:T(8,128)(2,1)} %w_ref.6, f32[8,512]{1,0:T(8,128)} %tw_ref.3), custom_call_target="tpu_custom_call" | custom-call | tf_op jit(solution)/shard_map/first_section/pallas_call | solution.py:37
  15.8 6.2 all-to-all-start
  21.9 1.5 collective-permute-start.2
  24.0 9.4 %first_section.2 = bf16[16,8,32,1024]{3,2,1,0:T(8,128)(2,1)} custom-call(bf16[2,8,512,1024]{3,2,1,0:T(8,128)(2,1)} %bitcast.21, bf16[512,512]{1,0:T(8,128)(2,1)} %w_ref.6, f32[8,512]{1,0:T(8,128)} %tw_ref.3), custom_call_target="tpu_custom_call" | custom-call | tf_op jit(solution)/shard_map/first_section/pallas_call | solution.py:37
  33.4 132.3 %collective-permute-done.2 = bf16[2,128,512]{2,1,0:T(8,128)(2,1)S(1)} collective-permute-done((bf16[2,128,512]{2,1,0:T(8,128)(2,1)}, bf16[2,128,512]{2,1,0:T(8,128)(2,1)S(1)}, u32[]{:S(2)}, u32[]{:S(2)}) %collective-permute-start.2) | collective-permute-done | bytes 262176 | tf_op jit(solution)/shard_map/ppermute | solution.py:197
  166.5 4.3 collective-permute-done.3
  171.7 32.8 %all-to-all-done = bf16[16,8,32,1024]{3,2,1,0:T(8,128)(2,1)} async-done(((bf16[16,8,32,1024]{3,2,1,0:T(8,128)(2,1)}), bf16[16,8,32,1024]{3,2,1,0:T(8,128)(2,1)}, u32[]{:S(2)}, u32[]{:S(2)}) %all-to-all-start) | async-done | bytes 8388640 | tf_op jit(solution)/shard_map/all_to_all | solution.py:192
  204.5 4.7 all-to-all-start.1
  209.2 1.5 collective-permute-start.4
  211.4 57.1 %collective-permute-done.4 = bf16[2,256,512]{2,1,0:T(8,128)(2,1)S(1)} collective-permute-done((bf16[2,256,512]{2,1,0:T(8,128)(2,1)}, bf16[2,256,512]{2,1,0:T(8,128)(2,1)S(1)}, u32[]{:S(2)}, u32[]{:S(2)}) %collective-permute-start.4) | collective-permute-done | bytes 524320 | tf_op jit(solution)/shard_map/ppermute | solution.py:197
  268.5 1.9 pad_maximum_fusion
  270.4 18.2 %collective-permute-done.5 = bf16[2,256,512]{2,1,0:T(8,128)(2,1)} collective-permute-done((bf16[2,256,512]{2,1,0:T(8,128)(2,1)}, bf16[2,256,512]{2,1,0:T(8,128)(2,1)}, u32[]{:S(2)}, u32[]{:S(2)}) %collective-permute-start.5) | collective-permute-done | bytes 524320 | tf_op jit(solution)/shard_map/ppermute | solution.py:197
  288.7 2.2 pad_maximum_fusion.1
  290.9 3.4 copy-done
  294.3 18.7 %outer_section.3 = bf16[16,8,32,1024]{3,2,1,0:T(8,128)(2,1)S(1)} custom-call(bf16[128,128]{1,0:T(8,128)(2,1)S(1)} %copy-done.13, bf16[128,128]{1,0:T(8,128)(2,1)S(1)} %copy-done.14, f32[2,128,16]{2,1,0:T(8,128)S(1)} %bitcast.9, bf16[128,32,1024]{2,1,0:T(8,128)(2,1)S(1)} %copy-done, bf16[128,32,1024]{2,1,0:T(8,128)(2,1)} %bitcast.6.spread_ref), custom_call_target="tpu_custom_call" | custom-call | tf_op jit(solution)/shard_map/outer_section/pallas_call | solution.py:78
  313.1 3.4 copy-done.2
  316.5 75.3 %all-to-all-done.1 = bf16[16,8,32,1024]{3,2,1,0:T(8,128)(2,1)} async-done(((bf16[16,8,32,1024]{3,2,1,0:T(8,128)(2,1)}), bf16[16,8,32,1024]{3,2,1,0:T(8,128)(2,1)}, u32[]{:S(2)}, u32[]{:S(2)}) %all-to-all-start.1) | async-done | bytes 8388640 | tf_op jit(solution)/shard_map/all_to_all | solution.py:192
  391.8 4.8 all-to-all-start.2
  397.1 1.6 constant_dynamic-update-slice_fusion.8
  399.5 1.9 constant_dynamic-update-slice_fusion.6
  401.5 1.5 copy-done.3
  403.1 1.3 copy-done.4
  404.4 3.4 copy-done.1
  407.8 18.7 %outer_section.2 = (bf16[16,6,32,1024]{3,2,1,0:T(8,128)(2,1)S(1)}, bf16[16,2,32,1024]{3,2,1,0:T(8,128)(2,1)S(1)}) custom-call(bf16[128,128]{1,0:T(8,128)(2,1)S(1)} %copy-done.13, bf16[128,128]{1,0:T(8,128)(2,1)S(1)} %copy-done.14, f32[2,128,16]{2,1,0:T(8,128)S(1)} %bitcast.10, bf16[128,32,1024]{2,1,0:T(8,128)(2,1)S(1)} %copy-done.1, ...), custom_call_target="tpu_custom_call" | custom-call | tf_op jit(solution)/shard_map/outer_section/pallas_call | solution.py:78
  426.5 2.6 copy-done.9
  429.1 1.3 copy-done.12
  430.5 148.7 %all-to-all-done.2.part_ref = bf16[16,8,32,1024]{3,2,1,0:T(8,128)(2,1)} async-done(((bf16[16,8,32,1024]{3,2,1,0:T(8,128)(2,1)}), bf16[16,8,32,1024]{3,2,1,0:T(8,128)(2,1)}, u32[]{:S(2)}, u32[]{:S(2)}) %all-to-all-start.2) | async-done | bytes 8388640 | tf_op jit(solution)/shard_map/all_to_all | solution.py:192
  579.1 4.9 all-to-all-start.3
  584.1 13.6 %gate_rows.3 = (bf16[8,512,1024]{2,1,0:T(8,128)(2,1)}, f32[8,1,512]{2,1,0:T(1,128)S(1)}) custom-call(bf16[2,8,512,1024]{3,2,1,0:T(8,128)(2,1)} %bitcast.22, bf16[512,512]{1,0:T(8,128)(2,1)S(1)} %copy-done.11, f32[1,1024]{1,0:T(1,128)S(1)} %bitcast.14, f32[1,1024]{1,0:T(1,128)S(1)} %bitcast.17, bf16[16,8,32,1024]{3,2,1,0:T(8,128)(2,1)} %all-to-all-done.2.part_ref), custom_call_target="tpu_custom_call" | custom-call | tf_op jit(solution)/shard_map/gate_rows/pallas_call | solution.py:118
  597.7 1.5 collective-permute-start.8
  599.2 2.2 collective-permute-done.8.rest_1_
  601.4 1.6 copy-done.5
  603.0 3.4 copy-done.8
  606.4 24.4 %mlp_rows.3.rest_2_ = bf16[16,512,1024]{2,1,0:T(8,128)(2,1)} custom-call(bf16[8,512,1024]{2,1,0:T(8,128)(2,1)S(1)} %copy-done.8, f32[1,1024]{1,0:T(1,128)S(1)} %bitcast.11, bf16[2,1024,512]{2,1,0:T(8,128)(2,1)S(1)} %constant_dynamic-update-slice_fusion.up_ref, bf16[2,1024,512]{2,1,0:T(8,128)(2,1)S(1)} %copy-done.5, ...), custom_call_target="tpu_custom_call" | custom-call | tf_op jit(solution)/shard_map/mlp_rows/pallas_call | solution.py:175
  630.7 90.8 %all-to-all-done.3.part_ref = bf16[16,6,32,1024]{3,2,1,0:T(8,128)(2,1)} async-done(((bf16[16,6,32,1024]{3,2,1,0:T(8,128)(2,1)}), bf16[16,6,32,1024]{3,2,1,0:T(8,128)(2,1)}, u32[]{:S(2)}, u32[]{:S(2)}) %all-to-all-start.3) | async-done | bytes 6291488 | tf_op jit(solution)/shard_map/all_to_all | solution.py:192
  721.6 4.7 all-to-all-start.4
  726.3 10.8 %gate_rows.4 = (bf16[6,512,1024]{2,1,0:T(8,128)(2,1)}, f32[6,1,512]{2,1,0:T(1,128)S(1)}) custom-call(bf16[2,8,512,1024]{3,2,1,0:T(8,128)(2,1)} %bitcast.23, bf16[512,512]{1,0:T(8,128)(2,1)S(1)} %copy-done.11, f32[1,1024]{1,0:T(1,128)S(1)} %bitcast.15, f32[1,1024]{1,0:T(1,128)S(1)} %bitcast.18, bf16[16,6,32,1024]{3,2,1,0:T(8,128)(2,1)} %all-to-all-done.3.part_ref), custom_call_target="tpu_custom_call" | custom-call | tf_op jit(solution)/shard_map/gate_rows/pallas_call | solution.py:118
  737.1 1.5 collective-permute-start.9
  738.6 2.2 collective-permute-done.9.rest_1_
  740.8 2.8 copy-done.10
  743.6 18.5 %mlp_rows.4.rest_2_ = bf16[16,512,1024]{2,1,0:T(8,128)(2,1)} custom-call(bf16[6,512,1024]{2,1,0:T(8,128)(2,1)S(1)} %copy-done.10, f32[1,1024]{1,0:T(1,128)S(1)} %bitcast.12, bf16[2,1024,512]{2,1,0:T(8,128)(2,1)S(1)} %constant_dynamic-update-slice_fusion.up_ref, bf16[2,1024,512]{2,1,0:T(8,128)(2,1)S(1)} %copy-done.6, ...), custom_call_target="tpu_custom_call", output_to_operand_aliasing={{}: (6, {})} | custom-call | tf_op jit(solution)/shard_map/mlp_rows/pallas_call | solution.py:175
  762.1 11.9 %all-to-all-done.4.part_ref = bf16[16,2,32,1024]{3,2,1,0:T(8,128)(2,1)} async-done(((bf16[16,2,32,1024]{3,2,1,0:T(8,128)(2,1)}), bf16[16,2,32,1024]{3,2,1,0:T(8,128)(2,1)}, u32[]{:S(2)}, u32[]{:S(2)}) %all-to-all-start.4) | async-done | bytes 2097184 | tf_op jit(solution)/shard_map/all_to_all | solution.py:192
  774.0 4.0 gate_rows.5
  778.0 1.6 collective-permute-start.10
  779.6 2.1 collective-permute-done.10.rest_1_
  781.7 6.8 mlp_rows.5
  (56 shorter events, 6.2 us)
Async XLA Ops:
  0.9 164.8 %copy-start.18 = (bf16[2,64,512]{2,1,0:T(8,128)(2,1)}, bf16[2,64,512]{2,1,0:T(8,128)(2,1)S(1)}, u32[]{:S(2)}) copy-start(bf16[2,64,512]{2,1,0:T(8,128)(2,1)S(1)} %get-tuple-element.38) | copy-start | bytes 393220
  0.9 14.1 %collective-permute-start = (bf16[2,64,512]{2,1,0:T(8,128)(2,1)S(1)}, bf16[2,64,512]{2,1,0:T(8,128)(2,1)S(1)}, u32[]{:S(2)}, u32[]{:S(2)}) collective-permute-start(bf16[2,64,512]{2,1,0:T(8,128)(2,1)S(1)} %get-tuple-element.38), channel_id=1, source_target_pairs={{0,16},{2,18},{4,20},{6,22},{8,24},{10,26},{12,28},{14,30},{16,0},... | collective-permute-start | bytes 393224 | tf_op jit(solution)/shard_map/ppermute | solution.py:197
  2.6 168.2 %copy-start.19 = (bf16[2,64,512]{2,1,0:T(8,128)(2,1)}, bf16[2,64,512]{2,1,0:T(8,128)(2,1)S(1)}, u32[]{:S(2)}) copy-start(bf16[2,64,512]{2,1,0:T(8,128)(2,1)S(1)} %get-tuple-element.36) | copy-start | bytes 393220
  2.6 13.1 %collective-permute-start.1 = (bf16[2,64,512]{2,1,0:T(8,128)(2,1)S(1)}, bf16[2,64,512]{2,1,0:T(8,128)(2,1)S(1)}, u32[]{:S(2)}, u32[]{:S(2)}) collective-permute-start(bf16[2,64,512]{2,1,0:T(8,128)(2,1)S(1)} %get-tuple-element.36), channel_id=1, source_target_pairs={{0,16},{2,18},{4,20},{6,22},{8,24},{10,26},{12,28},{14,30},{16,0},... | collective-permute-start | bytes 393224 | tf_op jit(solution)/shard_map/ppermute | solution.py:197
  15.7 155.1 %copy-start.17 = (bf16[2,64,512]{2,1,0:T(8,128)(2,1)}, bf16[2,64,512]{2,1,0:T(8,128)(2,1)S(1)}, u32[]{:S(2)}) copy-start(bf16[2,64,512]{2,1,0:T(8,128)(2,1)S(1)} %collective-permute-done.1) | copy-start | bytes 393220
  15.8 188.7 %all-to-all-start = ((bf16[16,8,32,1024]{3,2,1,0:T(8,128)(2,1)}), bf16[16,8,32,1024]{3,2,1,0:T(8,128)(2,1)}, u32[]{:S(2)}, u32[]{:S(2)}) async-start(bf16[16,8,32,1024]{3,2,1,0:T(8,128)(2,1)} %first_section.3), calls=%async_computation | async-start | bytes 16777216 | tf_op jit(solution)/shard_map/all_to_all | solution.py:192
  21.9 143.8 %collective-permute-start.2 = (bf16[2,128,512]{2,1,0:T(8,128)(2,1)}, bf16[2,128,512]{2,1,0:T(8,128)(2,1)S(1)}, u32[]{:S(2)}, u32[]{:S(2)}) collective-permute-start(bf16[2,128,512]{2,1,0:T(8,128)(2,1)} %pad_maximum_fusion.4), channel_id=1, source_target_pairs={{0,8},{2,10},{4,12},{6,14},{8,0},{10,2},{12,4},{14,6},{16,24},{18,... | collective-permute-start | bytes 786440 | tf_op jit(solution)/shard_map/ppermute | solution.py:197
  23.4 147.4 %collective-permute-start.3 = (bf16[2,128,512]{2,1,0:T(8,128)(2,1)S(1)}, bf16[2,128,512]{2,1,0:T(8,128)(2,1)S(1)}, u32[]{:S(2)}, u32[]{:S(2)}) collective-permute-start(bf16[2,128,512]{2,1,0:T(8,128)(2,1)S(1)} %pad_maximum_fusion.5), channel_id=1, source_target_pairs={{0,8},{2,10},{4,12},{6,14},{8,0},{10,2},{12,4},{14,6},{16,24},{18,... | collective-permute-start | bytes 786440 | tf_op jit(solution)/shard_map/ppermute | solution.py:197
  171.7 39.6 %copy-start.20 = (f32[128,32]{0,1:T(8,128)S(1)}, f32[128,32]{0,1:T(8,128)}, u32[]{:S(2)}) copy-start(f32[128,32]{0,1:T(8,128)} %param.20) | copy-start | bytes 49156
  204.5 187.3 %all-to-all-start.1 = ((bf16[16,8,32,1024]{3,2,1,0:T(8,128)(2,1)}), bf16[16,8,32,1024]{3,2,1,0:T(8,128)(2,1)}, u32[]{:S(2)}, u32[]{:S(2)}) async-start(bf16[16,8,32,1024]{3,2,1,0:T(8,128)(2,1)} %first_section.2), calls=%async_computation.1 | async-start | bytes 16777216 | tf_op jit(solution)/shard_map/all_to_all | solution.py:192
  209.2 59.3 %collective-permute-start.4 = (bf16[2,256,512]{2,1,0:T(8,128)(2,1)}, bf16[2,256,512]{2,1,0:T(8,128)(2,1)S(1)}, u32[]{:S(2)}, u32[]{:S(2)}) collective-permute-start(bf16[2,256,512]{2,1,0:T(8,128)(2,1)} %pad_maximum_fusion.2), channel_id=1, source_target_pairs={{0,4},{2,6},{4,0},{6,2},{8,12},{10,14},{12,8},{14,10},{16,20},{18,... | collective-permute-start | bytes 1572872 | tf_op jit(solution)/shard_map/ppermute | solution.py:197
  210.7 78.0 %collective-permute-start.5 = (bf16[2,256,512]{2,1,0:T(8,128)(2,1)}, bf16[2,256,512]{2,1,0:T(8,128)(2,1)}, u32[]{:S(2)}, u32[]{:S(2)}) collective-permute-start(bf16[2,256,512]{2,1,0:T(8,128)(2,1)} %pad_maximum_fusion.3), channel_id=1, source_target_pairs={{0,4},{2,6},{4,0},{6,2},{8,12},{10,14},{12,8},{14,10},{16,20},{18,... | collective-permute-start | bytes 1572872 | tf_op jit(solution)/shard_map/ppermute | solution.py:197
  211.4 79.5 %copy-start.13 = (bf16[128,128]{1,0:T(8,128)(2,1)S(1)}, bf16[128,128]{1,0:T(8,128)(2,1)}, u32[]{:S(2)}) copy-start(bf16[128,128]{1,0:T(8,128)(2,1)} %fwd_ref.3) | copy-start | bytes 98308
  211.4 79.5 %copy-start.14 = (bf16[128,128]{1,0:T(8,128)(2,1)S(1)}, bf16[128,128]{1,0:T(8,128)(2,1)}, u32[]{:S(2)}) copy-start(bf16[128,128]{1,0:T(8,128)(2,1)} %inv_ref.3) | copy-start | bytes 98308
  290.9 3.4 copy-start
  313.0 3.4 copy-start.2
  391.8 187.3 %all-to-all-start.2 = ((bf16[16,8,32,1024]{3,2,1,0:T(8,128)(2,1)}), bf16[16,8,32,1024]{3,2,1,0:T(8,128)(2,1)}, u32[]{:S(2)}, u32[]{:S(2)}) async-start(bf16[16,8,32,1024]{3,2,1,0:T(8,128)(2,1)} %copy-done.2), calls=%async_computation.2 | async-start | bytes 16777216 | tf_op jit(solution)/shard_map/all_to_all | solution.py:192
  396.5 4.8 collective-permute-start.6
  396.7 4.8 collective-permute-start.7
  401.4 1.6 copy-start.3
  403.0 1.3 copy-start.4
  404.4 3.4 copy-start.1
  426.5 2.6 copy-start.9
  429.1 1.3 copy-start.12
  579.1 4.9 copy-start.11
  579.1 4.9 copy-start.15
  579.1 4.9 copy-start.16
  579.1 142.4 %all-to-all-start.3 = ((bf16[16,6,32,1024]{3,2,1,0:T(8,128)(2,1)}), bf16[16,6,32,1024]{3,2,1,0:T(8,128)(2,1)}, u32[]{:S(2)}, u32[]{:S(2)}) async-start(bf16[16,6,32,1024]{3,2,1,0:T(8,128)(2,1)} %copy-done.9), calls=%async_computation.3 | async-start | bytes 12582912 | tf_op jit(solution)/shard_map/all_to_all | solution.py:192
  584.1 15.1 %copy-start.21 = (f32[2048]{0:T(1024)S(1)}, f32[2048]{0:T(1024)}, u32[]{:S(2)}) copy-start(f32[2048]{0:T(1024)} %param.23) | copy-start | bytes 24580
  597.7 3.7 collective-permute-start.8
  601.4 1.6 copy-start.5
  603.0 3.4 copy-start.8
  721.6 52.4 %all-to-all-start.4 = ((bf16[16,2,32,1024]{3,2,1,0:T(8,128)(2,1)}), bf16[16,2,32,1024]{3,2,1,0:T(8,128)(2,1)}, u32[]{:S(2)}, u32[]{:S(2)}) async-start(bf16[16,2,32,1024]{3,2,1,0:T(8,128)(2,1)} %copy-done.12), calls=%async_computation.4 | async-start | bytes 4194304 | tf_op jit(solution)/shard_map/all_to_all | solution.py:192
  726.3 14.5 %copy-start.6 = (bf16[2,1024,512]{2,1,0:T(8,128)(2,1)S(1)}, bf16[2,1024,512]{2,1,0:T(8,128)(2,1)}, u32[]{:S(2)}) copy-start(bf16[2,1024,512]{2,1,0:T(8,128)(2,1)} %copy-done.4) | copy-start | bytes 6291460
  737.1 3.7 collective-permute-start.9
  740.8 2.8 copy-start.10
  774.0 7.7 copy-start.7
  778.0 3.7 collective-permute-start.10

commit v6 on v5

--- a/solution.py
+++ b/solution.py
@@ -11,7 +11,7 @@
 MOST_VMEM_BYTES = 56 * 1024 * 1024
 GATE_VMEM_BYTES = 48 * 1024 * 1024
 EPS = 1e-06
-STEP_ROWS = 2
+STEP_ROWS = 4
 LAST_ROWS = 2
 
 
@@ -194,7 +194,8 @@
 
 def more_hidden(weights, n, step):
     pairs = [(j, j ^ step) for j in range(n)]
-    return [jnp.concatenate([w, lax.ppermute(w, "seq", pairs)], axis=1) for w in weights]
+    got = [lax.ppermute(w, "seq", pairs) for w in weights]
+    return [jnp.concatenate(both, axis=1) for both in zip(weights, got)], got
 
 
 def local_blocks(
@@ -226,21 +227,21 @@
     weights = [
         lax.dynamic_slice_in_dim(w, my_ch * held, held, 0) for w in (up_weight, down_weight)
     ]
-    weights = more_hidden(weights, n, n // 2)
+    weights, got = more_hidden(weights, n, n // 2)
 
     parts = [
         first_section(blocked, inner_forward, twiddle_forward, s, n) for s in range(seqs)
     ]
     step = n // 2
     spread = []
-    waits = weights
+    waits = got
     for p in parts:
         last = exchange(after(p, *waits))
         spread.append(last.reshape(outer, -1, ch))
         if step > 1:
             step //= 2
-            weights = more_hidden(weights, n, step)
-        waits = [last, *weights]
+            weights, got = more_hidden(weights, n, step)
+        waits = [last, *got]
     out = None
     for s in range(seqs):
         last_rows = LAST_ROWS if s + 1 == seqs and a_dev > LAST_ROWS else 0
@@ -256,8 +257,8 @@
                 part = after(part, out)
             while step > 1:
                 step //= 2
-                weights = more_hidden(weights, n, step)
-                waits += weights
+                weights, got = more_hidden(weights, n, step)
+                waits += got
             gated, sq = gate_rows(blocked, inner_inverse, gain, bias, part, s, first)
             sqs = [sq] + [
                 lax.ppermute(sq, "ch", [(j, (j + r) % n_ch) for j in range(n_ch)])

time: 790 us -> 789 us (level)
    all_to_all x5, waiting for transfers between devices: 360 us -> 389 us  [exchange(): return lax.all_to_all(x, 'seq', split_axis=0, concat_axis=0, tiled=True)]
    ppermute x8, waiting for transfers between devices: 212 us -> 187 us  [more_hidden(): got = [lax.ppermute(w, 'seq', pairs) for w in weights]]
    unnamed x52 -> x56, local copies, waits for them, and re-layouts: 31.6 us -> 27.5 us
where the time goes in v6:
time: 789 us; the launch traced here: 788 us
  waiting for transfers between devices  581 us (74%)
  Pallas kernels  134 us (17%)
  starting transfers between devices  38.4 us (5%)
  local copies, waits for them, and re-layouts  30.2 us (4%)
    all_to_all x5, waiting for transfers between devices, exchange(): return lax.all_to_all(x, 'seq', split_axis=0, concat_axis=0, tiled=True)  389 us
    ppermute x8, waiting for transfers between devices, more_hidden(): got = [lax.ppermute(w, 'seq', pairs) for w in weights]  187 us
    pallas_call x3, Pallas kernels, mlp_rows(): pl.pallas_call(functools.partial(mlp_kernel, width, len(sqs)), grid=(coun...  49.7 us
    pallas_call x2, Pallas kernels, outer_section(): pl.pallas_call(functools.partial(outer_kernel, groups), grid=(k_dev // ro...  37.4 us
    pallas_call x3, Pallas kernels, gate_rows(): pl.pallas_call(gate_kernel, grid=(count,), in_specs=[pl.BlockSpec((1, 1,...  28.6 us
    unnamed x56, local copies, waits for them, and re-layouts  27.5 us
    all_to_all x5, starting transfers between devices, exchange(): return lax.all_to_all(x, 'seq', split_axis=0, concat_axis=0, tiled=True)  26 us
    pallas_call x2, Pallas kernels, first_section(): pl.pallas_call(first_kernel, grid=(a_dev // step,), in_specs=[pl.BlockSpe...  18.1 us
  transfers between devices with their start and end apart: 16, of which 12 were waited for; matrix products, arithmetic and copies ran while one was open for 2% of the time, Pallas kernels for 16%

profile of v6, /device:TPU:16, one launch (start us, length us, event | category | flops | bytes accessed | tf_op | source)
XLA Modules:
  0.0 788.2 jit_solution(10694875534181601703)
XLA Ops:
  0.0 0.9 constant_dynamic-update-slice_fusion.4
  1.0 1.6 constant_dynamic-update-slice_fusion.9
  2.6 2.9 collective-permute-start.1
  5.5 9.1 %first_section.3 = bf16[16,8,32,1024]{3,2,1,0:T(8,128)(2,1)} custom-call(bf16[2,8,512,1024]{3,2,1,0:T(8,128)(2,1)} %bitcast.20, bf16[512,512]{1,0:T(8,128)(2,1)} %w_ref.6, f32[8,512]{1,0:T(8,128)} %tw_ref.3), custom_call_target="tpu_custom_call" | custom-call | tf_op jit(solution)/shard_map/first_section/pallas_call | solution.py:37
  14.6 7.0 all-to-all-start
  21.6 1.5 collective-permute-start.2
  23.8 9.1 %first_section.2 = bf16[16,8,32,1024]{3,2,1,0:T(8,128)(2,1)} custom-call(bf16[2,8,512,1024]{3,2,1,0:T(8,128)(2,1)} %bitcast.21, bf16[512,512]{1,0:T(8,128)(2,1)} %w_ref.6, f32[8,512]{1,0:T(8,128)} %tw_ref.3), custom_call_target="tpu_custom_call" | custom-call | tf_op jit(solution)/shard_map/first_section/pallas_call | solution.py:37
  32.9 132.5 %collective-permute-done.2 = bf16[2,128,512]{2,1,0:T(8,128)(2,1)S(1)} collective-permute-done((bf16[2,128,512]{2,1,0:T(8,128)(2,1)S(1)}, bf16[2,128,512]{2,1,0:T(8,128)(2,1)S(1)}, u32[]{:S(2)}, u32[]{:S(2)}) %collective-permute-start.2) | collective-permute-done | bytes 262176 | tf_op jit(solution)/shard_map/ppermute | solution.py:197
  165.4 5.1 collective-permute-done.3
  170.5 33.7 %all-to-all-done = bf16[16,8,32,1024]{3,2,1,0:T(8,128)(2,1)} async-done(((bf16[16,8,32,1024]{3,2,1,0:T(8,128)(2,1)}), bf16[16,8,32,1024]{3,2,1,0:T(8,128)(2,1)}, u32[]{:S(2)}, u32[]{:S(2)}) %all-to-all-start) | async-done | bytes 8388640 | tf_op jit(solution)/shard_map/all_to_all | solution.py:192
  204.2 4.7 all-to-all-start.1
  209.8 1.5 collective-permute-start.4
  211.2 1.8 pad_maximum_fusion.3
  213.7 3.4 copy-done
  217.1 18.7 %outer_section.3 = bf16[16,8,32,1024]{3,2,1,0:T(8,128)(2,1)S(1)} custom-call(bf16[128,128]{1,0:T(8,128)(2,1)S(1)} %copy-done.12, bf16[128,128]{1,0:T(8,128)(2,1)S(1)} %copy-done.13, f32[2,128,16]{2,1,0:T(8,128)S(1)} %bitcast.9, bf16[128,32,1024]{2,1,0:T(8,128)(2,1)S(1)} %copy-done, bf16[128,32,1024]{2,1,0:T(8,128)(2,1)} %bitcast.6.spread_ref), custom_call_target="tpu_custom_call" | custom-call | tf_op jit(solution)/shard_map/outer_section/pallas_call | solution.py:78
  235.8 3.3 copy-done.2
  239.1 29.1 %collective-permute-done.4 = bf16[2,256,512]{2,1,0:T(8,128)(2,1)S(1)} collective-permute-done((bf16[2,256,512]{2,1,0:T(8,128)(2,1)}, bf16[2,256,512]{2,1,0:T(8,128)(2,1)S(1)}, u32[]{:S(2)}, u32[]{:S(2)}) %collective-permute-start.4) | collective-permute-done | bytes 524320 | tf_op jit(solution)/shard_map/ppermute | solution.py:197
  268.2 20.2 %collective-permute-done.5 = bf16[2,256,512]{2,1,0:T(8,128)(2,1)} collective-permute-done((bf16[2,256,512]{2,1,0:T(8,128)(2,1)}, bf16[2,256,512]{2,1,0:T(8,128)(2,1)}, u32[]{:S(2)}, u32[]{:S(2)}) %collective-permute-start.5) | collective-permute-done | bytes 524320 | tf_op jit(solution)/shard_map/ppermute | solution.py:197
  288.4 103.1 %all-to-all-done.1 = bf16[16,8,32,1024]{3,2,1,0:T(8,128)(2,1)} async-done(((bf16[16,8,32,1024]{3,2,1,0:T(8,128)(2,1)}), bf16[16,8,32,1024]{3,2,1,0:T(8,128)(2,1)}, u32[]{:S(2)}, u32[]{:S(2)}) %all-to-all-start.1) | async-done | bytes 8388640 | tf_op jit(solution)/shard_map/all_to_all | solution.py:192
  391.4 4.8 all-to-all-start.2
  396.2 1.0 pad_maximum_fusion
  397.5 1.1 pad_maximum_fusion.1
  399.0 3.4 copy-done.1
  402.4 18.7 %outer_section.2 = (bf16[16,6,32,1024]{3,2,1,0:T(8,128)(2,1)S(1)}, bf16[16,2,32,1024]{3,2,1,0:T(8,128)(2,1)S(1)}) custom-call(bf16[128,128]{1,0:T(8,128)(2,1)S(1)} %copy-done.12, bf16[128,128]{1,0:T(8,128)(2,1)S(1)} %copy-done.13, f32[2,128,16]{2,1,0:T(8,128)S(1)} %bitcast.10, bf16[128,32,1024]{2,1,0:T(8,128)(2,1)S(1)} %copy-done.1, ...), custom_call_target="tpu_custom_call" | custom-call | tf_op jit(solution)/shard_map/outer_section/pallas_call | solution.py:78
  421.1 2.7 copy-done.8
  423.8 1.3 copy-done.11
  425.1 153.7 %all-to-all-done.2.part_ref = bf16[16,8,32,1024]{3,2,1,0:T(8,128)(2,1)} async-done(((bf16[16,8,32,1024]{3,2,1,0:T(8,128)(2,1)}), bf16[16,8,32,1024]{3,2,1,0:T(8,128)(2,1)}, u32[]{:S(2)}, u32[]{:S(2)}) %all-to-all-start.2) | async-done | bytes 8388640 | tf_op jit(solution)/shard_map/all_to_all | solution.py:192
  578.8 4.9 all-to-all-start.3
  585.2 1.9 constant_dynamic-update-slice_fusion.6
  587.1 1.3 constant_dynamic-update-slice_fusion.up_ref
  588.4 13.7 %gate_rows.3 = (bf16[8,512,1024]{2,1,0:T(8,128)(2,1)}, f32[8,1,512]{2,1,0:T(1,128)S(1)}) custom-call(bf16[2,8,512,1024]{3,2,1,0:T(8,128)(2,1)} %bitcast.22, bf16[512,512]{1,0:T(8,128)(2,1)S(1)} %copy-done.10, f32[1,1024]{1,0:T(1,128)S(1)} %bitcast.14, f32[1,1024]{1,0:T(1,128)S(1)} %bitcast.17, bf16[16,8,32,1024]{3,2,1,0:T(8,128)(2,1)} %all-to-all-done.2.part_ref), custom_call_target="tpu_custom_call" | custom-call | tf_op jit(solution)/shard_map/gate_rows/pallas_call | solution.py:118
  602.2 1.5 collective-permute-start.8
  603.7 1.3 constant_dynamic-update-slice_fusion.5.down_ref
  605.9 3.4 copy-done.7
  609.3 24.4 %mlp_rows.3.rest_2_ = bf16[16,512,1024]{2,1,0:T(8,128)(2,1)} custom-call(bf16[8,512,1024]{2,1,0:T(8,128)(2,1)S(1)} %copy-done.7, f32[1,1024]{1,0:T(1,128)S(1)} %bitcast.11, bf16[2,1024,512]{2,1,0:T(8,128)(2,1)S(1)} %constant_dynamic-update-slice_fusion.up_ref, bf16[2,1024,512]{2,1,0:T(8,128)(2,1)S(1)} %constant_dynamic-update-slice_fusion.5.down_ref, ...), custom_call_target="tpu_custom_call" | custom-call | tf_op jit(solution)/shard_map/mlp_rows/pallas_call | solution.py:175
  633.7 1.4 copy-done.4
  635.1 86.2 %all-to-all-done.3.part_ref = bf16[16,6,32,1024]{3,2,1,0:T(8,128)(2,1)} async-done(((bf16[16,6,32,1024]{3,2,1,0:T(8,128)(2,1)}), bf16[16,6,32,1024]{3,2,1,0:T(8,128)(2,1)}, u32[]{:S(2)}, u32[]{:S(2)}) %all-to-all-start.3) | async-done | bytes 6291488 | tf_op jit(solution)/shard_map/all_to_all | solution.py:192
  721.2 4.7 all-to-all-start.4
  725.9 10.8 %gate_rows.4 = (bf16[6,512,1024]{2,1,0:T(8,128)(2,1)}, f32[6,1,512]{2,1,0:T(1,128)S(1)}) custom-call(bf16[2,8,512,1024]{3,2,1,0:T(8,128)(2,1)} %bitcast.23, bf16[512,512]{1,0:T(8,128)(2,1)S(1)} %copy-done.10, f32[1,1024]{1,0:T(1,128)S(1)} %bitcast.15, f32[1,1024]{1,0:T(1,128)S(1)} %bitcast.18, bf16[16,6,32,1024]{3,2,1,0:T(8,128)(2,1)} %all-to-all-done.3.part_ref), custom_call_target="tpu_custom_call" | custom-call | tf_op jit(solution)/shard_map/gate_rows/pallas_call | solution.py:118
  736.7 1.5 collective-permute-start.9
  738.2 2.2 collective-permute-done.9.rest_1_
  740.4 2.8 copy-done.9
  743.2 18.5 %mlp_rows.4.rest_2_ = bf16[16,512,1024]{2,1,0:T(8,128)(2,1)} custom-call(bf16[6,512,1024]{2,1,0:T(8,128)(2,1)S(1)} %copy-done.9, f32[1,1024]{1,0:T(1,128)S(1)} %bitcast.12, bf16[2,1024,512]{2,1,0:T(8,128)(2,1)S(1)} %constant_dynamic-update-slice_fusion.up_ref, bf16[2,1024,512]{2,1,0:T(8,128)(2,1)S(1)} %copy-done.5, ...), custom_call_target="tpu_custom_call", output_to_operand_aliasing={{}: (6, {})} | custom-call | tf_op jit(solution)/shard_map/mlp_rows/pallas_call | solution.py:175
  761.7 11.9 %all-to-all-done.4.part_ref = bf16[16,2,32,1024]{3,2,1,0:T(8,128)(2,1)} async-done(((bf16[16,2,32,1024]{3,2,1,0:T(8,128)(2,1)}), bf16[16,2,32,1024]{3,2,1,0:T(8,128)(2,1)}, u32[]{:S(2)}, u32[]{:S(2)}) %all-to-all-start.4) | async-done | bytes 2097184 | tf_op jit(solution)/shard_map/all_to_all | solution.py:192
  773.7 4.0 gate_rows.5
  777.7 1.6 collective-permute-start.10
  779.3 2.1 collective-permute-done.10.rest_1_
  781.4 6.8 mlp_rows.5
  (60 shorter events, 5.4 us)
Async XLA Ops:
  0.9 207.9 %copy-start.19 = (bf16[2,64,512]{2,1,0:T(8,128)(2,1)}, bf16[2,64,512]{2,1,0:T(8,128)(2,1)S(1)}, u32[]{:S(2)}) copy-start(bf16[2,64,512]{2,1,0:T(8,128)(2,1)S(1)} %get-tuple-element.38) | copy-start | bytes 393220
  0.9 13.6 %collective-permute-start = (bf16[2,64,512]{2,1,0:T(8,128)(2,1)S(1)}, bf16[2,64,512]{2,1,0:T(8,128)(2,1)S(1)}, u32[]{:S(2)}, u32[]{:S(2)}) collective-permute-start(bf16[2,64,512]{2,1,0:T(8,128)(2,1)S(1)} %get-tuple-element.38), channel_id=1, source_target_pairs={{0,16},{2,18},{4,20},{6,22},{8,24},{10,26},{12,28},{14,30},{16,0},... | collective-permute-start | bytes 393224 | tf_op jit(solution)/shard_map/ppermute | solution.py:197
  2.6 20.6 %copy-start.20 = (bf16[2,64,512]{2,1,0:T(8,128)(2,1)}, bf16[2,64,512]{2,1,0:T(8,128)(2,1)S(1)}, u32[]{:S(2)}) copy-start(bf16[2,64,512]{2,1,0:T(8,128)(2,1)S(1)} %get-tuple-element.36) | copy-start | bytes 393220
  2.6 12.0 %collective-permute-start.1 = (bf16[2,64,512]{2,1,0:T(8,128)(2,1)S(1)}, bf16[2,64,512]{2,1,0:T(8,128)(2,1)S(1)}, u32[]{:S(2)}, u32[]{:S(2)}) collective-permute-start(bf16[2,64,512]{2,1,0:T(8,128)(2,1)S(1)} %get-tuple-element.36), channel_id=1, source_target_pairs={{0,16},{2,18},{4,20},{6,22},{8,24},{10,26},{12,28},{14,30},{16,0},... | collective-permute-start | bytes 393224 | tf_op jit(solution)/shard_map/ppermute | solution.py:197
  14.6 196.7 %copy-start.16 = (bf16[2,64,512]{2,1,0:T(8,128)(2,1)}, bf16[2,64,512]{2,1,0:T(8,128)(2,1)S(1)}, u32[]{:S(2)}) copy-start(bf16[2,64,512]{2,1,0:T(8,128)(2,1)S(1)} %collective-permute-done.1) | copy-start | bytes 393220
  14.6 189.6 %all-to-all-start = ((bf16[16,8,32,1024]{3,2,1,0:T(8,128)(2,1)}), bf16[16,8,32,1024]{3,2,1,0:T(8,128)(2,1)}, u32[]{:S(2)}, u32[]{:S(2)}) async-start(bf16[16,8,32,1024]{3,2,1,0:T(8,128)(2,1)} %first_section.3), calls=%async_computation | async-start | bytes 16777216 | tf_op jit(solution)/shard_map/all_to_all | solution.py:192
  21.6 143.7 %collective-permute-start.2 = (bf16[2,128,512]{2,1,0:T(8,128)(2,1)S(1)}, bf16[2,128,512]{2,1,0:T(8,128)(2,1)S(1)}, u32[]{:S(2)}, u32[]{:S(2)}) collective-permute-start(bf16[2,128,512]{2,1,0:T(8,128)(2,1)S(1)} %pad_maximum_fusion.4), channel_id=1, source_target_pairs={{0,8},{2,10},{4,12},{6,14},{8,0},{10,2},{12,4},{14,6},{16,24},{18,... | collective-permute-start | bytes 786440 | tf_op jit(solution)/shard_map/ppermute | solution.py:197
  23.2 147.3 %collective-permute-start.3 = (bf16[2,128,512]{2,1,0:T(8,128)(2,1)S(1)}, bf16[2,128,512]{2,1,0:T(8,128)(2,1)S(1)}, u32[]{:S(2)}, u32[]{:S(2)}) collective-permute-start(bf16[2,128,512]{2,1,0:T(8,128)(2,1)S(1)} %pad_maximum_fusion.5), channel_id=1, source_target_pairs={{0,8},{2,10},{4,12},{6,14},{8,0},{10,2},{12,4},{14,6},{16,24},{18,... | collective-permute-start | bytes 786440 | tf_op jit(solution)/shard_map/ppermute | solution.py:197
  204.2 187.3 %all-to-all-start.1 = ((bf16[16,8,32,1024]{3,2,1,0:T(8,128)(2,1)}), bf16[16,8,32,1024]{3,2,1,0:T(8,128)(2,1)}, u32[]{:S(2)}, u32[]{:S(2)}) async-start(bf16[16,8,32,1024]{3,2,1,0:T(8,128)(2,1)} %first_section.2), calls=%async_computation.1 | async-start | bytes 16777216 | tf_op jit(solution)/shard_map/all_to_all | solution.py:192
  208.9 4.7 copy-start.22
  208.9 4.8 copy-start.12
  208.9 4.8 copy-start.13
  209.8 58.4 %collective-permute-start.4 = (bf16[2,256,512]{2,1,0:T(8,128)(2,1)}, bf16[2,256,512]{2,1,0:T(8,128)(2,1)S(1)}, u32[]{:S(2)}, u32[]{:S(2)}) collective-permute-start(bf16[2,256,512]{2,1,0:T(8,128)(2,1)} %pad_maximum_fusion.2), channel_id=1, source_target_pairs={{0,4},{2,6},{4,0},{6,2},{8,12},{10,14},{12,8},{14,10},{16,20},{18,... | collective-permute-start | bytes 1572872 | tf_op jit(solution)/shard_map/ppermute | solution.py:197
  213.0 75.4 %collective-permute-start.5 = (bf16[2,256,512]{2,1,0:T(8,128)(2,1)}, bf16[2,256,512]{2,1,0:T(8,128)(2,1)}, u32[]{:S(2)}, u32[]{:S(2)}) collective-permute-start(bf16[2,256,512]{2,1,0:T(8,128)(2,1)} %pad_maximum_fusion.3), channel_id=1, source_target_pairs={{0,4},{2,6},{4,0},{6,2},{8,12},{10,14},{12,8},{14,10},{16,20},{18,... | collective-permute-start | bytes 1572872 | tf_op jit(solution)/shard_map/ppermute | solution.py:197
  213.7 3.4 copy-start
  235.8 3.3 copy-start.2
  391.4 187.3 %all-to-all-start.2 = ((bf16[16,8,32,1024]{3,2,1,0:T(8,128)(2,1)}), bf16[16,8,32,1024]{3,2,1,0:T(8,128)(2,1)}, u32[]{:S(2)}, u32[]{:S(2)}) async-start(bf16[16,8,32,1024]{3,2,1,0:T(8,128)(2,1)} %copy-done.2), calls=%async_computation.2 | async-start | bytes 16777216 | tf_op jit(solution)/shard_map/all_to_all | solution.py:192
  396.2 1.3 copy-start.17
  396.2 1.3 copy-start.21
  397.3 27.9 %collective-permute-start.6 = (bf16[2,512,512]{2,1,0:T(8,128)(2,1)S(1)}, bf16[2,512,512]{2,1,0:T(8,128)(2,1)}, u32[]{:S(2)}, u32[]{:S(2)}) collective-permute-start(bf16[2,512,512]{2,1,0:T(8,128)(2,1)S(1)} %pad_maximum_fusion), channel_id=1, source_target_pairs={{0,2},{2,0},{4,6},{6,4},{8,10},{10,8},{12,14},{14,12},{16,18},{18,... | collective-permute-start | bytes 3145736 | tf_op jit(solution)/shard_map/ppermute | solution.py:197
  398.6 26.5 %collective-permute-start.7 = (bf16[2,512,512]{2,1,0:T(8,128)(2,1)S(1)}, bf16[2,512,512]{2,1,0:T(8,128)(2,1)}, u32[]{:S(2)}, u32[]{:S(2)}) collective-permute-start(bf16[2,512,512]{2,1,0:T(8,128)(2,1)S(1)} %pad_maximum_fusion.1), channel_id=1, source_target_pairs={{0,2},{2,0},{4,6},{6,4},{8,10},{10,8},{12,14},{14,12},{16,18},{18,... | collective-permute-start | bytes 3145736 | tf_op jit(solution)/shard_map/ppermute | solution.py:197
  399.0 3.4 copy-start.1
  421.1 2.7 copy-start.8
  423.8 1.3 copy-start.11
  578.8 4.9 copy-start.23
  578.8 4.9 copy-start.18
  578.8 142.4 %all-to-all-start.3 = ((bf16[16,6,32,1024]{3,2,1,0:T(8,128)(2,1)}), bf16[16,6,32,1024]{3,2,1,0:T(8,128)(2,1)}, u32[]{:S(2)}, u32[]{:S(2)}) async-start(bf16[16,6,32,1024]{3,2,1,0:T(8,128)(2,1)} %copy-done.8), calls=%async_computation.3 | async-start | bytes 12582912 | tf_op jit(solution)/shard_map/all_to_all | solution.py:192
  585.1 3.3 copy-start.10
  585.1 3.3 copy-start.14
  585.1 3.3 copy-start.15
  588.4 15.3 %copy-start.3 = (bf16[2,1024,512]{2,1,0:T(8,128)(2,1)S(1)}, bf16[2,1024,512]{2,1,0:T(8,128)(2,1)}, u32[]{:S(2)}) copy-start(bf16[2,1024,512]{2,1,0:T(8,128)(2,1)} %constant_dynamic-update-slice_fusion.6) | copy-start | bytes 6291460
  602.2 3.7 collective-permute-start.8
  605.9 3.4 copy-start.7
  633.7 1.4 copy-start.4
  721.2 52.4 %all-to-all-start.4 = ((bf16[16,2,32,1024]{3,2,1,0:T(8,128)(2,1)}), bf16[16,2,32,1024]{3,2,1,0:T(8,128)(2,1)}, u32[]{:S(2)}, u32[]{:S(2)}) async-start(bf16[16,2,32,1024]{3,2,1,0:T(8,128)(2,1)} %copy-done.11), calls=%async_computation.4 | async-start | bytes 4194304 | tf_op jit(solution)/shard_map/all_to_all | solution.py:192
  725.9 14.5 %copy-start.5 = (bf16[2,1024,512]{2,1,0:T(8,128)(2,1)S(1)}, bf16[2,1024,512]{2,1,0:T(8,128)(2,1)}, u32[]{:S(2)}) copy-start(bf16[2,1024,512]{2,1,0:T(8,128)(2,1)} %copy-done.4) | copy-start | bytes 6291460
  736.7 3.7 collective-permute-start.9
  740.4 2.8 copy-start.9
  773.7 7.7 copy-start.6
  777.7 3.7 collective-permute-start.10
